TPU v7x, 32 devices: a whole 2x2x4 slice. The times are simulated.
32 devices in a mesh: dp: 16 (over z, y, x), mp: 2 (over core).
Axes of the slice: x: 2, y: 2, z: 4, core: 2. Of those that a mesh axis runs over, the one named last changes fastest.
Arguments:
- tokens: bfloat16 [32768, 768], P(('dp', 'mp')), may hold values from -6 to 6
- norm1_gain: float32 [768], replicated, may hold values from 0.1 to 1.9
- norm1_shift: float32 [768], replicated, may hold values from -3 to 3
- w_query: bfloat16 [768, 768], P('dp', 'mp'), may hold values from -0.21875 to 0.21875
- w_key: bfloat16 [768, 768], P('dp', 'mp'), may hold values from -0.21875 to 0.21875
- w_value: bfloat16 [768, 768], P('dp', 'mp'), may hold values from -0.21875 to 0.21875
- w_out: bfloat16 [768, 768], P('dp', 'mp'), may hold values from -3.5 to 3.5
- fmap_query: bfloat16 [12, 64, 64], P('mp'), may hold values from -0.75 to 0.75
- fmap_key: bfloat16 [12, 64, 64], P('mp'), may hold values from -0.75 to 0.75
- norm2_gain: float32 [768], replicated, may hold values from 0.1 to 1.9
- norm2_shift: float32 [768], replicated, may hold values from -3 to 3
- w_fc: bfloat16 [768, 3072], P('dp', 'mp'), may hold values from -0.21875 to 0.21875
- w_down: bfloat16 [768, 3072], P('dp', 'mp'), may hold values from -0.109375 to 0.109375
- lengths: int32 [16, 16], P('dp'), may hold values from 0 to 1536, as said below
- cotangent: bfloat16 [32768, 768], P(('dp', 'mp')), may hold values from -6 to 6
Outputs:
- mixed: bfloat16 [32768, 768], P(('dp', 'mp'))
- grad_tokens: bfloat16 [32768, 768], P(('dp', 'mp'))
- grad_norm1_gain: float32 [768], replicated
- grad_norm1_shift: float32 [768], replicated
- grad_w_query: float32 [768, 768], P('dp', 'mp')
- grad_w_key: float32 [768, 768], P('dp', 'mp')
- grad_w_value: float32 [768, 768], P('dp', 'mp')
- grad_w_out: float32 [768, 768], P('dp', 'mp')
- grad_fmap_query: float32 [12, 64, 64], P('mp')
- grad_fmap_key: float32 [12, 64, 64], P('mp')
- grad_norm2_gain: float32 [768], replicated
- grad_norm2_shift: float32 [768], replicated
- grad_w_fc: float32 [768, 3072], P('dp', 'mp')
- grad_w_down: float32 [768, 3072], P('dp', 'mp')
Inputs may be any that keep to these rules, and one draw needn't show every extreme that they name: Row b holds the lengths of the sequences packed one after another from the first row of bin b, followed by zeros; they sum to at most 2048, and rows after that sum are padding. Each nonzero length is at least 128. In every bin one sequence covers both rows 1023 and 1024.
All inputs are finite; a program needn't handle non-finite values.
Results may differ from a plain program's by a relative error of at most 0.015.
Values may be sent and summed in bfloat16 or wider, within the bound.
No kernel may reach another device: no remote copies, remote signals or barrier semaphores. Data moves between devices by JAX's collectives and lax.ppermute only.
A program may use at most 192 MiB of HBM per device.

v0:
```python
import jax
import jax.numpy as jnp
from jax import lax
from jax.sharding import PartitionSpec as P

HIGH = lax.Precision.HIGHEST
EPS = 1e-05
BLOCK = 512


def layer_norm(rows, gain, shift):
    center = rows - jnp.mean(rows, axis=-1, keepdims=True)
    spread = jnp.mean(center * center, axis=-1, keepdims=True)
    return center * lax.rsqrt(spread + EPS) * gain + shift


def features(logits):
    return jnp.concatenate(
        [jax.nn.softmax(logits, axis=-1), jax.nn.softmax(-logits, axis=-1)], axis=-1
    )


def gelu_tanh(inner):
    return jax.nn.gelu(inner, approximate=True)


def segment_rows(counts, total):
    ends = jnp.cumsum(counts)
    places = jnp.arange(total, dtype=jnp.int32)
    segment = jnp.sum((ends[None, :] <= places[:, None]).astype(jnp.int32), axis=1)
    living = places < ends[-1]
    return (segment, living)


def matmul(left, right, left_dim, right_dim):
    return lax.dot_general(
        left, right, (((left_dim,), (right_dim,)), ((), ())), preferred_element_type=jnp.float32
    )


def block_core(carry, block):
    state, totals = carry
    phi_q, phi_k, values, segment, living, end_before, end_now, kept = block
    width = segment.shape[0]
    order = jnp.arange(width, dtype=jnp.int32)
    mask = (
        (segment[:, None] == segment[None, :])
        & (order[None, :] <= order[:, None])
        & living[:, None]
    )
    scores = jnp.einsum("thf,shf->hts", phi_q, phi_k, precision=HIGH)
    weights = jnp.where(mask[None], scores, 0.0)
    numer = jnp.einsum("hts,shd->thd", weights, values, precision=HIGH)
    denom = jnp.sum(weights, axis=2).T
    reach = ((segment == end_before) & living).astype(jnp.float32)
    numer = numer + reach[:, None, None] * jnp.einsum("thf,hfd->thd", phi_q, state, precision=HIGH)
    denom = denom + reach[:, None] * jnp.einsum("thf,hf->th", phi_q, totals, precision=HIGH)
    denom = denom + (1.0 - living.astype(jnp.float32))[:, None]
    written = (segment == end_now).astype(jnp.float32)
    masked_keys = phi_k * written[:, None, None]
    state = kept * state + jnp.einsum("shf,shd->hfd", masked_keys, values, precision=HIGH)
    totals = kept * totals + jnp.sum(masked_keys, axis=0)
    return ((state, totals), numer / denom[:, :, None])


def attend(query_logits, key_logits, values, segment, living):
    total, heads, width = values.shape
    span = min(BLOCK, total)
    count = total // span
    phi_q = features(query_logits).reshape(count, span, heads, 2 * width)
    phi_k = features(key_logits).reshape(count, span, heads, 2 * width)
    blocked = values.reshape(count, span, heads, width)
    segment_blocks = segment.reshape(count, span)
    living_blocks = living.reshape(count, span)
    ends = segment_blocks[:, -1]
    before = jnp.concatenate([jnp.full((1,), -1, jnp.int32), ends[:-1]])
    kept = (ends == before).astype(jnp.float32)
    initial = (
        jnp.zeros((heads, 2 * width, width), jnp.float32),
        jnp.zeros((heads, 2 * width), jnp.float32),
    )
    unused, outputs = lax.scan(
        jax.checkpoint(block_core),
        initial,
        (phi_q, phi_k, blocked, segment_blocks, living_blocks, before, ends, kept),
    )
    return outputs.reshape(total, heads, width)


def per_device(
    tokens,
    norm1_gain,
    norm1_shift,
    w_query,
    w_key,
    w_value,
    w_out,
    fmap_query,
    fmap_key,
    norm2_gain,
    norm2_shift,
    w_fc,
    w_down,
    lengths,
    cotangent,
):
    full_query, full_key, full_value, full_out, full_fc, full_down = (
        lax.all_gather(w_query, "dp", axis=0, tiled=True),
        lax.all_gather(w_key, "dp", axis=0, tiled=True),
        lax.all_gather(w_value, "dp", axis=0, tiled=True),
        lax.all_gather(w_out, "dp", axis=0, tiled=True),
        lax.all_gather(w_fc, "dp", axis=0, tiled=True),
        lax.all_gather(w_down, "dp", axis=0, tiled=True),
    )
    residual = tokens.astype(jnp.float32)
    bin_rows = tokens.shape[0] * lax.axis_size("mp")
    heads = fmap_query.shape[0]
    width = fmap_query.shape[1]
    segment, living = segment_rows(lengths[0], bin_rows)
    normed1, norm1_back = jax.vjp(layer_norm, residual, norm1_gain, norm1_shift)
    inputs1 = lax.all_gather(normed1.astype(jnp.bfloat16), "mp", axis=0, tiled=True)
    query = matmul(inputs1, full_query, 1, 0).astype(jnp.bfloat16)
    keyed = matmul(inputs1, full_key, 1, 0).astype(jnp.bfloat16)
    valued = matmul(inputs1, full_value, 1, 0).astype(jnp.bfloat16)
    query_heads = query.reshape(bin_rows, heads, width)
    key_heads = keyed.reshape(bin_rows, heads, width)
    query_logits = jnp.einsum(
        "rhd,hde->rhe", query_heads, fmap_query, preferred_element_type=jnp.float32
    )
    key_logits = jnp.einsum("rhd,hde->rhe", key_heads, fmap_key, preferred_element_type=jnp.float32)

    def core(first_logits, second_logits, value_rows):
        return attend(first_logits, second_logits, value_rows, segment, living)

    attended, core_back = jax.vjp(
        core, query_logits, key_logits, valued.reshape(bin_rows, heads, width).astype(jnp.float32)
    )
    attended_low = attended.reshape(bin_rows, heads * width).astype(jnp.bfloat16)
    branch = lax.psum_scatter(
        matmul(attended_low, full_out, 1, 1).astype(jnp.bfloat16),
        "mp",
        scatter_dimension=0,
        tiled=True,
    ).astype(jnp.float32)
    hidden_state = residual + branch
    normed2, norm2_back = jax.vjp(layer_norm, hidden_state, norm2_gain, norm2_shift)
    inputs2 = lax.all_gather(normed2.astype(jnp.bfloat16), "mp", axis=0, tiled=True)
    inner = matmul(inputs2, full_fc, 1, 0)
    activated, gelu_back = jax.vjp(gelu_tanh, inner)
    activated_low = activated.astype(jnp.bfloat16)
    feed = lax.psum_scatter(
        matmul(activated_low, full_down, 1, 1).astype(jnp.bfloat16),
        "mp",
        scatter_dimension=0,
        tiled=True,
    ).astype(jnp.float32)
    mixed = (hidden_state + feed).astype(jnp.bfloat16)
    grad_full = lax.all_gather(cotangent, "mp", axis=0, tiled=True)
    grad_down = matmul(grad_full, activated_low, 0, 0)
    (grad_inner,) = gelu_back(matmul(grad_full, full_down, 1, 0))
    grad_inner_low = grad_inner.astype(jnp.bfloat16)
    grad_fc = matmul(inputs2, grad_inner_low, 0, 0)
    grad_normed2 = lax.psum_scatter(
        matmul(grad_inner_low, full_fc, 1, 1).astype(jnp.bfloat16),
        "mp",
        scatter_dimension=0,
        tiled=True,
    ).astype(jnp.float32)
    grad_hidden, grad_gain2, grad_shift2 = norm2_back(grad_normed2)
    grad_hidden = grad_hidden + cotangent.astype(jnp.float32)
    grad_branch = lax.all_gather(grad_hidden.astype(jnp.bfloat16), "mp", axis=0, tiled=True)
    grad_out = matmul(grad_branch, attended_low, 0, 0)
    grad_attended = matmul(grad_branch, full_out, 1, 0).reshape(bin_rows, heads, width)
    grad_query_logits, grad_key_logits, grad_values = core_back(grad_attended)
    grad_query_low = grad_query_logits.astype(jnp.bfloat16)
    grad_key_low = grad_key_logits.astype(jnp.bfloat16)
    grad_fmap_query = jnp.einsum(
        "rhd,rhe->hde", query_heads, grad_query_low, preferred_element_type=jnp.float32
    )
    grad_fmap_key = jnp.einsum(
        "rhd,rhe->hde", key_heads, grad_key_low, preferred_element_type=jnp.float32
    )
    grad_query = (
        jnp.einsum("rhe,hde->rhd", grad_query_low, fmap_query, preferred_element_type=jnp.float32)
        .reshape(bin_rows, heads * width)
        .astype(jnp.bfloat16)
    )
    grad_key = (
        jnp.einsum("rhe,hde->rhd", grad_key_low, fmap_key, preferred_element_type=jnp.float32)
        .reshape(bin_rows, heads * width)
        .astype(jnp.bfloat16)
    )
    grad_value = grad_values.reshape(bin_rows, heads * width).astype(jnp.bfloat16)
    grad_wquery = matmul(inputs1, grad_query, 0, 0)
    grad_wkey = matmul(inputs1, grad_key, 0, 0)
    grad_wvalue = matmul(inputs1, grad_value, 0, 0)
    grad_terms = (
        matmul(grad_query, full_query, 1, 1)
        + matmul(grad_key, full_key, 1, 1)
        + matmul(grad_value, full_value, 1, 1)
    )
    grad_normed1 = lax.psum_scatter(
        grad_terms.astype(jnp.bfloat16), "mp", scatter_dimension=0, tiled=True
    ).astype(jnp.float32)
    grad_rows, grad_gain1, grad_shift1 = norm1_back(grad_normed1)
    grad_tokens = (grad_hidden + grad_rows).astype(jnp.bfloat16)
    grad_wquery, grad_wkey, grad_wvalue, grad_out, grad_fc, grad_down = (
        lax.psum_scatter(grad_wquery, "dp", scatter_dimension=0, tiled=True),
        lax.psum_scatter(grad_wkey, "dp", scatter_dimension=0, tiled=True),
        lax.psum_scatter(grad_wvalue, "dp", scatter_dimension=0, tiled=True),
        lax.psum_scatter(grad_out, "dp", scatter_dimension=0, tiled=True),
        lax.psum_scatter(grad_fc, "dp", scatter_dimension=0, tiled=True),
        lax.psum_scatter(grad_down, "dp", scatter_dimension=0, tiled=True),
    )
    grad_gain1, grad_shift1, grad_gain2, grad_shift2 = lax.psum(
        (grad_gain1, grad_shift1, grad_gain2, grad_shift2), ("dp", "mp")
    )
    grad_fmap_query, grad_fmap_key = lax.psum((grad_fmap_query, grad_fmap_key), "dp")
    return (
        mixed,
        grad_tokens,
        grad_gain1,
        grad_shift1,
        grad_wquery,
        grad_wkey,
        grad_wvalue,
        grad_out,
        grad_fmap_query,
        grad_fmap_key,
        grad_gain2,
        grad_shift2,
        grad_fc,
        grad_down,
    )


def solution(mesh):
    placed = (
        P(("dp", "mp"), None),
        P(),
        P(),
        P("dp", "mp"),
        P("dp", "mp"),
        P("dp", "mp"),
        P("dp", "mp"),
        P("mp", None, None),
        P("mp", None, None),
        P(),
        P(),
        P("dp", "mp"),
        P("dp", "mp"),
        P("dp", None),
        P(("dp", "mp"), None),
    )
    return jax.shard_map(
        per_device,
        mesh=mesh,
        in_specs=placed,
        out_specs=(
            P(("dp", "mp"), None),
            P(("dp", "mp"), None),
            P(),
            P(),
            P("dp", "mp"),
            P("dp", "mp"),
            P("dp", "mp"),
            P("dp", "mp"),
            P("mp", None, None),
            P("mp", None, None),
            P(),
            P(),
            P("dp", "mp"),
            P("dp", "mp"),
        ),
        check_vma=False,
    )
```

profile of v0, /device:TPU:0, one launch (start us, length us, event | category | flops | bytes accessed | tf_op | source)
XLA Modules:
  0.0 2167.7 jit_solution(768115912579338275)
XLA Ops:
  17.1 48.5 %all_gather.33 = bf16[768,384]{1,0:T(8,128)(2,1)} all-gather(bf16[48,384]{1,0:T(8,128)(2,1)S(1)} %copy-done.56), channel_id=1, replica_groups=mesh['dp'=16,'mp'=2] {'dp'}, dimensions={0}, use_global_device_ids=true | all-gather | bytes 626688 | tf_op jit(solution)/shard_map/all_gather | solution.py:108
  65.6 41.1 %all_gather.31 = bf16[768,384]{1,0:T(8,128)(2,1)} all-gather(bf16[48,384]{1,0:T(8,128)(2,1)S(1)} %copy-done.57), channel_id=1, replica_groups=mesh['dp'=16,'mp'=2] {'dp'}, dimensions={0}, use_global_device_ids=true | all-gather | bytes 626688 | tf_op jit(solution)/shard_map/all_gather | solution.py:109
  106.8 43.6 %all_gather.32 = bf16[768,384]{1,0:T(8,128)(2,1)} all-gather(bf16[48,384]{1,0:T(8,128)(2,1)S(1)} %copy-done.58), channel_id=1, replica_groups=mesh['dp'=16,'mp'=2] {'dp'}, dimensions={0}, use_global_device_ids=true | all-gather | bytes 626688 | tf_op jit(solution)/shard_map/all_gather | solution.py:110
  150.4 41.3 %all_gather.34 = bf16[768,384]{1,0:T(8,128)(2,1)} all-gather(bf16[48,384]{1,0:T(8,128)(2,1)S(1)} %copy-done.59), channel_id=1, replica_groups=mesh['dp'=16,'mp'=2] {'dp'}, dimensions={0}, use_global_device_ids=true | all-gather | bytes 626688 | tf_op jit(solution)/shard_map/all_gather | solution.py:111
  279.2 114.2 %while.43 = (s32[]{:T(128)}, f32[6,128,64]{1,2,0:T(8,128)S(1)}, f32[6,128]{1,0:T(8,128)S(1)}, bf16[4,512,6,64]{1,3,2,0:T(8,128)(2,1)S(1)}, f32[4,6,128,64]{2,3,1...) while((s32[]{:T(128)}, f32[6,128,64]{1,2,0:T(8,128)S(1)}, ...), condition=%wide.region_15.16_spmd.clone, body=%wide.region_12.15_spmd.clone.sunk | while | flops 4240371456 | bytes 53023500 | solution.py:82
  414.4 49.0 %all-gather.11.cloned.1.call-done = bf16[768,1536]{1,0:T(8,128)(2,1)} async-done(((bf16[48,1536]{1,0:T(8,128)(2,1)}), bf16[768,1536]{1,0:T(8,128)(2,1)}) %all-gather.11.cloned.1.call-update) | async-done | bytes 2359312 | tf_op jit(solution)/shard_map/all_gather | solution.py:112
  463.4 12.4 all-gather.9.cloned.1.call-done
  490.5 67.0 %all-gather.13.cloned.1.call-done = bf16[768,1536]{1,0:T(8,128)(2,1)} async-done(((bf16[48,1536]{1,0:T(8,128)(2,1)}), bf16[768,1536]{1,0:T(8,128)(2,1)}) %all-gather.13.cloned.1.call-update) | async-done | bytes 2359312 | tf_op jit(solution)/shard_map/all_gather | solution.py:113
  557.4 15.8 fusion.136
  582.3 12.2 convolution_convert_fusion.2
  614.7 11.8 all-gather.17.cloned.1.call-done
  642.2 534.5 %while.44 = (s32[]{:T(128)}, f32[6,128,64]{1,2,0:T(8,128)S(1)}, f32[6,128]{1,0:T(8,128)S(1)}, f32[4,512,6,128]{1,0,3,2:T(4,128)}, f32[4,512,6,128]{1,0,3,2:T(4,1...) while((s32[]{:T(128)}, f32[6,128,64]{1,2,0:T(8,128)S(1)}, ...), condition=%wide.region_26.27_spmd.clone, body=%wide.region_23.26_spmd.clone.sunk | while | flops 12409944064 | bytes 99036968 | solution.py:82
  694.3 10.5 fusion.360
  712.1 30.9 %dynamic_update_slice.67 = f32[4,512,6,128]{1,0,3,2:T(4,128)} dynamic-update-slice(f32[4,512,6,128]{1,0,3,2:T(4,128)} %get-tuple-element.1221, f32[1,512,6,128]{1,0,3,2:T(1,128)S(1)} %copy.191, s32[]{:T(128)S(6)} %sub.165, s32[]{:T(128)} %constant.132.clone.1..sunk.1, s32[]{:T(128)} %constant.132.clone.1..sunk.1, s32[]{:T(128)} %constant.132.clone.1..sunk.1) | dynamic-update-slice | bytes 3145732 | tf_op jit(solution)/shard_map/transpose(jvp())/while/body/jit(dynamic_update_index_in_dim)/dynamic_update_slice | solution.py:82
  743.0 30.9 %dynamic_update_slice.66 = f32[4,512,6,128]{1,0,3,2:T(4,128)} dynamic-update-slice(f32[4,512,6,128]{1,0,3,2:T(4,128)} %get-tuple-element.1220, f32[1,512,6,128]{1,0,3,2:T(1,128)S(1)} %copy.190, s32[]{:T(128)S(6)} %sub.165, s32[]{:T(128)} %constant.132.clone.1..sunk.1, s32[]{:T(128)} %constant.132.clone.1..sunk.1, s32[]{:T(128)} %constant.132.clone.1..sunk.1) | dynamic-update-slice | bytes 3145732 | tf_op jit(solution)/shard_map/transpose(jvp())/while/body/jit(dynamic_update_index_in_dim)/dynamic_update_slice | solution.py:82
  826.1 10.7 fusion.360
  844.0 30.9 %dynamic_update_slice.67 = f32[4,512,6,128]{1,0,3,2:T(4,128)} dynamic-update-slice(f32[4,512,6,128]{1,0,3,2:T(4,128)} %get-tuple-element.1221, f32[1,512,6,128]{1,0,3,2:T(1,128)S(1)} %copy.191, s32[]{:T(128)S(6)} %sub.165, s32[]{:T(128)} %constant.132.clone.1..sunk.1, s32[]{:T(128)} %constant.132.clone.1..sunk.1, s32[]{:T(128)} %constant.132.clone.1..sunk.1) | dynamic-update-slice | bytes 3145732 | tf_op jit(solution)/shard_map/transpose(jvp())/while/body/jit(dynamic_update_index_in_dim)/dynamic_update_slice | solution.py:82
  875.0 30.9 %dynamic_update_slice.66 = f32[4,512,6,128]{1,0,3,2:T(4,128)} dynamic-update-slice(f32[4,512,6,128]{1,0,3,2:T(4,128)} %get-tuple-element.1220, f32[1,512,6,128]{1,0,3,2:T(1,128)S(1)} %copy.190, s32[]{:T(128)S(6)} %sub.165, s32[]{:T(128)} %constant.132.clone.1..sunk.1, s32[]{:T(128)} %constant.132.clone.1..sunk.1, s32[]{:T(128)} %constant.132.clone.1..sunk.1) | dynamic-update-slice | bytes 3145732 | tf_op jit(solution)/shard_map/transpose(jvp())/while/body/jit(dynamic_update_index_in_dim)/dynamic_update_slice | solution.py:82
  958.0 10.5 fusion.360
  976.0 30.9 %dynamic_update_slice.67 = f32[4,512,6,128]{1,0,3,2:T(4,128)} dynamic-update-slice(f32[4,512,6,128]{1,0,3,2:T(4,128)} %get-tuple-element.1221, f32[1,512,6,128]{1,0,3,2:T(1,128)S(1)} %copy.191, s32[]{:T(128)S(6)} %sub.165, s32[]{:T(128)} %constant.132.clone.1..sunk.1, s32[]{:T(128)} %constant.132.clone.1..sunk.1, s32[]{:T(128)} %constant.132.clone.1..sunk.1) | dynamic-update-slice | bytes 3145732 | tf_op jit(solution)/shard_map/transpose(jvp())/while/body/jit(dynamic_update_index_in_dim)/dynamic_update_slice | solution.py:82
  1006.9 30.9 %dynamic_update_slice.66 = f32[4,512,6,128]{1,0,3,2:T(4,128)} dynamic-update-slice(f32[4,512,6,128]{1,0,3,2:T(4,128)} %get-tuple-element.1220, f32[1,512,6,128]{1,0,3,2:T(1,128)S(1)} %copy.190, s32[]{:T(128)S(6)} %sub.165, s32[]{:T(128)} %constant.132.clone.1..sunk.1, s32[]{:T(128)} %constant.132.clone.1..sunk.1, s32[]{:T(128)} %constant.132.clone.1..sunk.1) | dynamic-update-slice | bytes 3145732 | tf_op jit(solution)/shard_map/transpose(jvp())/while/body/jit(dynamic_update_index_in_dim)/dynamic_update_slice | solution.py:82
  1107.7 30.9 %dynamic_update_slice.67 = f32[4,512,6,128]{1,0,3,2:T(4,128)} dynamic-update-slice(f32[4,512,6,128]{1,0,3,2:T(4,128)} %get-tuple-element.1221, f32[1,512,6,128]{1,0,3,2:T(1,128)S(1)} %copy.191, s32[]{:T(128)S(6)} %sub.165, s32[]{:T(128)} %constant.132.clone.1..sunk.1, s32[]{:T(128)} %constant.132.clone.1..sunk.1, s32[]{:T(128)} %constant.132.clone.1..sunk.1) | dynamic-update-slice | bytes 3145732 | tf_op jit(solution)/shard_map/transpose(jvp())/while/body/jit(dynamic_update_index_in_dim)/dynamic_update_slice | solution.py:82
  1138.6 30.9 %dynamic_update_slice.66 = f32[4,512,6,128]{1,0,3,2:T(4,128)} dynamic-update-slice(f32[4,512,6,128]{1,0,3,2:T(4,128)} %get-tuple-element.1220, f32[1,512,6,128]{1,0,3,2:T(1,128)S(1)} %copy.190, s32[]{:T(128)S(6)} %sub.165, s32[]{:T(128)} %constant.132.clone.1..sunk.1, s32[]{:T(128)} %constant.132.clone.1..sunk.1, s32[]{:T(128)} %constant.132.clone.1..sunk.1) | dynamic-update-slice | bytes 3145732 | tf_op jit(solution)/shard_map/transpose(jvp())/while/body/jit(dynamic_update_index_in_dim)/dynamic_update_slice | solution.py:82
  1230.9 10.8 convolution_bitcast_fusion
  1290.5 40.8 %all-reduce = (f32[768]{0:T(1024)}, f32[768]{0:T(1024)}, f32[768]{0:T(1024)}, f32[768]{0:T(1024)}) all-reduce(f32[768]{0:T(1024)S(1)} %get-tuple-element.795, f32[768]{0:T(1024)S(1)} %get-tuple-element.798, f32[768]{0:T(1024)S(1)} %copy-done.62, f32[768]{0:T(1024)S(1)} %copy-done.63), channel_id=1, replica_groups=mesh['dp'=16,'mp'=2] {'dp','mp'}, use_global_device_ids=true, to_apply=%region_35.36 | all-reduce | flops 3072 | bytes 24576 | tf_op jit(solution)/shard_map/psum | solution.py:215
  1335.5 51.0 %reduce-scatter.31.cloned.1.call-done = f32[48,1536]{1,0:T(8,128)} async-done(((f32[768,1536]{1,0:T(8,128)}), f32[48,1536]{1,0:T(8,128)}) %reduce-scatter.31.cloned.1.call-update) | async-done | bytes 294928
  1386.5 143.1 %reduce-scatter.29.cloned.1.call-done = f32[48,1536]{1,0:T(8,128)} async-done(((f32[768,1536]{1,0:T(8,128)}), f32[48,1536]{1,0:T(8,128)}) %reduce-scatter.29.cloned.1.call-update) | async-done | bytes 294928 | tf_op jit(solution)/shard_map/reduce_scatter | solution.py:212
  1529.6 112.3 %all-reduce.4.cloned.1.call-done = (f32[6,64,64]{2,1,0:T(8,128)}, f32[6,64,64]{2,1,0:T(8,128)}) async-done(((f32[6,64,64]{2,1,0:T(8,128)}, f32[6,64,64]{2,1,0:T(8,128)}), (f32[6,64,64]{2,1,0:T(8,128)}, f32[6,64,64]{2,1,0:T(8,128)})) %all-reduce.4.cloned.1.call-update) | async-done | bytes 196624 | tf_op jit(solution)/shard_map/psum | solution.py:218
  1641.9 128.8 %reduce-scatter.27.cloned.1.call-done = f32[48,384]{1,0:T(8,128)} async-done(((f32[768,384]{1,0:T(8,128)}), f32[48,384]{1,0:T(8,128)}) %reduce-scatter.27.cloned.1.call-update) | async-done | bytes 73744 | tf_op jit(solution)/shard_map/reduce_scatter | solution.py:211
  1770.7 128.7 %reduce-scatter.21.cloned.1.call-done = f32[48,384]{1,0:T(8,128)} async-done(((f32[768,384]{1,0:T(8,128)}), f32[48,384]{1,0:T(8,128)}) %reduce-scatter.21.cloned.1.call-update) | async-done | bytes 73744 | tf_op jit(solution)/shard_map/reduce_scatter | solution.py:208
  1899.4 128.8 %reduce-scatter.25.cloned.1.call-done = f32[48,384]{1,0:T(8,128)} async-done(((f32[768,384]{1,0:T(8,128)}), f32[48,384]{1,0:T(8,128)}) %reduce-scatter.25.cloned.1.call-update) | async-done | bytes 73744 | tf_op jit(solution)/shard_map/reduce_scatter | solution.py:210
  2028.2 128.6 %reduce-scatter.23.cloned.1.call-done = f32[48,384]{1,0:T(8,128)} async-done(((f32[768,384]{1,0:T(8,128)}), f32[48,384]{1,0:T(8,128)}) %reduce-scatter.23.cloned.1.call-update) | async-done | bytes 73744 | tf_op jit(solution)/shard_map/reduce_scatter | solution.py:209
  (507 shorter events, 646.5 us)
Async XLA Ops:
  8.0 199.9 %copy-start = (bf16[6,64,64]{2,1,0:T(8,128)(2,1)S(1)}, bf16[6,64,64]{2,1,0:T(8,128)(2,1)}, u32[]{:S(2)}) copy-start(bf16[6,64,64]{2,1,0:T(8,128)(2,1)} %param.26) | copy-start | bytes 147460
  8.1 183.6 %all-gather.7.cloned.1.call-start = ((), (), s32[]{:S(2)}) async-start(), calls=%async_computation.10 | async-start | bytes 4718592 | tf_op jit(solution)/shard_map/all_gather | solution.py:121
  9.9 55.7 %copy-start.57 = (bf16[48,384]{1,0:T(8,128)(2,1)S(1)}, bf16[48,384]{1,0:T(8,128)(2,1)}, u32[]{:S(2)}) copy-start(bf16[48,384]{1,0:T(8,128)(2,1)} %param.23) | copy-start | bytes 110596
  12.6 94.2 %copy-start.58 = (bf16[48,384]{1,0:T(8,128)(2,1)S(1)}, bf16[48,384]{1,0:T(8,128)(2,1)}, u32[]{:S(2)}) copy-start(bf16[48,384]{1,0:T(8,128)(2,1)} %param.24) | copy-start | bytes 110596
  13.2 137.2 %copy-start.59 = (bf16[48,384]{1,0:T(8,128)(2,1)S(1)}, bf16[48,384]{1,0:T(8,128)(2,1)}, u32[]{:S(2)}) copy-start(bf16[48,384]{1,0:T(8,128)(2,1)} %param.25) | copy-start | bytes 110596
  15.0 393.2 %reduce-scatter.13.cloned.1.call-start = ((), (), s32[]{:S(2)}) async-start(), calls=%async_computation.11 | async-start | bytes 4718592 | tf_op jit(solution)/shard_map/reduce_scatter | solution.py:139
  203.3 410.0 %copy-start.30 = (f32[2048,6]{0,1:T(8,128)}, f32[2048,6]{0,1:T(8,128)S(1)}, u32[]{:S(2)}) copy-start(f32[2048,6]{0,1:T(8,128)S(1)} %get-tuple-element.889) | copy-start | bytes 147460
  225.5 10.0 copy-start.32
  225.5 10.0 copy-start.38
  282.7 9.8 copy-start.1
  311.1 9.8 copy-start.1
  339.5 9.8 copy-start.1
  367.9 9.8 copy-start.1
  399.8 63.6 %all-gather.11.cloned.1.call-start = ((), (), s32[]{:S(2)}) async-start(), calls=%async_computation.13 | async-start | bytes 2506752 | tf_op jit(solution)/shard_map/all_gather | solution.py:112
  400.3 10.7 copy-start.53
  400.3 10.7 copy-start.65
  400.4 75.4 %all-gather.9.cloned.1.call-start = ((), (), s32[]{:S(2)}) async-start(), calls=%async_computation.12 | async-start | bytes 4718592 | tf_op jit(solution)/shard_map/all_gather | solution.py:147
  413.0 77.4 %all-gather.15.cloned.1.call-start = ((), (), s32[]{:S(2)}) async-start(), calls=%async_computation.16 | async-start | bytes 4718592 | tf_op jit(solution)/shard_map/all_gather | solution.py:158
  413.6 143.8 %all-gather.13.cloned.1.call-start = ((), (), s32[]{:S(2)}) async-start(), calls=%async_computation.14 | async-start | bytes 2506752 | tf_op jit(solution)/shard_map/all_gather | solution.py:113
  414.3 180.3 %reduce-scatter.17.cloned.1.call-start = ((), (), s32[]{:S(2)}) async-start(), calls=%async_computation.17 | async-start | bytes 4718592 | tf_op jit(solution)/shard_map/reduce_scatter | solution.py:163
  557.4 18.4 copy-start.69
  582.3 23.5 %reduce-scatter.15.cloned.1.call-start = ((), (), s32[]{:S(2)}) async-start(), calls=%async_computation.15 | async-start | bytes 4718592 | tf_op jit(solution)/shard_map/reduce_scatter | solution.py:151
  594.6 31.9 %all-gather.17.cloned.1.call-start = ((), (), s32[]{:S(2)}) async-start(), calls=%async_computation.18 | async-start | bytes 4718592 | tf_op jit(solution)/shard_map/all_gather | solution.py:171
  613.2 672.6 %reduce-scatter.19.cloned.1.call-start = ((), (), s32[]{:S(2)}) async-start(), calls=%async_computation.19 | async-start | bytes 4718592 | tf_op jit(solution)/shard_map/reduce_scatter | solution.py:202
  1229.0 157.4 %reduce-scatter.31.cloned.1.call-start = ((), (), s32[]{:S(2)}) async-start(), calls=%async_computation.25 | async-start | bytes 5013504
  1247.7 281.8 %reduce-scatter.29.cloned.1.call-start = ((), (), s32[]{:S(2)}) async-start(), calls=%async_computation.24 | async-start | bytes 5013504 | tf_op jit(solution)/shard_map/reduce_scatter | solution.py:212
  1259.4 382.4 %all-reduce.4.cloned.1.call-start = ((), (), s32[]{:S(2)}) async-start(), calls=%async_computation.26 | async-start | bytes 786432 | tf_op jit(solution)/shard_map/psum | solution.py:218
  1264.9 505.8 %reduce-scatter.27.cloned.1.call-start = ((), (), s32[]{:S(2)}) async-start(), calls=%async_computation.23 | async-start | bytes 1253376 | tf_op jit(solution)/shard_map/reduce_scatter | solution.py:211
  1270.3 629.1 %reduce-scatter.21.cloned.1.call-start = ((), (), s32[]{:S(2)}) async-start(), calls=%async_computation.20 | async-start | bytes 1253376 | tf_op jit(solution)/shard_map/reduce_scatter | solution.py:208
  1275.3 753.0 %reduce-scatter.25.cloned.1.call-start = ((), (), s32[]{:S(2)}) async-start(), calls=%async_computation.22 | async-start | bytes 1253376 | tf_op jit(solution)/shard_map/reduce_scatter | solution.py:210
  1280.7 876.1 %reduce-scatter.23.cloned.1.call-start = ((), (), s32[]{:S(2)}) async-start(), calls=%async_computation.21 | async-start | bytes 1253376 | tf_op jit(solution)/shard_map/reduce_scatter | solution.py:209
  1285.8 45.6 %copy-start.61 = (f32[1024]{0:T(1024)S(1)}, f32[1024]{0:T(1024)}, u32[]{:S(2)}) copy-start(f32[1024]{0:T(1024)} %copy-done.60) | copy-start | bytes 12292
  (65 other events, 293.6 us)
Sparse Core Ops, SparseCore 0:
  15.1 14.8 all-gather.6
  399.9 8.2 reduce-scatter.12
  582.4 9.1 reduce-scatter.16
  594.7 11.0 reduce-scatter.14
Sparse Core Ops, SparseCore 1:
  403.4 59.9 all-gather.10
  465.4 10.2 all-gather.8
  477.2 13.2 all-gather.14
  493.7 63.7 all-gather.12
  613.3 13.1 all-gather.16
  1229.1 11.9 reduce-scatter.18
  1247.8 138.6 reduce-scatter.30
  1392.9 136.6 reduce-scatter.28
  1535.2 106.6 all-reduce.3
  1647.9 122.7 reduce-scatter.26
  1776.6 122.8 reduce-scatter.20
  1905.5 122.7 reduce-scatter.24
  2034.1 122.7 reduce-scatter.22
where the time goes:
time: 2180 us; the launch traced here: 2170 us
  waiting for transfers between devices  983 us (45%)
  matrix products  439 us (20%)
  local copies, waits for them, and re-layouts  416 us (19%)
  blocking collectives  215 us (10%)
  other arithmetic  86.4 us (4%)
    dynamic_update_slice x16, local copies, waits for them, and re-layouts, attend(): lax.scan(jax.checkpoint(block_core), initial, (phi_q, phi_k, blocked, seg...  265 us
    reduce_scatter x1, waiting for transfers between devices, per_device(): lax.psum_scatter(grad_fc, 'dp', scatter_dimension=0, tiled=True)  143 us
    reduce_scatter x1, waiting for transfers between devices, per_device(): lax.psum_scatter(grad_wvalue, 'dp', scatter_dimension=0, tiled=True)  129 us
    reduce_scatter x1, waiting for transfers between devices, per_device(): lax.psum_scatter(grad_out, 'dp', scatter_dimension=0, tiled=True)  129 us
    reduce_scatter x1, waiting for transfers between devices, per_device(): lax.psum_scatter(grad_wquery, 'dp', scatter_dimension=0, tiled=True)  129 us
    reduce_scatter x1, waiting for transfers between devices, per_device(): lax.psum_scatter(grad_wkey, 'dp', scatter_dimension=0, tiled=True)  129 us
    dot_general x16, matrix products, block_core(): scores = jnp.einsum('thf,shf->hts', phi_q, phi_k, precision=HIGH)  126 us
    dot_general x18, matrix products, matmul(): lax.dot_general(left, right, (((left_dim,), (right_dim,)), ((), ())), pre...  116 us
  transfers between devices with their start and end apart: 17, of which 14 were waited for; matrix products, arithmetic and copies ran while one was open for 4% of the time, Pallas kernels for 0%

commit v1 on v0

v1 whole, which is shorter than its diff:
```python
import functools

import jax
import jax.numpy as jnp
from jax import lax
from jax.experimental import pallas as pl
from jax.experimental.pallas import tpu as pltpu
from jax.sharding import PartitionSpec as P

EPS = 1e-05
CHUNK = 256
EXT = 80
LOW = jnp.bfloat16
F32 = jnp.float32
VMEM = 56 * 1024 * 1024
GELU_C = 0.7978845608028654
GELU_A = 0.044715


def nn(a, b):
    return lax.dot_general(a, b, (((1,), (0,)), ((), ())), preferred_element_type=F32)


def nt(a, b):
    return lax.dot_general(a, b, (((1,), (1,)), ((), ())), preferred_element_type=F32)


def tn(a, b):
    return lax.dot_general(a, b, (((0,), (0,)), ((), ())), preferred_element_type=F32)


def norm_parts(rows):
    center = rows - jnp.mean(rows, axis=-1, keepdims=True)
    spread = jnp.mean(center * center, axis=-1, keepdims=True)
    rstd = lax.rsqrt(spread + EPS)
    return center * rstd, rstd


def norm_back(grad, xhat, rstd, gain):
    e = grad * gain
    return rstd * (
        e - jnp.mean(e, axis=-1, keepdims=True) - xhat * jnp.mean(e * xhat, axis=-1, keepdims=True)
    )


def softmax_pair(logits):
    high = jnp.max(logits, axis=0, keepdims=True)
    least = jnp.min(logits, axis=0, keepdims=True)
    pos = jnp.exp(logits - high)
    neg = jnp.exp(least - logits)
    pos = pos * (1.0 / jnp.sum(pos, axis=0, keepdims=True))
    neg = neg * (1.0 / jnp.sum(neg, axis=0, keepdims=True))
    return jnp.concatenate([pos, neg], axis=0).astype(LOW)


def softmax_pair_back(phi, grad):
    width = phi.shape[0] // 2
    pos = phi[:width].astype(F32)
    neg = phi[width:].astype(F32)
    gp = grad[:width]
    gn = grad[width:]
    gp = gp - jnp.sum(pos * gp, axis=0, keepdims=True)
    gn = gn - jnp.sum(neg * gn, axis=0, keepdims=True)
    return pos * gp - neg * gn


def project_kernel(
    kept,
    tokens,
    gain,
    shift,
    w_own,
    w_oth,
    fq,
    fk,
    aux,
    normed_t,
    q_t,
    k_t,
    v_nat,
    v_ext,
    phi_q,
    phi_k,
    phi_k_nat,
    prefix,
    final,
    v_sum,
    state,
):
    step = pl.program_id(0)
    width = v_ext.shape[1] - 16
    xhat, unused = norm_parts(tokens[...].astype(F32))
    normed = (xhat * gain[...] + shift[...]).astype(LOW)
    normed_t[...] = normed.T
    written = aux[1:2, :].astype(LOW)
    rows = normed.shape[0]
    tail = jnp.where(lax.broadcasted_iota(jnp.int32, (16, rows), 0) == 0, 1.0, 0.0).astype(LOW)

    @pl.when(step == 0)
    def _():
        state[...] = jnp.zeros_like(state)
        v_sum[...] = jnp.zeros_like(v_sum)

    prefix[0] = state[...]
    keep = kept[step]
    for side, weights in enumerate((w_own, w_oth)):
        made = nn(normed, weights[...]).astype(LOW)
        part = made.shape[1] // 3
        v_nat[:, side * part : (side + 1) * part] = made[:, 2 * part :]
        v_sum[:, side * part : (side + 1) * part] += jnp.sum(
            made[:, 2 * part :].astype(F32), axis=0, keepdims=True
        )
        for pair in range(part // (2 * width)):
            at = side * part + pair * 2 * width
            index = at // (2 * width)
            lanes = slice(pair * 2 * width, (pair + 1) * 2 * width)
            q = made[:, :part][:, lanes].T
            k = made[:, part : 2 * part][:, lanes].T
            v = made[:, 2 * part :][:, lanes].T
            q_t[at : at + 2 * width, :] = q
            k_t[at : at + 2 * width, :] = k
            q_logits = nn(fq[index], q)
            k_logits = nn(fk[index], k)
            for one in range(2):
                head = 2 * index + one
                inside = slice(one * width, (one + 1) * width)
                feat_q = softmax_pair(q_logits[inside])
                feat_k = softmax_pair(k_logits[inside])
                phi_q[head] = feat_q
                phi_k[head] = feat_k
                phi_k_nat[:, head * 2 * width : (head + 1) * 2 * width] = feat_k.T
                value = jnp.concatenate([v[inside], tail], axis=0)
                v_ext[head] = value
                state[head] = keep * state[head] + nt(value, feat_k * written)
    final[...] = state[...]


def project(tokens, gain, shift, w_own, w_oth, fq, fk, aux, kept, heads, width):
    rows, dim = tokens.shape
    count = rows // CHUNK
    feat = 2 * width
    outs = (
        jax.ShapeDtypeStruct((dim, rows), LOW),
        jax.ShapeDtypeStruct((heads * width, rows), LOW),
        jax.ShapeDtypeStruct((heads * width, rows), LOW),
        jax.ShapeDtypeStruct((rows, heads * width), LOW),
        jax.ShapeDtypeStruct((heads, EXT, rows), LOW),
        jax.ShapeDtypeStruct((heads, feat, rows), LOW),
        jax.ShapeDtypeStruct((heads, feat, rows), LOW),
        jax.ShapeDtypeStruct((rows, heads * feat), LOW),
        jax.ShapeDtypeStruct((count, heads, EXT, feat), F32),
        jax.ShapeDtypeStruct((heads, EXT, feat), F32),
        jax.ShapeDtypeStruct((1, heads * width), F32),
    )
    whole = lambda a: pl.BlockSpec(a.shape, lambda c, *_: (0,) * a.ndim)
    return pl.pallas_call(
        project_kernel,
        grid_spec=pltpu.PrefetchScalarGridSpec(
            num_scalar_prefetch=1,
            grid=(count,),
            in_specs=[
                pl.BlockSpec((CHUNK, dim), lambda c, *_: (c, 0)),
                whole(gain),
                whole(shift),
                whole(w_own),
                whole(w_oth),
                whole(fq),
                whole(fk),
                pl.BlockSpec((8, CHUNK), lambda c, *_: (0, c)),
            ],
            out_specs=[
                pl.BlockSpec((dim, CHUNK), lambda c, *_: (0, c)),
                pl.BlockSpec((heads * width, CHUNK), lambda c, *_: (0, c)),
                pl.BlockSpec((heads * width, CHUNK), lambda c, *_: (0, c)),
                pl.BlockSpec((CHUNK, heads * width), lambda c, *_: (c, 0)),
                pl.BlockSpec((heads, EXT, CHUNK), lambda c, *_: (0, 0, c)),
                pl.BlockSpec((heads, feat, CHUNK), lambda c, *_: (0, 0, c)),
                pl.BlockSpec((heads, feat, CHUNK), lambda c, *_: (0, 0, c)),
                pl.BlockSpec((CHUNK, heads * feat), lambda c, *_: (c, 0)),
                pl.BlockSpec((1, heads, EXT, feat), lambda c, *_: (c, 0, 0, 0)),
                pl.BlockSpec((heads, EXT, feat), lambda c, *_: (0, 0, 0)),
                pl.BlockSpec((1, heads * width), lambda c, *_: (0, 0)),
            ],
            scratch_shapes=[pltpu.VMEM((heads, EXT, feat), F32)],
        ),
        out_shape=outs,
        compiler_params=pltpu.CompilerParams(vmem_limit_bytes=VMEM),
        cost_estimate=pl.CostEstimate(
            flops=2 * rows * dim * 3 * heads * width * 3, bytes_accessed=20 << 20, transcendentals=0
        ),
        name="project",
    )(kept, tokens, gain, shift, w_own, w_oth, fq, fk, aux)


def attend_kernel(
    carry,
    tokens,
    gain,
    shift,
    w_own,
    w_oth,
    aux,
    mask,
    phi_q,
    phi_k_nat,
    v_ext,
    prefix,
    entering,
    center,
    att_t,
    att_c,
    denom,
    hidden,
    normed,
    normed_t,
):
    step = pl.program_id(0)
    heads, feat, unused = phi_q.shape
    width = feat // 2
    reach = aux[0:1, :]
    padding = aux[3:4, :]
    keep = carry[step]
    for head in range(heads):
        pq = phi_q[head]
        scores = nn(phi_k_nat[:, head * feat : (head + 1) * feat], pq)
        weights = scores.astype(LOW) * mask[0]
        state = (prefix[0, head] + keep * entering[head]).astype(LOW)
        numer = nn(v_ext[head], weights) + reach * nn(state, pq)
        below = numer[width : width + 1] + padding
        denom[head : head + 1, :] = below
        place = slice(head * width, (head + 1) * width)
        att = numer[:width] * (1.0 / below)
        att_t[place, :] = att.astype(LOW)
        att_c[place, :] = (att - center[place, :]).astype(LOW)
    att = att_t[...].T
    part = w_own.shape[1]
    branch = nt(att[:, :part], w_own[...]) + nt(att[:, part:], w_oth[...])
    total = tokens[...].astype(F32) + branch
    hidden[...] = total
    xhat, unused = norm_parts(total)
    low = (xhat * gain[...] + shift[...]).astype(LOW)
    normed[...] = low
    normed_t[...] = low.T


def attend(tokens, gain, shift, w_own, w_oth, aux, mask, phi_q, phi_k_nat, v_ext, prefix, entering, center, carry):
    rows, dim = tokens.shape
    count = rows // CHUNK
    heads, feat, unused = phi_q.shape
    width = feat // 2
    outs = (
        jax.ShapeDtypeStruct((heads * width, rows), LOW),
        jax.ShapeDtypeStruct((heads * width, rows), LOW),
        jax.ShapeDtypeStruct((16, rows), F32),
        jax.ShapeDtypeStruct((rows, dim), F32),
        jax.ShapeDtypeStruct((rows, dim), LOW),
        jax.ShapeDtypeStruct((dim, rows), LOW),
    )
    whole = lambda a: pl.BlockSpec(a.shape, lambda c, *_: (0,) * a.ndim)
    return pl.pallas_call(
        attend_kernel,
        grid_spec=pltpu.PrefetchScalarGridSpec(
            num_scalar_prefetch=1,
            grid=(count,),
            in_specs=[
                pl.BlockSpec((CHUNK, dim), lambda c, *_: (c, 0)),
                whole(gain),
                whole(shift),
                whole(w_own),
                whole(w_oth),
                pl.BlockSpec((8, CHUNK), lambda c, *_: (0, c)),
                pl.BlockSpec((1, CHUNK, CHUNK), lambda c, *_: (c, 0, 0)),
                pl.BlockSpec((heads, feat, CHUNK), lambda c, *_: (0, 0, c)),
                pl.BlockSpec((CHUNK, heads * feat), lambda c, *_: (c, 0)),
                pl.BlockSpec((heads, EXT, CHUNK), lambda c, *_: (0, 0, c)),
                pl.BlockSpec((1, heads, EXT, feat), lambda c, *_: (c, 0, 0, 0)),
                whole(entering),
                whole(center),
            ],
            out_specs=[
                pl.BlockSpec((heads * width, CHUNK), lambda c, *_: (0, c)),
                pl.BlockSpec((heads * width, CHUNK), lambda c, *_: (0, c)),
                pl.BlockSpec((16, CHUNK), lambda c, *_: (0, c)),
                pl.BlockSpec((CHUNK, dim), lambda c, *_: (c, 0)),
                pl.BlockSpec((CHUNK, dim), lambda c, *_: (c, 0)),
                pl.BlockSpec((dim, CHUNK), lambda c, *_: (0, c)),
            ],
        ),
        out_shape=outs,
        compiler_params=pltpu.CompilerParams(vmem_limit_bytes=VMEM),
        cost_estimate=pl.CostEstimate(
            flops=2 * rows * dim * heads * width * 6, bytes_accessed=20 << 20, transcendentals=0
        ),
        name="attend",
    )(carry, tokens, gain, shift, w_own, w_oth, aux, mask, phi_q, phi_k_nat, v_ext, prefix, entering, center)


def feed_kernel(
    normed,
    normed_t,
    cot,
    cot_t,
    fc_own,
    fc_oth,
    down_own,
    down_oth,
    feed,
    grad_normed,
    d_fc_own,
    d_fc_oth,
    d_down_own,
    d_down_oth,
):
    step = pl.program_id(0)

    acts = []
    grads = []
    for fc, down, d_fc, d_down in (
        (fc_own, down_own, d_fc_own, d_down_own),
        (fc_oth, down_oth, d_fc_oth, d_down_oth),
    ):
        u = nn(normed[...], fc[...])
        square = u * u
        t = jnp.tanh(u * (GELU_C + (GELU_C * GELU_A) * square))
        half = 0.5 + 0.5 * t
        act = (u * half).astype(LOW)
        slope = half + (0.5 * u) * (1.0 - t * t) * (GELU_C + (3.0 * GELU_C * GELU_A) * square)
        d_down[...] = nn(cot_t[...], act).astype(LOW)
        grad = (nn(cot[...], down[...]) * slope).astype(LOW)
        d_fc[...] = nn(normed_t[...], grad).astype(LOW)
        acts.append(act)
        grads.append(grad)
    more = nt(
        jnp.concatenate(acts, axis=1), jnp.concatenate([down_own[...], down_oth[...]], axis=1)
    )
    more_grad = nt(
        jnp.concatenate(grads, axis=1), jnp.concatenate([fc_own[...], fc_oth[...]], axis=1)
    )

    @pl.when(step == 0)
    def _():
        feed[...] = more
        grad_normed[...] = more_grad

    @pl.when(step > 0)
    def _():
        feed[...] += more
        grad_normed[...] += more_grad


def feed_forward(normed, normed_t, cot, cot_t, fc_own, fc_oth, down_own, down_oth):
    rows, dim = normed.shape
    units = fc_own.shape[1]
    tile = 256
    whole = lambda a: pl.BlockSpec(a.shape, lambda j: (0,) * a.ndim)
    tiled = pl.BlockSpec((dim, tile), lambda j: (0, j))
    total = pl.BlockSpec((rows, dim), lambda j: (0, 0))
    grad = jax.ShapeDtypeStruct((dim, units), LOW)
    return pl.pallas_call(
        feed_kernel,
        grid=(units // tile,),
        in_specs=[whole(normed), whole(normed_t), whole(cot), whole(cot_t)] + [tiled] * 4,
        out_specs=[total, total] + [tiled] * 4,
        out_shape=(
            jax.ShapeDtypeStruct((rows, dim), F32),
            jax.ShapeDtypeStruct((rows, dim), F32),
            grad,
            grad,
            grad,
            grad,
        ),
        compiler_params=pltpu.CompilerParams(vmem_limit_bytes=VMEM),
        cost_estimate=pl.CostEstimate(
            flops=2 * 6 * rows * dim * 2 * units, bytes_accessed=24 << 20, transcendentals=0
        ),
        name="feed",
    )(normed, normed_t, cot, cot_t, fc_own, fc_oth, down_own, down_oth)


def middle_kernel(
    hidden,
    feed_a,
    feed_b,
    gn_a,
    gn_b,
    cot,
    gain,
    w_own,
    w_oth,
    att_t,
    att_c,
    denom,
    phi_q,
    aux,
    mixed,
    grad_hidden,
    d_gain,
    d_shift,
    g_ext,
    leaving,
    d_out_own,
    d_out_oth,
    branch_t,
    att_all,
    state,
):
    step = pl.program_id(0)
    count = pl.num_programs(0)
    rows = hidden.shape[0]
    heads, feat, unused = phi_q.shape
    width = feat // 2
    hid = hidden[...]
    mixed[...] = (hid + (feed_a[...] + feed_b[...])).astype(LOW)
    xhat, rstd = norm_parts(hid)
    grad = gn_a[...] + gn_b[...]
    back = cot[...].astype(F32) + norm_back(grad, xhat, rstd, gain[...])
    grad_hidden[...] = back
    gain_part = jnp.sum(grad * xhat, axis=0, keepdims=True)
    shift_part = jnp.sum(grad, axis=0, keepdims=True)

    @pl.when(step == 0)
    def _():
        d_gain[...] = gain_part
        d_shift[...] = shift_part
        state[...] = jnp.zeros_like(state)

    @pl.when(step > 0)
    def _():
        d_gain[...] += gain_part
        d_shift[...] += shift_part

    low = back.astype(LOW)
    place = pl.ds(pl.multiple_of(step * rows, rows), rows)
    branch_t[:, place] = low.T
    att_all[:, place] = att_t[...]
    reach = aux[2:3, :].astype(LOW)
    part = w_own.shape[1]
    first = lax.broadcasted_iota(jnp.int32, (16, rows), 0) == 0
    for side, weights in enumerate((w_own, w_oth)):
        grad_att = nn(low, weights[...])
        for pair in range(part // (2 * width)):
            turned = grad_att[:, pair * 2 * width : (pair + 1) * 2 * width].T
            for one in range(2):
                head = side * (part // width) + pair * 2 + one
                ga = turned[one * width : (one + 1) * width]
                inverse = 1.0 / denom[head : head + 1, :]
                at = att_c[head * width : (head + 1) * width, :].astype(F32)
                gd = -jnp.sum(ga * at, axis=0, keepdims=True) * inverse
                ext = jnp.concatenate(
                    [(ga * inverse).astype(LOW), jnp.where(first, gd, 0.0).astype(LOW)], axis=0
                )
                g_ext[head] = ext
                state[head] += nt(ext * reach, phi_q[head])
    leaving[...] = state[...].astype(LOW)

    @pl.when(step == count - 1)
    def _():
        d_out_own[...] = nt(branch_t[...], att_all[:part, :]).astype(LOW)
        d_out_oth[...] = nt(branch_t[...], att_all[part:, :]).astype(LOW)


def middle(hidden, feed_a, feed_b, gn_a, gn_b, cot, gain, w_own, w_oth, att_t, att_c, denom, phi_q, aux):
    rows, dim = hidden.shape
    count = rows // CHUNK
    heads, feat, unused = phi_q.shape
    width = feat // 2
    part = w_own.shape[1]
    whole = lambda a: pl.BlockSpec(a.shape, lambda c: (0,) * a.ndim)
    rowed = pl.BlockSpec((CHUNK, dim), lambda c: (c, 0))
    fixed = lambda *shape: pl.BlockSpec(shape, lambda c: (0,) * len(shape))
    return pl.pallas_call(
        middle_kernel,
        grid=(count,),
        in_specs=[rowed] * 6
        + [
            whole(gain),
            whole(w_own),
            whole(w_oth),
            pl.BlockSpec((heads * width, CHUNK), lambda c: (0, c)),
            pl.BlockSpec((heads * width, CHUNK), lambda c: (0, c)),
            pl.BlockSpec((16, CHUNK), lambda c: (0, c)),
            pl.BlockSpec((heads, feat, CHUNK), lambda c: (0, 0, c)),
            pl.BlockSpec((8, CHUNK), lambda c: (0, c)),
        ],
        out_specs=[
            rowed,
            rowed,
            fixed(1, dim),
            fixed(1, dim),
            pl.BlockSpec((heads, EXT, CHUNK), lambda c: (0, 0, c)),
            fixed(heads, EXT, feat),
            fixed(dim, part),
            fixed(dim, part),
        ],
        out_shape=(
            jax.ShapeDtypeStruct((rows, dim), LOW),
            jax.ShapeDtypeStruct((rows, dim), F32),
            jax.ShapeDtypeStruct((1, dim), F32),
            jax.ShapeDtypeStruct((1, dim), F32),
            jax.ShapeDtypeStruct((heads, EXT, rows), LOW),
            jax.ShapeDtypeStruct((heads, EXT, feat), LOW),
            jax.ShapeDtypeStruct((dim, part), LOW),
            jax.ShapeDtypeStruct((dim, part), LOW),
        ),
        scratch_shapes=[
            pltpu.VMEM((dim, rows), LOW),
            pltpu.VMEM((heads * width, rows), LOW),
            pltpu.VMEM((heads, EXT, feat), F32),
        ],
        compiler_params=pltpu.CompilerParams(vmem_limit_bytes=VMEM),
        cost_estimate=pl.CostEstimate(
            flops=2 * rows * dim * heads * width * 3, bytes_accessed=24 << 20, transcendentals=0
        ),
        name="middle",
    )(hidden, feed_a, feed_b, gn_a, gn_b, cot, gain, w_own, w_oth, att_t, att_c, denom, phi_q, aux)


def attend_back_kernel(
    carry,
    kept,
    aux,
    mask,
    phi_q,
    phi_k,
    phi_k_nat,
    v_nat,
    v_ext,
    g_ext,
    prefix,
    entering,
    arriving,
    q_t,
    k_t,
    fq,
    fk,
    center,
    center_row,
    gq_t,
    gk_t,
    gv_t,
    d_fq,
    d_fk,
    state,
):
    step = pl.program_id(0)
    count = pl.num_programs(0)
    heads, feat, rows = phi_q.shape
    width = feat // 2
    chunk = count - 1 - step
    keep_in = carry[chunk]
    keep = kept[chunk]
    reach = aux[0:1, :].astype(LOW)
    written = aux[1:2, :].astype(LOW)

    @pl.when(step == 0)
    def _():
        state[...] = arriving[...].astype(F32)
        d_fq[...] = jnp.zeros_like(d_fq)
        d_fk[...] = jnp.zeros_like(d_fk)

    for pair in range(heads // 2):
        logit_grads = ([], [])
        lanes = slice(pair * feat, (pair + 1) * feat)
        v_pair = (v_nat[:, lanes].astype(F32) - center_row[:, lanes]).astype(LOW)
        for one in range(2):
            head = 2 * pair + one
            pq = phi_q[head]
            pk = phi_k[head]
            scores = nn(phi_k_nat[:, head * feat : (head + 1) * feat], pq)
            weights = scores.astype(LOW) * mask[0]
            ext = g_ext[head]
            numer = ext[:width]
            blank = jnp.zeros_like(numer)
            padded = jnp.concatenate([numer, blank] if one == 0 else [blank, numer], axis=0)
            gw = nn(v_pair, padded)
            gw = (gw + ext[width : width + 1].astype(F32)).astype(LOW) * mask[0]
            middle_v = center[head * width : (head + 1) * width, :]
            before = prefix[0, head] + keep_in * entering[head]
            before = jnp.concatenate(
                [before[:width] - middle_v * before[width : width + 1], before[width:]], axis=0
            ).astype(LOW)
            value = v_ext[head]
            value = jnp.concatenate(
                [(value[:width].astype(F32) - middle_v).astype(LOW), value[width:]], axis=0
            )
            after = state[head].astype(LOW)
            reached = ext * reach
            g_phi_q = nn(pk, gw) + tn(before, reached)
            g_phi_k = nt(pq, gw) + tn(after, value * written)
            g_value = nt(numer, weights) + nn(after[:width], pk * written)
            gv_t[head * width : (head + 1) * width, :] = g_value.astype(LOW)
            state[head] = keep * state[head] + nt(reached, pq)
            logit_grads[0].append(softmax_pair_back(pq, g_phi_q).astype(LOW))
            logit_grads[1].append(softmax_pair_back(pk, g_phi_k).astype(LOW))
        place = slice(pair * feat, (pair + 1) * feat)
        for grads, fmap, source, grad_out, d_fmap in (
            (logit_grads[0], fq, q_t, gq_t, d_fq),
            (logit_grads[1], fk, k_t, gk_t, d_fk),
        ):
            both = jnp.concatenate(grads, axis=0)
            grad_out[place, :] = nn(fmap[pair], both).astype(LOW)
            d_fmap[pair] += nt(source[place, :], both)


def attend_back(
    aux, mask, phi_q, phi_k, phi_k_nat, v_nat, v_ext, g_ext, prefix, entering, arriving, q_t, k_t, fq, fk, center, center_row, carry, kept
):
    heads, feat, rows = phi_q.shape
    width = feat // 2
    count = rows // CHUNK
    whole = lambda a: pl.BlockSpec(a.shape, lambda c, *_: (0,) * a.ndim)
    lanes = lambda size: pl.BlockSpec((size, CHUNK), lambda c, *_: (0, count - 1 - c))
    headed = lambda size: pl.BlockSpec((heads, size, CHUNK), lambda c, *_: (0, 0, count - 1 - c))
    natural = lambda size: pl.BlockSpec((CHUNK, size), lambda c, *_: (count - 1 - c, 0))
    fixed = lambda *shape: pl.BlockSpec(shape, lambda c, *_: (0,) * len(shape))
    grad = jax.ShapeDtypeStruct((heads * width, rows), LOW)
    grad_map = jax.ShapeDtypeStruct((heads // 2, feat, feat), F32)
    return pl.pallas_call(
        attend_back_kernel,
        grid_spec=pltpu.PrefetchScalarGridSpec(
            num_scalar_prefetch=2,
            grid=(count,),
            in_specs=[
                lanes(8),
                pl.BlockSpec((1, CHUNK, CHUNK), lambda c, *_: (count - 1 - c, 0, 0)),
                headed(feat),
                headed(feat),
                natural(heads * feat),
                natural(heads * width),
                headed(EXT),
                headed(EXT),
                pl.BlockSpec((1, heads, EXT, feat), lambda c, *_: (count - 1 - c, 0, 0, 0)),
                whole(entering),
                whole(arriving),
                lanes(heads * width),
                lanes(heads * width),
                whole(fq),
                whole(fk),
                whole(center),
                whole(center_row),
            ],
            out_specs=[
                lanes(heads * width),
                lanes(heads * width),
                lanes(heads * width),
                fixed(heads // 2, feat, feat),
                fixed(heads // 2, feat, feat),
            ],
            scratch_shapes=[pltpu.VMEM((heads, EXT, feat), F32)],
        ),
        out_shape=(grad, grad, grad, grad_map, grad_map),
        compiler_params=pltpu.CompilerParams(vmem_limit_bytes=VMEM),
        cost_estimate=pl.CostEstimate(
            flops=2 * rows * heads * CHUNK * feat * 10, bytes_accessed=24 << 20, transcendentals=0
        ),
        name="attend_back",
    )(carry, kept, aux, mask, phi_q, phi_k, phi_k_nat, v_nat, v_ext, g_ext, prefix, entering, arriving, q_t, k_t, fq, fk, center, center_row)


def weight_kernel(normed_t, gq_t, gk_t, gv_t, out):
    part = out.shape[1] // 3
    for place, grad in enumerate((gq_t, gk_t, gv_t)):
        out[:, place * part : (place + 1) * part] = nt(normed_t[...], grad[...]).astype(LOW)


def weight_grads(normed_t, gq_t, gk_t, gv_t):
    dim, rows = normed_t.shape
    part = gq_t.shape[0] // 2
    spec = pl.BlockSpec((part, rows), lambda s: (s, 0))
    return pl.pallas_call(
        weight_kernel,
        grid=(2,),
        in_specs=[pl.BlockSpec((dim, rows), lambda s: (0, 0)), spec, spec, spec],
        out_specs=pl.BlockSpec((dim, 3 * part), lambda s: (0, s)),
        out_shape=jax.ShapeDtypeStruct((dim, 6 * part), LOW),
        compiler_params=pltpu.CompilerParams(vmem_limit_bytes=VMEM),
        cost_estimate=pl.CostEstimate(
            flops=2 * 6 * part * dim * rows, bytes_accessed=10 << 20, transcendentals=0
        ),
        name="weight_grads",
    )(normed_t, gq_t, gk_t, gv_t)


def first_kernel(tokens, gain, grad_hidden, w_own, w_oth, gq_t, gk_t, gv_t, out, d_gain, d_shift):
    step = pl.program_id(0)
    part = w_own.shape[1] // 3
    total = None
    for side, weights in enumerate((w_own, w_oth)):
        place = slice(side * part, (side + 1) * part)
        stacked = jnp.concatenate([gq_t[place, :], gk_t[place, :], gv_t[place, :]], axis=0)
        term = nn(weights[...], stacked)
        total = term if total is None else total + term
    grad = total.T
    xhat, rstd = norm_parts(tokens[...].astype(F32))
    out[...] = (grad_hidden[...] + norm_back(grad, xhat, rstd, gain[...])).astype(LOW)
    gain_part = jnp.sum(grad * xhat, axis=0, keepdims=True)
    shift_part = jnp.sum(grad, axis=0, keepdims=True)

    @pl.when(step == 0)
    def _():
        d_gain[...] = gain_part
        d_shift[...] = shift_part

    @pl.when(step > 0)
    def _():
        d_gain[...] += gain_part
        d_shift[...] += shift_part


def first_back(tokens, gain, grad_hidden, w_own, w_oth, gq_t, gk_t, gv_t):
    rows, dim = tokens.shape
    size = gq_t.shape[0]
    whole = lambda a: pl.BlockSpec(a.shape, lambda c: (0,) * a.ndim)
    rowed = pl.BlockSpec((CHUNK, dim), lambda c: (c, 0))
    lanes = pl.BlockSpec((size, CHUNK), lambda c: (0, c))
    fixed = pl.BlockSpec((1, dim), lambda c: (0, 0))
    return pl.pallas_call(
        first_kernel,
        grid=(rows // CHUNK,),
        in_specs=[rowed, whole(gain), rowed, whole(w_own), whole(w_oth), lanes, lanes, lanes],
        out_specs=[rowed, fixed, fixed],
        out_shape=(
            jax.ShapeDtypeStruct((rows, dim), LOW),
            jax.ShapeDtypeStruct((1, dim), F32),
            jax.ShapeDtypeStruct((1, dim), F32),
        ),
        compiler_params=pltpu.CompilerParams(vmem_limit_bytes=VMEM),
        cost_estimate=pl.CostEstimate(
            flops=2 * 3 * size * dim * rows, bytes_accessed=14 << 20, transcendentals=0
        ),
        name="first_back",
    )(tokens, gain, grad_hidden, w_own, w_oth, gq_t, gk_t, gv_t)


SWAP = [(0, 1), (1, 0)]


def swap(piece):
    return lax.ppermute(piece, "mp", SWAP)


def flip(piece, bit, size):
    return lax.ppermute(piece, "dp", [(i, i ^ bit) for i in range(size)])


def turn(piece, by, size):
    return lax.ppermute(piece, "dp", [(i, (i + by) % size) for i in range(size)])


def other_order(state):
    half = state.shape[0] // 2
    return jnp.concatenate([state[half:], state[:half]], axis=0)


def ordered(mine, theirs, bit, axis):
    low = jnp.where(bit == 0, mine, theirs)
    high = jnp.where(bit == 0, theirs, mine)
    return jnp.stack([low, high], axis=axis)


def gather(shard, size):
    rows, columns = shard.shape
    if size % 4:
        own = lax.all_gather(shard, "dp", axis=0, tiled=True)
        return own, swap(own)
    place = lax.axis_index("dp")
    deep = size // 4
    x, y, z = place % 2, (place // 2) % 2, place // 4
    pieces = [shard] + [turn(shard, 4 * s, size) for s in range(1, deep)]
    ring = jnp.concatenate([pieces[deep - 1 - s] for s in range(deep)] * 2, axis=0)
    line = lax.dynamic_slice_in_dim(ring, (deep - 1 - z) * rows, deep * rows, 0)
    half = columns // 2
    a = line[:, :half].reshape(deep, rows, half)
    b = line[:, half:].reshape(deep, rows, half)
    a = ordered(a, flip(a, 1, size), x, 1)
    b = ordered(b, flip(b, 2, size), y, 1)
    a = ordered(a, flip(a, 2, size), y, 1)
    b = ordered(b, flip(b, 1, size), x, 2)
    own = jnp.concatenate(
        [a.reshape(size * rows, half), b.reshape(size * rows, half)], axis=1
    )
    return own, swap(own)


def scatter(own, other, size):
    got = own.astype(F32) + swap(other).astype(F32)
    rows = own.shape[0] // size
    columns = own.shape[1]
    if size % 4:
        return lax.psum_scatter(got, "dp", scatter_dimension=0, tiled=True)
    place = lax.axis_index("dp")
    deep = size // 4
    x, y, z = place % 2, (place // 2) % 2, place // 4
    half = columns // 2
    got = got.astype(LOW).reshape(deep, 2, 2, rows, columns)

    def fold(value, axis, bit, step):
        keep = lax.dynamic_index_in_dim(value, bit, axis, False)
        send = lax.dynamic_index_in_dim(value, 1 - bit, axis, False)
        return (keep.astype(F32) + flip(send, step, size).astype(F32)).astype(LOW)

    a = fold(got[..., :half], 2, x, 1)
    b = fold(got[..., half:], 1, y, 2)
    a = fold(a, 1, y, 2)
    b = fold(b, 1, x, 1)
    line = jnp.concatenate([a, b], axis=-1)
    total = lax.dynamic_index_in_dim(line, z, 0, False).astype(F32)
    for s in range(1, deep):
        send = lax.dynamic_index_in_dim(line, (z + s) % deep, 0, False)
        total = total + turn(send, 4 * s, size).astype(F32)
    return total


def block_pairs(fmap):
    heads, width, unused = fmap.shape
    pairs = fmap.reshape(heads // 2, 2, width, width)
    blank = jnp.zeros_like(pairs[:, 0])
    return jnp.concatenate(
        [
            jnp.concatenate([pairs[:, 0], blank], axis=2),
            jnp.concatenate([blank, pairs[:, 1]], axis=2),
        ],
        axis=1,
    )


def unblock_pairs(pairs):
    width = pairs.shape[1] // 2
    both = jnp.stack([pairs[:, :width, :width], pairs[:, width:, width:]], axis=1)
    return both.reshape(-1, width, width)


def per_device(
    size,
    tokens,
    norm1_gain,
    norm1_shift,
    w_query,
    w_key,
    w_value,
    w_out,
    fmap_query,
    fmap_key,
    norm2_gain,
    norm2_shift,
    w_fc,
    w_down,
    lengths,
    cotangent,
):
    rows, dim = tokens.shape
    heads = 2 * fmap_query.shape[0]
    width = fmap_query.shape[1]
    part = w_query.shape[1]
    slots = lengths.shape[1]
    count = rows // CHUNK
    core = lax.axis_index("mp")

    ends = jnp.cumsum(lengths[0])
    places = core * rows - 1 + jnp.arange(rows + 1, dtype=jnp.int32)
    numbers = jnp.sum((ends[None, :] <= places[:, None]).astype(jnp.int32), axis=1)
    numbers = jnp.where(places < 0, -1, numbers)
    segment = numbers[1:]
    living = places[1:] < ends[-1]
    blocks = segment.reshape(count, CHUNK)
    last = blocks[:, -1]
    before = jnp.concatenate([numbers[:1], last[:-1]])
    kept = (last == before).astype(F32)
    carry = (before == numbers[0]).astype(F32)
    reach = (blocks == before[:, None]).reshape(rows) & living
    written = (blocks == last[:, None]).reshape(rows)
    reach_in = (segment == numbers[0]) & living
    aux = jnp.stack([reach, written, reach_in, ~living] + [jnp.zeros_like(living)] * 4).astype(F32)
    order = jnp.arange(CHUNK, dtype=jnp.int32)
    mask = (
        (blocks[:, :, None] == blocks[:, None, :])
        & (order[:, None] <= order[None, :])
        & living.reshape(count, 1, CHUNK)
    ).astype(LOW)

    fq = block_pairs(jnp.concatenate([fmap_query, swap(fmap_query)], axis=0))
    fk = block_pairs(jnp.concatenate([fmap_key, swap(fmap_key)], axis=0))
    gain1, shift1 = norm1_gain[None, :], norm1_shift[None, :]
    gain2, shift2 = norm2_gain[None, :], norm2_shift[None, :]

    qkv_own, qkv_oth = gather(jnp.concatenate([w_query, w_key, w_value], axis=1), size)
    out_own, out_oth = gather(w_out, size)
    split = w_fc.shape[1] // 2
    groups = []
    for g in range(2):
        cut = slice(g * split, (g + 1) * split)
        own, oth = gather(jnp.concatenate([w_fc[:, cut], w_down[:, cut]], axis=1), size)
        groups.append((own[:, :split], oth[:, :split], own[:, split:], oth[:, split:]))

    normed1_t, q_t, k_t, v_nat, v_ext, phi_q, phi_k, phi_k_nat, prefix, final, v_sum = project(
        tokens,
        gain1,
        shift1,
        qkv_own,
        qkv_oth,
        fq.swapaxes(1, 2),
        fk.swapaxes(1, 2),
        aux,
        kept,
        heads,
        width,
    )
    entering = other_order(lax.ppermute(final, "mp", [(0, 1)]))
    center = (v_sum[0] + other_order(swap(v_sum[0]))) * (1.0 / (2 * rows))
    att_t, att_c, denom, hidden, normed2, normed2_t = attend(
        tokens, gain2, shift2, out_own, out_oth, aux, mask, phi_q, phi_k_nat, v_ext, prefix, entering, center[:, None], carry
    )
    cot_t = cotangent.T
    parts = []
    for fc_own, fc_oth, down_own, down_oth in groups:
        parts.append(
            feed_forward(normed2, normed2_t, cotangent, cot_t, fc_own, fc_oth, down_own, down_oth)
        )
    mixed, grad_hidden, d_gain2, d_shift2, g_ext, leaving, d_out_own, d_out_oth = middle(
        hidden,
        parts[0][0],
        parts[1][0],
        parts[0][1],
        parts[1][1],
        cotangent,
        gain2,
        out_own,
        out_oth,
        att_t,
        att_c,
        denom,
        phi_q,
        aux,
    )
    arriving = other_order(lax.ppermute(leaving, "mp", [(1, 0)]))
    gq_t, gk_t, gv_t, d_fq, d_fk = attend_back(
        aux,
        mask,
        phi_q,
        phi_k,
        phi_k_nat,
        v_nat,
        v_ext,
        g_ext,
        prefix,
        entering,
        arriving,
        q_t,
        k_t,
        fq,
        fk,
        center[:, None],
        center[None, :],
        carry,
        kept,
    )
    d_qkv = weight_grads(normed1_t, gq_t, gk_t, gv_t)
    grad_tokens, d_gain1, d_shift1 = first_back(
        tokens, gain1, grad_hidden, qkv_own, qkv_oth, gq_t, gk_t, gv_t
    )

    sums = []
    for members in parts:
        sums.append(
            scatter(
                jnp.concatenate([members[2], members[4]], axis=1),
                jnp.concatenate([members[3], members[5]], axis=1),
                size,
            )
        )
    grad_fc = jnp.concatenate([member[:, :split] for member in sums], axis=1)
    grad_down = jnp.concatenate([member[:, split:] for member in sums], axis=1)
    grad_out = scatter(d_out_own, d_out_oth, size)
    grad_qkv = scatter(d_qkv[:, : 3 * part], d_qkv[:, 3 * part :], size)
    d_fq = unblock_pairs(d_fq)
    d_fk = unblock_pairs(d_fk)
    local = heads // 2
    d_fq = d_fq[:local] + swap(d_fq[local:])
    d_fk = d_fk[:local] + swap(d_fk[local:])
    d_fq, d_fk = lax.psum((d_fq, d_fk), "dp")
    d_gain1, d_shift1, d_gain2, d_shift2 = lax.psum(
        (d_gain1[0], d_shift1[0], d_gain2[0], d_shift2[0]), ("dp", "mp")
    )
    return (
        mixed,
        grad_tokens,
        d_gain1,
        d_shift1,
        grad_qkv[:, :part],
        grad_qkv[:, part : 2 * part],
        grad_qkv[:, 2 * part :],
        grad_out,
        d_fq,
        d_fk,
        d_gain2,
        d_shift2,
        grad_fc,
        grad_down,
    )


def solution(mesh):
    placed = (
        P(("dp", "mp"), None),
        P(),
        P(),
        P("dp", "mp"),
        P("dp", "mp"),
        P("dp", "mp"),
        P("dp", "mp"),
        P("mp", None, None),
        P("mp", None, None),
        P(),
        P(),
        P("dp", "mp"),
        P("dp", "mp"),
        P("dp", None),
        P(("dp", "mp"), None),
    )
    return jax.shard_map(
        functools.partial(per_device, mesh.shape["dp"]),
        mesh=mesh,
        in_specs=placed,
        out_specs=(
            P(("dp", "mp"), None),
            P(("dp", "mp"), None),
            P(),
            P(),
            P("dp", "mp"),
            P("dp", "mp"),
            P("dp", "mp"),
            P("dp", "mp"),
            P("mp", None, None),
            P("mp", None, None),
            P(),
            P(),
            P("dp", "mp"),
            P("dp", "mp"),
        ),
        check_vma=False,
    )
```

time: 2180 us -> 500 us (0.23)
  waiting for transfers between devices: 983 us -> 126 us
  matrix products: 439 us -> 0 us
  local copies, waits for them, and re-layouts: 416 us -> 31.4 us
  blocking collectives: 215 us -> 41.6 us
  Pallas kernels: 0 us -> 152 us
  starting transfers between devices: 0.73 us -> 90.6 us
  other arithmetic: 86.4 us -> 37.5 us
    reduce_scatter x9 -> x0, waiting for transfers between devices: 673 us -> none  [the longest x1 143 us: per_device(): lax.psum_scatter(grad_fc, 'dp', scatter_dimension=0, tiled=True)]
    dot_general x94 -> x0, matrix products: 423 us -> none  [the longest x16 126 us: block_core(): scores = jnp.einsum('thf,shf->hts', phi_q, phi_k, precision=HIGH)]
    dynamic_update_slice x16 -> x0, local copies, waits for them, and re-layouts: 265 us -> none  [attend(): lax.scan(jax.checkpoint(block_core), initial, (phi_q, phi_k, blocked, seg...]
    all_gather x4 -> x0, blocking collectives: 175 us -> none  [the longest x1 48.5 us: per_device(): lax.all_gather(w_query, 'dp', axis=0, tiled=True)]
    pallas_call x0 -> x8, Pallas kernels: none -> 152 us  [the longest x2 52.2 us: feed_forward(): pl.pallas_call(feed_kernel, grid=(units // tile,), in_specs=[whole(normed...]
    all_gather x6 -> x0, waiting for transfers between devices: 145 us -> none  [the longest x1 67 us: per_device(): lax.all_gather(w_down, 'dp', axis=0, tiled=True)]
    ppermute x0 -> x71, waiting for transfers between devices: none -> 113 us  [the longest x32 81.5 us: flip(): return lax.ppermute(piece, 'dp', [(i, i ^ bit) for i in range(size)])]
    psum x1, waiting for transfers between devices: 112 us -> 13 us  [per_device(): d_fq, d_fk = lax.psum((d_fq, d_fk), 'dp')]
  transfers between devices with their start and end apart: 17 -> 72, of which waited for: 14 -> 35; matrix products, arithmetic and copies ran while one was open for 4% -> 13% of each run, Pallas kernels for 0% -> 31%
where the time goes in v1:
time: 500 us; the launch traced here: 495 us
  Pallas kernels  152 us (30%)
  waiting for transfers between devices  126 us (25%)
  starting transfers between devices  90.6 us (18%)
  blocking collectives  41.6 us (8%)
  other arithmetic  37.5 us (8%)
  local copies, waits for them, and re-layouts  31.4 us (6%)
  between operations  16 us (3%)
    ppermute x32, waiting for transfers between devices, flip(): return lax.ppermute(piece, 'dp', [(i, i ^ bit) for i in range(size)])  81.5 us
    pallas_call x2, Pallas kernels, feed_forward(): pl.pallas_call(feed_kernel, grid=(units // tile,), in_specs=[whole(normed...  52.2 us
    ppermute x32, starting transfers between devices, flip(): return lax.ppermute(piece, 'dp', [(i, i ^ bit) for i in range(size)])  43.4 us
    psum x1, blocking collectives, per_device(): lax.psum((d_gain1[0], d_shift1[0], d_gain2[0], d_shift2[0]), ('dp', 'mp'))  41.6 us
    ppermute x24, starting transfers between devices, turn(): lax.ppermute(piece, 'dp', [(i, (i + by) % size) for i in range(size)])  39.2 us
    ppermute x24, waiting for transfers between devices, turn(): lax.ppermute(piece, 'dp', [(i, (i + by) % size) for i in range(size)])  28.7 us
    pallas_call x1, Pallas kernels, attend_back(): pl.pallas_call(attend_back_kernel, grid_spec=pltpu.PrefetchScalarGridSpec...  26.9 us
    pallas_call x1, Pallas kernels, project(): pl.pallas_call(project_kernel, grid_spec=pltpu.PrefetchScalarGridSpec(num...  18.3 us
  transfers between devices with their start and end apart: 72, of which 35 were waited for; matrix products, arithmetic and copies ran while one was open for 13% of the time, Pallas kernels for 31%

profile of v1, /device:TPU:0, one launch (start us, length us, event | category | flops | bytes accessed | tf_op | source)
XLA Modules:
  0.0 495.0 jit_solution(11250848418312423717)
XLA Ops:
  8.5 5.1 %collective-permute-start.20 = (bf16[48,1536]{1,0:T(8,128)(2,1)S(1)}, bf16[48,1536]{1,0:T(8,128)(2,1)S(1)}, u32[]{:S(2)}, u32[]{:S(2)}) collective-permute-start(bf16[48,1536]{1,0:T(8,128)(2,1)S(1)} %pad_maximum_fusion.30), channel_id=1, source_target_pairs={{0,24},{2,26},{4,28},{6,30},{8,0},{10,2},{12,4},{14,6},{16,8},{18,... | collective-permute-start | bytes 442376 | tf_op jit(solution)/shard_map/ppermute | solution.py:747
  31.8 3.9 collective-permute-start.8
  47.9 3.8 collective-permute-done.10
  53.4 3.0 collective-permute-done.3
  58.0 3.0 collective-permute-done.5
  70.8 5.9 %collective-permute-done.4 = bf16[4,2,48,192]{3,2,1,0:T(8,128)(2,1)S(1)} collective-permute-done((bf16[4,2,48,192]{3,2,1,0:T(8,128)(2,1)S(1)}, bf16[4,2,48,192]{3,2,1,0:T(8,128)(2,1)S(1)}, u32[]{:S(2)}, u32[]{:S(2)}) %collective-permute-start.4) | collective-permute-done | bytes 147488 | tf_op jit(solution)/shard_map/ppermute | solution.py:743
  90.0 5.5 %collective-permute-done.12 = bf16[4,2,48,576]{3,2,1,0:T(8,128)(2,1)S(1)} collective-permute-done((bf16[4,2,48,576]{3,2,1,0:T(8,128)(2,1)S(1)}, bf16[4,2,48,576]{3,2,1,0:T(8,128)(2,1)S(1)}, u32[]{:S(2)}, u32[]{:S(2)}) %collective-permute-start.12) | collective-permute-done | bytes 442400 | tf_op jit(solution)/shard_map/ppermute | solution.py:743
  101.4 10.1 %collective-permute-done.26 = bf16[4,2,48,768]{3,2,1,0:T(8,128)(2,1)S(1)} collective-permute-done((bf16[4,2,48,768]{3,2,1,0:T(8,128)(2,1)S(1)}, bf16[4,2,48,768]{3,2,1,0:T(8,128)(2,1)S(1)}, u32[]{:S(2)}, u32[]{:S(2)}) %collective-permute-start.26) | collective-permute-done | bytes 589856 | tf_op jit(solution)/shard_map/ppermute | solution.py:743
  115.0 7.4 %collective-permute-done.34 = bf16[4,2,48,768]{3,2,1,0:T(8,128)(2,1)S(1)} collective-permute-done((bf16[4,2,48,768]{3,2,1,0:T(8,128)(2,1)S(1)}, bf16[4,2,48,768]{3,2,1,0:T(8,128)(2,1)S(1)}, u32[]{:S(2)}, u32[]{:S(2)}) %collective-permute-start.34) | collective-permute-done | bytes 589856 | tf_op jit(solution)/shard_map/ppermute | solution.py:743
  124.4 18.3 %project.1 = (bf16[768,1024]{1,0:T(8,128)(2,1)}, bf16[768,1024]{1,0:T(8,128)(2,1)}, bf16[768,1024]{1,0:T(8,128)(2,1)}, bf16[1024,768]{1,0:T(8,128)(2,1)}, bf16[1...) custom-call(f32[4]{0:T(128)} %get-tuple-element.110.kept, ...), custom_call_target="tpu_custom_call" | custom-call | flops 10871635968 | bytes 20971520 | tf_op jit(solution)/shard_map/project/pallas_call | solution.py:156
  145.6 3.2 collective-permute-start.18
  152.7 18.2 %attend.1 = (bf16[768,1024]{1,0:T(8,128)(2,1)}, bf16[768,1024]{1,0:T(8,128)(2,1)}, f32[16,1024]{1,0:T(8,128)}, f32[1024,768]{1,0:T(8,128)}, bf16[1024,768]{1,0:T(8,128)(2,1)}, /*index=5*/bf16[768,1024]{1,0:T(8,128)(2,1)}) custom-call(f32[4]{0:T(128)} %compare_convert_fusion.1.carry, bf16[1024,768]{1,0:T(8,128)(2,1)} %tokens.5, ...), custom_call_target="tpu_custom_call" | custom-call | flops 7247757312 | bytes 20971520 | tf_op jit(solution)/shard_map/attend/pallas_call | solution.py:260
  170.9 3.3 fusion.71
  174.1 26.0 %feed.2 = (f32[1024,768]{1,0:T(8,128)}, f32[1024,768]{1,0:T(8,128)}, bf16[768,768]{1,0:T(8,128)(2,1)}, bf16[768,768]{1,0:T(8,128)(2,1)}, bf16[768,768]{1,0:T(8,128)(2,1)}, /*index=5*/bf16[768,768]{1,0:T(8,128)(2,1)}) custom-call(bf16[1024,768]{1,0:T(8,128)(2,1)} %get-tuple-element.66.normed, bf16[768,1024]{1,0:T(8,128)(2,1)} %get-tuple-element.67.normed_t, ...), custom_call_target="tpu_custom_call" | custom-call | flops 14495514624 | bytes 25165824 | tf_op jit(solution)/shard_map/feed/pallas_call | solution.py:359
  200.2 3.2 pad_maximum_fusion.2
  205.3 26.2 %feed.3 = (f32[1024,768]{1,0:T(8,128)}, f32[1024,768]{1,0:T(8,128)}, bf16[768,768]{1,0:T(8,128)(2,1)}, bf16[768,768]{1,0:T(8,128)(2,1)}, bf16[768,768]{1,0:T(8,128)(2,1)}, /*index=5*/bf16[768,768]{1,0:T(8,128)(2,1)}) custom-call(bf16[1024,768]{1,0:T(8,128)(2,1)} %get-tuple-element.66.normed, bf16[768,1024]{1,0:T(8,128)(2,1)} %get-tuple-element.67.normed_t, ...), custom_call_target="tpu_custom_call" | custom-call | flops 14495514624 | bytes 25165824 | tf_op jit(solution)/shard_map/feed/pallas_call | solution.py:359
  231.5 17.1 %middle.1 = (bf16[1024,768]{1,0:T(8,128)(2,1)}, f32[1024,768]{1,0:T(8,128)}, f32[1,768]{1,0:T(1,128)}, f32[1,768]{1,0:T(1,128)}, bf16[12,80,1024]{2,1,0:T(8,128)...) custom-call(f32[1024,768]{1,0:T(8,128)} %get-tuple-element.65.hidden, ...), custom_call_target="tpu_custom_call" | custom-call | flops 3623878656 | bytes 25165824 | tf_op jit(solution)/shard_map/middle/pallas_call | solution.py:471
  254.9 26.9 %attend_back.1 = (bf16[768,1024]{1,0:T(8,128)(2,1)}, bf16[768,1024]{1,0:T(8,128)(2,1)}, bf16[768,1024]{1,0:T(8,128)(2,1)}, f32[6,128,128]{2,1,0:T(8,128)}, f32[6,128,128]{2,1,0:T(8,128)}) custom-call(f32[4]{0:T(128)} %compare_convert_fusion.1.carry, f32[4]{0:T(128)} %get-tuple-element.110.kept, f32[8,1024]{1,0:T(8,128)} %convert_element_type.305.aux, ...), custom_call_target="tpu_custom_call" | custom-call | flops 8053063680 | bytes 25165824 | tf_op jit(solution)/shard_map/attend_back/pallas_call | solution.py:618
  285.2 9.1 %weight_grads.1 = bf16[768,2304]{1,0:T(8,128)(2,1)} custom-call(bf16[768,1024]{1,0:T(8,128)(2,1)} %get-tuple-element.89.normed_t, bf16[768,1024]{1,0:T(8,128)(2,1)} %get-tuple-element.83.gq_t, bf16[768,1024]{1,0:T(8,128)(2,1)} %get-tuple-element.84.gk_t, bf16[768,1024]{1,0:T(8,128)(2,1)} %get-tuple-element.85.gv_t), custom_call_target="tpu_custom_call" | custom-call | flops 3623878656 | bytes 10485760 | tf_op jit(solution)/shard_map/weight_grads/pallas_call | solution.py:670
  294.3 2.9 slice.271
  297.3 10.5 %first_back.1 = (bf16[1024,768]{1,0:T(8,128)(2,1)}, f32[1,768]{1,0:T(1,128)}, f32[1,768]{1,0:T(1,128)}) custom-call(bf16[1024,768]{1,0:T(8,128)(2,1)} %tokens.5, f32[1,768]{1,0:T(1,128)} %broadcast_in_dim.28.gain, f32[1024,768]{1,0:T(8,128)} %get-tuple-element.76.grad_hidden, bf16[768,1152]{1,0:T(8,128)(2,1)} %copy-done.7, bf16[768,1152]{1,0:T(8,128)(2,1)} %copy-done.30, ...), custom_call_target="tpu_custom_call" | custom-call | flops 3623878656 | bytes 14680064 | tf_op jit(solution)/shard_map/first_back/pallas_call | solution.py:717
  309.1 41.6 %all-reduce.4 = (f32[768]{0:T(1024)}, f32[768]{0:T(1024)}, f32[768]{0:T(1024)}, f32[768]{0:T(1024)}) all-reduce(f32[768]{0:T(1024)S(1)} %reduce.4, f32[768]{0:T(1024)S(1)} %reduce.5, f32[768]{0:T(1024)S(1)} %reduce.6, f32[768]{0:T(1024)S(1)} %reduce.7), channel_id=1, replica_groups=mesh['dp'=16,'mp'=2] {'dp','mp'}, use_global_device_ids=true, to_apply=%region_2.3 | all-reduce | flops 3072 | bytes 24576 | tf_op jit(solution)/shard_map/psum | solution.py:981
  351.1 2.9 collective-permute-start.48
  363.0 3.2 collective-permute-done.47
  387.1 5.1 %collective-permute-done.40 = bf16[4,2,48,576]{3,2,0,1:T(8,128)(2,1)S(1)} collective-permute-done((bf16[4,2,48,576]{3,2,0,1:T(8,128)(2,1)S(1)}, bf16[4,2,48,576]{3,2,0,1:T(8,128)(2,1)S(1)}, u32[]{:S(2)}, u32[]{:S(2)}) %collective-permute-start.40) | collective-permute-done | bytes 442400 | tf_op jit(solution)/shard_map/ppermute | solution.py:743
  394.8 14.9 %collective-permute-done.41 = bf16[4,48,576]{2,1,0:T(8,128)(2,1)S(1)} collective-permute-done((bf16[4,48,576]{2,1,0:T(8,128)(2,1)S(1)}, bf16[4,48,576]{2,1,0:T(8,128)(2,1)S(1)}, u32[]{:S(2)}, u32[]{:S(2)}) %collective-permute-start.41) | collective-permute-done | bytes 221216 | tf_op jit(solution)/shard_map/ppermute | solution.py:743
  425.5 8.7 %collective-permute-done.66 = bf16[4,2,48,768]{3,2,0,1:T(8,128)(2,1)S(1)} collective-permute-done((bf16[4,2,48,768]{3,2,0,1:T(8,128)(2,1)S(1)}, bf16[4,2,48,768]{3,2,0,1:T(8,128)(2,1)S(1)}, u32[]{:S(2)}, u32[]{:S(2)}) %collective-permute-start.66) | collective-permute-done | bytes 589856 | tf_op jit(solution)/shard_map/ppermute | solution.py:743
  438.9 3.8 collective-permute-done.59
  445.5 3.4 collective-permute-start.61
  456.1 5.7 %collective-permute-done.61 = bf16[48,1536]{1,0:T(8,128)(2,1)S(1)} collective-permute-done((bf16[48,1536]{1,0:T(8,128)(2,1)S(1)}, bf16[48,1536]{1,0:T(8,128)(2,1)S(1)}, u32[]{:S(2)}, u32[]{:S(2)}) %collective-permute-start.61) | collective-permute-done | bytes 147488 | tf_op jit(solution)/shard_map/ppermute | solution.py:747
  462.2 7.9 %collective-permute-done.69 = bf16[48,1536]{1,0:T(8,128)(2,1)S(1)} collective-permute-done((bf16[48,1536]{1,0:T(8,128)(2,1)S(1)}, bf16[48,1536]{1,0:T(8,128)(2,1)S(1)}, u32[]{:S(2)}, u32[]{:S(2)}) %collective-permute-start.69) | collective-permute-done | bytes 147488 | tf_op jit(solution)/shard_map/ppermute | solution.py:747
  471.6 13.0 %all-reduce.8.cloned.1.call-done = (f32[6,64,64]{2,1,0:T(8,128)}, f32[6,64,64]{2,1,0:T(8,128)}) async-done(((f32[6,64,64]{2,1,0:T(8,128)}, f32[6,64,64]{2,1,0:T(8,128)}), (f32[6,64,64]{2,1,0:T(8,128)}, f32[6,64,64]{2,1,0:T(8,128)})) %all-reduce.8.cloned.1.call-update) | async-done | bytes 196624 | tf_op jit(solution)/shard_map/psum | solution.py:980
  (406 shorter events, 156.3 us)
Async XLA Ops:
  7.3 477.4 %all-reduce.8.cloned.1.call-start = ((), (), s32[]{:S(2)}) async-start(), calls=%async_computation | async-start | bytes 786432 | tf_op jit(solution)/shard_map/psum | solution.py:980
  8.5 52.8 %collective-permute-start.20 = (bf16[48,1536]{1,0:T(8,128)(2,1)S(1)}, bf16[48,1536]{1,0:T(8,128)(2,1)S(1)}, u32[]{:S(2)}, u32[]{:S(2)}) collective-permute-start(bf16[48,1536]{1,0:T(8,128)(2,1)S(1)} %pad_maximum_fusion.30), channel_id=1, source_target_pairs={{0,24},{2,26},{4,28},{6,30},{8,0},{10,2},{12,4},{14,6},{16,8},{18,... | collective-permute-start | bytes 442376 | tf_op jit(solution)/shard_map/ppermute | solution.py:747
  13.6 48.2 %collective-permute-start.21 = (bf16[48,1536]{1,0:T(8,128)(2,1)S(1)}, bf16[48,1536]{1,0:T(8,128)(2,1)S(1)}, u32[]{:S(2)}, u32[]{:S(2)}) collective-permute-start(bf16[48,1536]{1,0:T(8,128)(2,1)S(1)} %pad_maximum_fusion.30), channel_id=1, source_target_pairs={{0,16},{2,18},{4,20},{6,22},{8,24},{10,26},{12,28},{14,30},{16,0},... | collective-permute-start | bytes 442376 | tf_op jit(solution)/shard_map/ppermute | solution.py:747
  13.6 50.1 %collective-permute-start.22 = (bf16[48,1536]{1,0:T(8,128)(2,1)S(1)}, bf16[48,1536]{1,0:T(8,128)(2,1)S(1)}, u32[]{:S(2)}, u32[]{:S(2)}) collective-permute-start(bf16[48,1536]{1,0:T(8,128)(2,1)S(1)} %pad_maximum_fusion.30), channel_id=1, source_target_pairs={{0,8},{2,10},{4,12},{6,14},{8,16},{10,18},{12,20},{14,22},{16,24},... | collective-permute-start | bytes 442376 | tf_op jit(solution)/shard_map/ppermute | solution.py:747
  14.6 17.2 %collective-permute-start = (bf16[48,384]{1,0:T(8,128)(2,1)}, bf16[48,384]{1,0:T(8,128)(2,1)S(1)}, u32[]{:S(2)}, u32[]{:S(2)}) collective-permute-start(bf16[48,384]{1,0:T(8,128)(2,1)} %param.21), channel_id=1, source_target_pairs={{0,24},{2,26},{4,28},{6,30},{8,0},{10,2},{12,4},{14,6},{16,8},{18,... | collective-permute-start | bytes 110600 | tf_op jit(solution)/shard_map/ppermute | solution.py:747
  46.2 19.1 %collective-permute-start.28 = (bf16[48,1536]{1,0:T(8,128)(2,1)S(1)}, bf16[48,1536]{1,0:T(8,128)(2,1)S(1)}, u32[]{:S(2)}, u32[]{:S(2)}) collective-permute-start(bf16[48,1536]{1,0:T(8,128)(2,1)S(1)} %pad_maximum_fusion.31), channel_id=1, source_target_pairs={{0,24},{2,26},{4,28},{6,30},{8,0},{10,2},{12,4},{14,6},{16,8},{18,... | collective-permute-start | bytes 442376 | tf_op jit(solution)/shard_map/ppermute | solution.py:747
  61.7 17.0 %collective-permute-start.11 = (bf16[4,48,576]{2,1,0:T(8,128)(2,1)S(1)}, bf16[4,48,576]{2,1,0:T(8,128)(2,1)S(1)}, u32[]{:S(2)}, u32[]{:S(2)}) collective-permute-start(bf16[4,48,576]{2,1,0:T(8,128)(2,1)S(1)} %bitcast.340), channel_id=1, source_target_pairs={{0,2},{2,0},{4,6},{6,4},{8,10},{10,8},{12,14},{14,12},{16,18},{18,... | collective-permute-start | bytes 663560 | tf_op jit(solution)/shard_map/ppermute | solution.py:743
  63.6 17.3 %collective-permute-start.13 = (bf16[4,48,576]{2,1,0:T(8,128)(2,1)S(1)}, bf16[4,48,576]{2,1,0:T(8,128)(2,1)S(1)}, u32[]{:S(2)}, u32[]{:S(2)}) collective-permute-start(bf16[4,48,576]{2,1,0:T(8,128)(2,1)S(1)} %bitcast.338), channel_id=1, source_target_pairs={{0,4},{2,6},{4,0},{6,2},{8,12},{10,14},{12,8},{14,10},{16,20},{18,... | collective-permute-start | bytes 663560 | tf_op jit(solution)/shard_map/ppermute | solution.py:743
  80.9 71.8 %collective-permute-start.7 = (bf16[768,384]{1,0:T(8,128)(2,1)S(1)}, bf16[768,384]{1,0:T(8,128)(2,1)}, u32[]{:S(2)}, u32[]{:S(2)}) collective-permute-start(bf16[768,384]{1,0:T(8,128)(2,1)S(1)} %pad_maximum_fusion.11.w_own), channel_id=1, source_target_pairs={{0,1},{1,0},{2,3},{3,2},{4,5},{5,4},{6,7},{7,6},{8,9},{9,8},{10,11... | collective-permute-start | bytes 1769480 | tf_op jit(solution)/shard_map/ppermute | solution.py:739
  84.9 26.6 %collective-permute-start.26 = (bf16[4,2,48,768]{3,2,1,0:T(8,128)(2,1)S(1)}, bf16[4,2,48,768]{3,2,1,0:T(8,128)(2,1)S(1)}, u32[]{:S(2)}, u32[]{:S(2)}) collective-permute-start(bf16[4,2,48,768]{3,2,1,0:T(8,128)(2,1)S(1)} %pad_maximum_fusion.13), channel_id=1, source_target_pairs={{0,2},{2,0},{4,6},{6,4},{8,10},{10,8},{12,14},{14,12},{16,18},{18,... | collective-permute-start | bytes 1769480 | tf_op jit(solution)/shard_map/ppermute | solution.py:743
  88.3 23.5 %collective-permute-start.24 = (bf16[4,2,48,768]{3,2,1,0:T(8,128)(2,1)S(1)}, bf16[4,2,48,768]{3,2,1,0:T(8,128)(2,1)S(1)}, u32[]{:S(2)}, u32[]{:S(2)}) collective-permute-start(bf16[4,2,48,768]{3,2,1,0:T(8,128)(2,1)S(1)} %pad_maximum_fusion.12), channel_id=1, source_target_pairs={{0,4},{2,6},{4,0},{6,2},{8,12},{10,14},{12,8},{14,10},{16,20},{18,... | collective-permute-start | bytes 1769480 | tf_op jit(solution)/shard_map/ppermute | solution.py:743
  95.5 26.8 %collective-permute-start.34 = (bf16[4,2,48,768]{3,2,1,0:T(8,128)(2,1)S(1)}, bf16[4,2,48,768]{3,2,1,0:T(8,128)(2,1)S(1)}, u32[]{:S(2)}, u32[]{:S(2)}) collective-permute-start(bf16[4,2,48,768]{3,2,1,0:T(8,128)(2,1)S(1)} %pad_maximum_fusion.15), channel_id=1, source_target_pairs={{0,2},{2,0},{4,6},{6,4},{8,10},{10,8},{12,14},{14,12},{16,18},{18,... | collective-permute-start | bytes 1769480 | tf_op jit(solution)/shard_map/ppermute | solution.py:743
  98.8 23.8 %collective-permute-start.32 = (bf16[4,2,48,768]{3,2,1,0:T(8,128)(2,1)S(1)}, bf16[4,2,48,768]{3,2,1,0:T(8,128)(2,1)S(1)}, u32[]{:S(2)}, u32[]{:S(2)}) collective-permute-start(bf16[4,2,48,768]{3,2,1,0:T(8,128)(2,1)S(1)} %pad_maximum_fusion.14), channel_id=1, source_target_pairs={{0,4},{2,6},{4,0},{6,2},{8,12},{10,14},{12,8},{14,10},{16,20},{18,... | collective-permute-start | bytes 1769480 | tf_op jit(solution)/shard_map/ppermute | solution.py:743
  114.5 56.4 %collective-permute-start.27 = (bf16[768,1536]{1,0:T(8,128)(2,1)}, bf16[768,1536]{1,0:T(8,128)(2,1)}, u32[]{:S(2)}, u32[]{:S(2)}) collective-permute-start(bf16[768,1536]{1,0:T(8,128)(2,1)} %pad_maximum_fusion), channel_id=1, source_target_pairs={{0,1},{1,0},{2,3},{3,2},{4,5},{5,4},{6,7},{7,6},{8,9},{9,8},{10,11... | collective-permute-start | bytes 7077896 | tf_op jit(solution)/shard_map/ppermute | solution.py:739
  145.1 58.6 %collective-permute-start.35 = (bf16[768,1536]{1,0:T(8,128)(2,1)}, bf16[768,1536]{1,0:T(8,128)(2,1)S(1)}, u32[]{:S(2)}, u32[]{:S(2)}) collective-permute-start(bf16[768,1536]{1,0:T(8,128)(2,1)} %pad_maximum_fusion.1), channel_id=1, source_target_pairs={{0,1},{1,0},{2,3},{3,2},{4,5},{5,4},{6,7},{7,6},{8,9},{9,8},{10,11... | collective-permute-start | bytes 7077896 | tf_op jit(solution)/shard_map/ppermute | solution.py:739
  203.4 177.0 %collective-permute-start.55 = (bf16[768,1536]{1,0:T(8,128)(2,1)}, bf16[768,1536]{1,0:T(8,128)(2,1)}, u32[]{:S(2)}, u32[]{:S(2)}) collective-permute-start(bf16[768,1536]{1,0:T(8,128)(2,1)} %pad_maximum_fusion.2), channel_id=1, source_target_pairs={{0,1},{1,0},{2,3},{3,2},{4,5},{5,4},{6,7},{7,6},{8,9},{9,8},{10,11... | collective-permute-start | bytes 7077896 | tf_op jit(solution)/shard_map/ppermute | solution.py:739
  249.8 100.9 %collective-permute-start.45 = (bf16[768,384]{1,0:T(8,128)(2,1)}, bf16[768,384]{1,0:T(8,128)(2,1)S(1)}, u32[]{:S(2)}, u32[]{:S(2)}) collective-permute-start(bf16[768,384]{1,0:T(8,128)(2,1)} %get-tuple-element.91), channel_id=1, source_target_pairs={{0,1},{1,0},{2,3},{3,2},{4,5},{5,4},{6,7},{7,6},{8,9},{9,8},{10,11... | collective-permute-start | bytes 1769480 | tf_op jit(solution)/shard_map/ppermute | solution.py:739
  283.1 71.0 %collective-permute-start.54 = (f32[6,64,64]{2,1,0:T(8,128)S(1)}, f32[6,64,64]{2,1,0:T(8,128)S(1)}, u32[]{:S(2)}, u32[]{:S(2)}) collective-permute-start(f32[6,64,64]{2,1,0:T(8,128)S(1)} %bitcast.354), channel_id=1, source_target_pairs={{0,1},{1,0},{2,3},{3,2},{4,5},{5,4},{6,7},{7,6},{8,9},{9,8},{10,11... | collective-permute-start | bytes 294920 | tf_op jit(solution)/shard_map/ppermute | solution.py:739
  284.0 85.1 %collective-permute-start.53 = (f32[6,64,64]{2,1,0:T(8,128)}, f32[6,64,64]{2,1,0:T(8,128)}, u32[]{:S(2)}, u32[]{:S(2)}) collective-permute-start(f32[6,64,64]{2,1,0:T(8,128)} %bitcast.106), channel_id=1, source_target_pairs={{0,1},{1,0},{2,3},{3,2},{4,5},{5,4},{6,7},{7,6},{8,9},{9,8},{10,11... | collective-permute-start | bytes 294920 | tf_op jit(solution)/shard_map/ppermute | solution.py:739
  297.2 78.2 %collective-permute-start.37 = (bf16[768,1152]{1,0:T(8,128)(2,1)}, bf16[768,1152]{1,0:T(8,128)(2,1)}, u32[]{:S(2)}, u32[]{:S(2)}) collective-permute-start(bf16[768,1152]{1,0:T(8,128)(2,1)} %slice.271), channel_id=1, source_target_pairs={{0,1},{1,0},{2,3},{3,2},{4,5},{5,4},{6,7},{7,6},{8,9},{9,8},{10,11... | collective-permute-start | bytes 5308424 | tf_op jit(solution)/shard_map/ppermute | solution.py:739
  378.3 15.5 %collective-permute-start.38 = (bf16[4,2,48,576]{3,2,0,1:T(8,128)(2,1)S(1)}, bf16[4,2,48,576]{3,2,0,1:T(8,128)(2,1)S(1)}, u32[]{:S(2)}, u32[]{:S(2)}) collective-permute-start(bf16[4,2,48,576]{3,2,0,1:T(8,128)(2,1)S(1)} %bitcast.348), channel_id=1, source_target_pairs={{0,2},{2,0},{4,6},{6,4},{8,10},{10,8},{12,14},{14,12},{16,18},{18,... | collective-permute-start | bytes 1327112 | tf_op jit(solution)/shard_map/ppermute | solution.py:743
  383.0 40.7 %collective-permute-start.58 = (bf16[4,2,48,768]{3,2,0,1:T(8,128)(2,1)S(1)}, bf16[4,2,48,768]{3,2,0,1:T(8,128)(2,1)S(1)}, u32[]{:S(2)}, u32[]{:S(2)}) collective-permute-start(bf16[4,2,48,768]{3,2,0,1:T(8,128)(2,1)S(1)} %bitcast.345), channel_id=1, source_target_pairs={{0,4},{2,6},{4,0},{6,2},{8,12},{10,14},{12,8},{14,10},{16,20},{18,... | collective-permute-start | bytes 1769480 | tf_op jit(solution)/shard_map/ppermute | solution.py:743
  384.5 39.9 %collective-permute-start.56 = (bf16[4,2,48,768]{3,2,0,1:T(8,128)(2,1)S(1)}, bf16[4,2,48,768]{3,2,0,1:T(8,128)(2,1)S(1)}, u32[]{:S(2)}, u32[]{:S(2)}) collective-permute-start(bf16[4,2,48,768]{3,2,0,1:T(8,128)(2,1)S(1)} %bitcast.344), channel_id=1, source_target_pairs={{0,2},{2,0},{4,6},{6,4},{8,10},{10,8},{12,14},{14,12},{16,18},{18,... | collective-permute-start | bytes 1769480 | tf_op jit(solution)/shard_map/ppermute | solution.py:743
  392.4 17.3 %collective-permute-start.41 = (bf16[4,48,576]{2,1,0:T(8,128)(2,1)S(1)}, bf16[4,48,576]{2,1,0:T(8,128)(2,1)S(1)}, u32[]{:S(2)}, u32[]{:S(2)}) collective-permute-start(bf16[4,48,576]{2,1,0:T(8,128)(2,1)S(1)} %dynamic-slice_bitcast_fusion.4), channel_id=1, source_target_pairs={{0,2},{2,0},{4,6},{6,4},{8,10},{10,8},{12,14},{14,12},{16,18},{18,... | collective-permute-start | bytes 663560 | tf_op jit(solution)/shard_map/ppermute | solution.py:743
  393.9 15.8 %collective-permute-start.39 = (bf16[4,48,576]{2,1,0:T(8,128)(2,1)S(1)}, bf16[4,48,576]{2,1,0:T(8,128)(2,1)S(1)}, u32[]{:S(2)}, u32[]{:S(2)}) collective-permute-start(bf16[4,48,576]{2,1,0:T(8,128)(2,1)S(1)} %dynamic-slice_bitcast_fusion.5), channel_id=1, source_target_pairs={{0,4},{2,6},{4,0},{6,2},{8,12},{10,14},{12,8},{14,10},{16,20},{18,... | collective-permute-start | bytes 663560 | tf_op jit(solution)/shard_map/ppermute | solution.py:743
  417.8 16.5 %collective-permute-start.66 = (bf16[4,2,48,768]{3,2,0,1:T(8,128)(2,1)S(1)}, bf16[4,2,48,768]{3,2,0,1:T(8,128)(2,1)S(1)}, u32[]{:S(2)}, u32[]{:S(2)}) collective-permute-start(bf16[4,2,48,768]{3,2,0,1:T(8,128)(2,1)S(1)} %bitcast.346), channel_id=1, source_target_pairs={{0,4},{2,6},{4,0},{6,2},{8,12},{10,14},{12,8},{14,10},{16,20},{18,... | collective-permute-start | bytes 1769480 | tf_op jit(solution)/shard_map/ppermute | solution.py:743
  421.4 16.4 %collective-permute-start.64 = (bf16[4,2,48,768]{3,2,0,1:T(8,128)(2,1)S(1)}, bf16[4,2,48,768]{3,2,0,1:T(8,128)(2,1)S(1)}, u32[]{:S(2)}, u32[]{:S(2)}) collective-permute-start(bf16[4,2,48,768]{3,2,0,1:T(8,128)(2,1)S(1)} %bitcast.347), channel_id=1, source_target_pairs={{0,2},{2,0},{4,6},{6,4},{8,10},{10,8},{12,14},{14,12},{16,18},{18,... | collective-permute-start | bytes 1769480 | tf_op jit(solution)/shard_map/ppermute | solution.py:743
  423.8 18.8 %collective-permute-start.59 = (bf16[4,48,768]{2,1,0:T(8,128)(2,1)S(1)}, bf16[4,48,768]{2,1,0:T(8,128)(2,1)S(1)}, u32[]{:S(2)}, u32[]{:S(2)}) collective-permute-start(bf16[4,48,768]{2,1,0:T(8,128)(2,1)S(1)} %dynamic-slice_bitcast_fusion.2), channel_id=1, source_target_pairs={{0,2},{2,0},{4,6},{6,4},{8,10},{10,8},{12,14},{14,12},{16,18},{18,... | collective-permute-start | bytes 884744 | tf_op jit(solution)/shard_map/ppermute | solution.py:743
  424.6 18.1 %collective-permute-start.57 = (bf16[4,48,768]{2,1,0:T(8,128)(2,1)S(1)}, bf16[4,48,768]{2,1,0:T(8,128)(2,1)S(1)}, u32[]{:S(2)}, u32[]{:S(2)}) collective-permute-start(bf16[4,48,768]{2,1,0:T(8,128)(2,1)S(1)} %dynamic-slice_bitcast_fusion.3), channel_id=1, source_target_pairs={{0,4},{2,6},{4,0},{6,2},{8,12},{10,14},{12,8},{14,10},{16,20},{18,... | collective-permute-start | bytes 884744 | tf_op jit(solution)/shard_map/ppermute | solution.py:743
  445.5 16.4 %collective-permute-start.61 = (bf16[48,1536]{1,0:T(8,128)(2,1)S(1)}, bf16[48,1536]{1,0:T(8,128)(2,1)S(1)}, u32[]{:S(2)}, u32[]{:S(2)}) collective-permute-start(bf16[48,1536]{1,0:T(8,128)(2,1)S(1)} %get-tuple-element.155), channel_id=1, source_target_pairs={{0,16},{2,18},{4,20},{6,22},{8,24},{10,26},{12,28},{14,30},{16,0},... | collective-permute-start | bytes 442376 | tf_op jit(solution)/shard_map/ppermute | solution.py:747
  451.1 18.9 %collective-permute-start.69 = (bf16[48,1536]{1,0:T(8,128)(2,1)S(1)}, bf16[48,1536]{1,0:T(8,128)(2,1)S(1)}, u32[]{:S(2)}, u32[]{:S(2)}) collective-permute-start(bf16[48,1536]{1,0:T(8,128)(2,1)S(1)} %get-tuple-element.158), channel_id=1, source_target_pairs={{0,16},{2,18},{4,20},{6,22},{8,24},{10,26},{12,28},{14,30},{16,0},... | collective-permute-start | bytes 442376 | tf_op jit(solution)/shard_map/ppermute | solution.py:747
  453.3 16.8 %collective-permute-start.70 = (bf16[48,1536]{1,0:T(8,128)(2,1)S(1)}, bf16[48,1536]{1,0:T(8,128)(2,1)S(1)}, u32[]{:S(2)}, u32[]{:S(2)}) collective-permute-start(bf16[48,1536]{1,0:T(8,128)(2,1)S(1)} %get-tuple-element.159), channel_id=1, source_target_pairs={{0,24},{2,26},{4,28},{6,30},{8,0},{10,2},{12,4},{14,6},{16,8},{18,... | collective-permute-start | bytes 442376 | tf_op jit(solution)/shard_map/ppermute | solution.py:747
  (71 other events, 723.6 us)
Sparse Core Ops, SparseCore 0:
  372.9 111.7 all-reduce.7

commit v2 on v0

v2 whole, which is shorter than its diff:
```python
import functools

import jax
import jax.numpy as jnp
from jax import lax
from jax.experimental import pallas as pl
from jax.experimental.pallas import tpu as pltpu
from jax.sharding import PartitionSpec as P

EPS = 1e-05
CHUNK = 256
EXT = 80
LOW = jnp.bfloat16
F32 = jnp.float32
MIB = 1024 * 1024
PACE = 3_000_000_000
GELU_C = 0.7978845608028654
GELU_A = 0.044715


def nn(a, b):
    return lax.dot_general(a, b, (((1,), (0,)), ((), ())), preferred_element_type=F32)


def nt(a, b):
    return lax.dot_general(a, b, (((1,), (1,)), ((), ())), preferred_element_type=F32)


def tn(a, b):
    return lax.dot_general(a, b, (((0,), (0,)), ((), ())), preferred_element_type=F32)


def norm_parts(rows):
    center = rows - jnp.mean(rows, axis=-1, keepdims=True)
    spread = jnp.mean(center * center, axis=-1, keepdims=True)
    rstd = lax.rsqrt(spread + EPS)
    return center * rstd, rstd


def norm_back(grad, xhat, rstd, gain):
    e = grad * gain
    return rstd * (
        e - jnp.mean(e, axis=-1, keepdims=True) - xhat * jnp.mean(e * xhat, axis=-1, keepdims=True)
    )


def softmax_pair(logits):
    high = jnp.max(logits, axis=0, keepdims=True)
    least = jnp.min(logits, axis=0, keepdims=True)
    pos = jnp.exp(logits - high)
    neg = jnp.exp(least - logits)
    pos = pos * (1.0 / jnp.sum(pos, axis=0, keepdims=True))
    neg = neg * (1.0 / jnp.sum(neg, axis=0, keepdims=True))
    return jnp.concatenate([pos, neg], axis=0).astype(LOW)


def softmax_pair_back(phi, grad):
    width = phi.shape[0] // 2
    pos = phi[:width].astype(F32)
    neg = phi[width:].astype(F32)
    gp = grad[:width]
    gn = grad[width:]
    gp = gp - jnp.sum(pos * gp, axis=0, keepdims=True)
    gn = gn - jnp.sum(neg * gn, axis=0, keepdims=True)
    return pos * gp - neg * gn


def flat(value):
    return value.reshape(-1, value.shape[-1])


def kept_in_vmem(shape, dtype):
    return pltpu.VMEM(shape, dtype)


def streamed(shape, dtype):
    return pltpu.HBM(shape, dtype)


def apart(*arrays):
    return tuple(pltpu.with_memory_space_constraint(a, pltpu.HBM) for a in arrays)


def pinned(*arrays):
    return tuple(pltpu.with_memory_space_constraint(a, pltpu.VMEM) for a in arrays)


def whole(array):
    return pl.BlockSpec(
        array.shape, lambda *_: (0,) * array.ndim, pipeline_mode=pl.Buffered(1)
    )


def fixed(*shape):
    return pl.BlockSpec(shape, lambda *_: (0,) * len(shape))


STAYS = pl.BlockSpec(memory_space=pltpu.VMEM)


def at(step, size):
    return pl.ds(pl.multiple_of(step * size, size), size)


def call(kernel, name, grid, in_specs, out_specs, out_shape, scratch, limit, micros, args, scalars=0, alias=None):
    return pl.pallas_call(
        kernel,
        grid_spec=pltpu.PrefetchScalarGridSpec(
            num_scalar_prefetch=scalars,
            grid=grid,
            in_specs=in_specs,
            out_specs=out_specs,
            scratch_shapes=scratch,
        ),
        out_shape=out_shape,
        input_output_aliases=alias or {},
        compiler_params=pltpu.CompilerParams(vmem_limit_bytes=limit * MIB),
        cost_estimate=pl.CostEstimate(flops=micros * PACE, bytes_accessed=1024, transcendentals=0),
        name=name,
    )(*args)


def prepare_kernel(
    tokens, cot, norms, fq_own, fq_oth, fk_own, fk_oth, normed, normed_t, held_cot, cot_t, maps
):
    step = pl.program_id(0)
    rows = at(step, CHUNK)
    xhat, unused = norm_parts(tokens[...].astype(F32))
    low = (xhat * norms[0:1, :] + norms[1:2, :]).astype(LOW)
    normed[rows, :] = low
    normed_t[...] = low.T
    held_cot[rows, :] = cot[...]
    cot_t[:, rows] = cot[...].T

    @pl.when(step == 0)
    def _():
        half, width, unused = fq_own.shape
        blank = jnp.zeros((width, width), F32)
        for kind, (own, oth) in enumerate(((fq_own, fq_oth), (fk_own, fk_oth))):
            for pair in range(half):
                source = own if pair < half // 2 else oth
                first = 2 * pair % half
                block = jnp.concatenate(
                    [
                        jnp.concatenate([source[first].astype(F32), blank], axis=1),
                        jnp.concatenate([blank, source[first + 1].astype(F32)], axis=1),
                    ],
                    axis=0,
                )
                maps[2 * kind, pair] = block.astype(LOW)
                maps[2 * kind + 1, pair] = block.T.astype(LOW)


def prepare(tokens, cot, norms, fq_own, fq_oth, fk_own, fk_oth):
    rows, dim = tokens.shape
    half, width, unused = fq_own.shape
    block = pl.BlockSpec((CHUNK, dim), lambda c: (c, 0))
    natural = kept_in_vmem((rows, dim), LOW)
    turned = kept_in_vmem((dim, rows), LOW)
    return call(
        prepare_kernel,
        "prepare",
        (rows // CHUNK,),
        [block, block] + [whole(a) for a in (norms, fq_own, fq_oth, fk_own, fk_oth)],
        [STAYS, pl.BlockSpec((dim, CHUNK), lambda c: (0, c))] + [STAYS] * 3,
        (natural, streamed((dim, rows), LOW), natural, turned, kept_in_vmem((4, half, 2 * width, 2 * width), LOW)),
        [],
        8,
        5,
        (*apart(tokens, cot), norms, fq_own, fq_oth, fk_own, fk_oth),
    )


def project_kernel(
    kept,
    normed,
    wa_own,
    wb_own,
    wa_oth,
    wb_oth,
    maps,
    aux,
    q_t,
    k_t,
    v_nat,
    v_ext,
    phi_q,
    phi_k,
    phi_k_nat,
    prefix,
    final,
    state,
):
    step = pl.program_id(0)
    heads, feat, unused = phi_q.shape
    width = feat // 2
    rows = at(step, CHUNK)
    normed_now = normed[rows, :]
    written = aux[1:2, rows].astype(LOW)
    tail = jnp.where(lax.broadcasted_iota(jnp.int32, (16, CHUNK), 0) == 0, 1.0, 0.0).astype(LOW)

    @pl.when(step == 0)
    def _():
        state[...] = jnp.zeros_like(state)

    prefix[0] = state[:heads]
    keep = kept[step]
    for side, (wa, wb) in enumerate(((wa_own, wb_own), (wa_oth, wb_oth))):
        made = jnp.concatenate([nn(normed_now, wa[...]), nn(normed_now, wb[...])], axis=1).astype(LOW)
        part = made.shape[1] // 3
        values = made[:, 2 * part :]
        v_nat[:, side * part : (side + 1) * part] = values
        for pair in range(part // feat):
            place = side * part + pair * feat
            index = place // feat
            lanes = slice(pair * feat, (pair + 1) * feat)
            q = made[:, :part][:, lanes].T
            k = made[:, part : 2 * part][:, lanes].T
            v = values[:, lanes].T
            state[heads, index : index + 1, :] += jnp.sum(
                values[:, lanes].astype(F32), axis=0, keepdims=True
            )
            q_t[place : place + feat, :] = q
            k_t[place : place + feat, :] = k
            q_logits = nn(maps[1, index], q)
            k_logits = nn(maps[3, index], k)
            for one in range(2):
                head = 2 * index + one
                inside = slice(one * width, (one + 1) * width)
                feat_q = softmax_pair(q_logits[inside])
                feat_k = softmax_pair(k_logits[inside])
                phi_q[head, :, rows] = feat_q
                phi_k[head] = feat_k
                phi_k_nat[rows, head * feat : (head + 1) * feat] = feat_k.T
                value = jnp.concatenate([v[inside], tail], axis=0)
                v_ext[head, :, rows] = value
                state[head] = keep * state[head] + nt(value, feat_k * written)
    final[...] = state[...]


def project(normed, wa_own, wb_own, wa_oth, wb_oth, maps, aux, kept, heads, width):
    rows, dim = normed.shape
    count = rows // CHUNK
    feat = 2 * width
    return call(
        project_kernel,
        "project",
        (count,),
        [STAYS] + [whole(a) for a in (wa_own, wb_own, wa_oth, wb_oth)] + [STAYS, whole(aux)],
        [
            pl.BlockSpec((heads * width, CHUNK), lambda c, *_: (0, c)),
            pl.BlockSpec((heads * width, CHUNK), lambda c, *_: (0, c)),
            pl.BlockSpec((CHUNK, heads * width), lambda c, *_: (c, 0)),
            STAYS,
            STAYS,
            pl.BlockSpec((heads, feat, CHUNK), lambda c, *_: (0, 0, c)),
            STAYS,
            pl.BlockSpec((1, heads, EXT, feat), lambda c, *_: (c, 0, 0, 0)),
            fixed(heads + 1, EXT, feat),
        ],
        (
            streamed((heads * width, rows), LOW),
            streamed((heads * width, rows), LOW),
            streamed((rows, heads * width), LOW),
            kept_in_vmem((heads, EXT, rows), LOW),
            kept_in_vmem((heads, feat, rows), LOW),
            streamed((heads, feat, rows), LOW),
            kept_in_vmem((rows, heads * feat), LOW),
            streamed((count, heads, EXT, feat), F32),
            streamed((heads + 1, EXT, feat), F32),
        ),
        [pltpu.VMEM((heads + 1, EXT, feat), F32)],
        16,
        14,
        (kept, *pinned(normed), wa_own, wb_own, wa_oth, wb_oth, *pinned(maps), aux),
        scalars=1,
    )


def center_of(final, entering, pair, rows):
    heads, unused, feat = final.shape
    other = (pair + (heads - 1) // 4) % ((heads - 1) // 2)
    total = final[heads - 1, pair : pair + 1, :] + entering[heads - 1, other : other + 1, :]
    return jnp.broadcast_to(total * (1.0 / rows), (feat, feat))


def attend_kernel(
    carry,
    aux,
    mask,
    phi_q,
    phi_k_nat,
    v_ext,
    prefix,
    final,
    entering,
    att_t,
    att_c,
    denom,
):
    step = pl.program_id(0)
    heads, feat, unused = phi_q.shape
    width = feat // 2
    rows = at(step, CHUNK)
    reach = aux[0:1, rows]
    padding = aux[3:4, rows]
    keep = carry[step]
    mask_now = mask[0]
    for head in range(heads):
        if head % 2 == 0:
            center = center_of(final, entering, head // 2, 2 * att_t.shape[1]).T
        pq = phi_q[head, :, rows]
        scores = nn(phi_k_nat[rows, head * feat : (head + 1) * feat], pq)
        weights = scores.astype(LOW) * mask_now
        state = (prefix[0, head] + keep * entering[(head + heads // 2) % heads]).astype(LOW)
        numer = nn(v_ext[head, :, rows], weights) + reach * nn(state, pq)
        below = numer[width : width + 1] + padding
        denom[head : head + 1, rows] = below
        place = slice(head * width, (head + 1) * width)
        att = numer[:width] * (1.0 / below)
        att_t[place, rows] = att.astype(LOW)
        near = center[head % 2 * width : (head % 2 + 1) * width, :]
        att_c[place, :] = (att - jnp.concatenate([near] * (CHUNK // feat), axis=1)).astype(LOW)


def attend(aux, mask, phi_q, phi_k_nat, v_ext, prefix, final, entering, carry):
    heads, feat, rows = phi_q.shape
    width = feat // 2
    turned = kept_in_vmem((heads * width, rows), LOW)
    return call(
        attend_kernel,
        "attend",
        (rows // CHUNK,),
        [whole(aux), pl.BlockSpec((1, CHUNK, CHUNK), lambda c, *_: (c, 0, 0))]
        + [STAYS] * 3
        + [pl.BlockSpec((1, heads, EXT, feat), lambda c, *_: (c, 0, 0, 0))]
        + [whole(final), whole(entering)],
        [STAYS, pl.BlockSpec((heads * width, CHUNK), lambda c, *_: (0, c)), STAYS],
        (turned, streamed((heads * width, rows), LOW), kept_in_vmem((16, rows), F32)),
        [],
        8,
        14,
        (carry, aux, *apart(mask), *pinned(phi_q, phi_k_nat, v_ext), *apart(prefix, final, entering)),
        scalars=1,
    )


def mix_kernel(spots, tokens, norms, w_own, w_oth, att_t, hidden, normed, normed_t):
    step = pl.program_id(0)
    rows = at(step, CHUNK)
    att = att_t[:, rows].T
    part = w_own.shape[-1]
    total = tokens[...].astype(F32)
    total = total + nt(att[:, :part], flat(w_own[...])) + nt(att[:, part:], flat(w_oth[...]))
    hidden[...] = total
    xhat, unused = norm_parts(total)
    low = (xhat * norms[2:3, :] + norms[3:4, :]).astype(LOW)
    normed[rows, :] = low
    normed_t[:, rows] = low.T


def gathered(array, width, index, side):
    return pl.BlockSpec(
        (array.shape[0], 1, array.shape[2], width),
        lambda c, spots: (0, spots[3] if side == 0 else 1 - spots[3], 0, index),
        pipeline_mode=pl.Buffered(1),
    )


def mix(spots, tokens, norms, early, units, att_t):
    rows, dim = tokens.shape
    part = att_t.shape[0] // 2
    weights = [gathered(early, part, 2 * units // part, side) for side in (0, 1)]
    block = pl.BlockSpec((CHUNK, dim), lambda c, *_: (c, 0))
    return call(
        mix_kernel,
        "mix",
        (rows // CHUNK,),
        [block, whole(norms)] + weights + [STAYS],
        [block, STAYS, STAYS],
        (
            streamed((rows, dim), F32),
            kept_in_vmem((rows, dim), LOW),
            kept_in_vmem((dim, rows), LOW),
        ),
        [],
        10,
        7,
        (spots, *apart(tokens), norms, *apart(early, early), *pinned(att_t)),
        scalars=1,
    )


def feed_kernel(first, sides, spots, normed, normed_t, cot, cot_t, *refs):
    feed, grad_normed = refs[-2 - sides : -sides]
    for side in range(sides):
        fc = flat(refs[2 * side][...])
        down = flat(refs[2 * side + 1][...])
        d_weights = refs[len(refs) - sides + side]
        units = fc.shape[1]
        u = nn(normed[...], fc)
        square = u * u
        t = jnp.tanh(u * (GELU_C + (GELU_C * GELU_A) * square))
        half = 0.5 + 0.5 * t
        act = (u * half).astype(LOW)
        slope = half + (0.5 * u) * (1.0 - t * t) * (GELU_C + (3.0 * GELU_C * GELU_A) * square)
        d_weights[:, units:] = nn(cot_t[...], act).astype(LOW)
        grad = (nn(cot[...], down) * slope).astype(LOW)
        d_weights[:, :units] = nn(normed_t[...], grad).astype(LOW)
        if first and side == 0:
            feed[...] = nt(act, down)
            grad_normed[...] = nt(grad, fc)
        else:
            feed[...] += nt(act, down)
            grad_normed[...] += nt(grad, fc)


def feed_forward(spots, normed, normed_t, cot, cot_t, weights, specs, units, sums):
    rows, dim = normed.shape
    sides = len(weights) // 2
    total = kept_in_vmem((rows, dim), F32)
    return call(
        functools.partial(feed_kernel, sums is None, sides),
        "feed",
        (1,),
        [STAYS] * 4 + specs + ([] if sums is None else [STAYS] * 2),
        [STAYS] * 2 + [fixed(dim, 2 * units)] * sides,
        (total, total) + (jax.ShapeDtypeStruct((dim, 2 * units), LOW),) * sides,
        [],
        24,
        9 * sides,
        (
            spots,
            *pinned(normed, normed_t, cot, cot_t),
            *weights,
            *(() if sums is None else pinned(*sums)),
        ),
        scalars=1,
        alias=None if sums is None else {5 + 2 * sides: 0, 6 + 2 * sides: 1},
    )


def middle_kernel(
    spots,
    hidden,
    feed,
    grad_normed,
    cot,
    norms,
    w_own,
    w_oth,
    att_t,
    att_c,
    denom,
    phi_q,
    aux,
    mixed,
    grad_hidden,
    d_gain,
    d_shift,
    g_ext,
    leaving,
    d_own,
    d_oth,
    branch_t,
    state,
):
    step = pl.program_id(0)
    count = pl.num_programs(0)
    heads, feat, unused = phi_q.shape
    width = feat // 2
    rows = at(step, CHUNK)
    hid = hidden[...]
    mixed[...] = (hid + feed[rows, :]).astype(LOW)
    xhat, rstd = norm_parts(hid)
    grad = grad_normed[rows, :]
    back = cot[rows, :].astype(F32) + norm_back(grad, xhat, rstd, norms[2:3, :])
    grad_hidden[...] = back

    @pl.when(step == 0)
    def _():
        d_gain[...] = jnp.zeros_like(d_gain)
        d_shift[...] = jnp.zeros_like(d_shift)
        state[...] = jnp.zeros_like(state)

    d_gain[...] += jnp.sum(grad * xhat, axis=0, keepdims=True)
    d_shift[...] += jnp.sum(grad, axis=0, keepdims=True)
    low = back.astype(LOW)
    branch_t[:, rows] = low.T
    reach = aux[2:3, rows].astype(LOW)
    first = lax.broadcasted_iota(jnp.int32, (16, CHUNK), 0) == 0
    pair = 0
    for weights in (w_own, w_oth):
        grad_att = nn(low, flat(weights[...]))
        for inner in range(weights.shape[-1] // feat):
            turned = grad_att[:, inner * feat : (inner + 1) * feat].T
            for one in range(2):
                head = 2 * pair + one
                ga = turned[one * width : (one + 1) * width]
                inverse = 1.0 / denom[head : head + 1, rows]
                centered = att_c[head * width : (head + 1) * width, :].astype(F32)
                gd = -jnp.sum(ga * centered, axis=0, keepdims=True) * inverse
                ext = jnp.concatenate(
                    [(ga * inverse).astype(LOW), jnp.where(first, gd, 0.0).astype(LOW)], axis=0
                )
                g_ext[head, :, rows] = ext
                state[head] += nt(ext * reach, phi_q[head, :, rows])
            pair += 1
    leaving[...] = state[...].astype(LOW)

    @pl.when(step == count - 1)
    def _():
        start = 0
        for out in (d_own, d_oth):
            size = out.shape[1]
            out[...] = nt(branch_t[...], att_t[start : start + size, :]).astype(LOW)
            start += size


def middle(spots, hidden, feed, grad_normed, cot, norms, early, units, att_t, att_c, denom, phi_q, aux):
    rows, dim = hidden.shape
    heads, feat, unused = phi_q.shape
    width = feat // 2
    part = heads * width // 2
    block = pl.BlockSpec((CHUNK, dim), lambda c, *_: (c, 0))
    weights = [gathered(early, part, 2 * units // part, side) for side in (0, 1)]
    return call(
        middle_kernel,
        "middle",
        (rows // CHUNK,),
        [block]
        + [STAYS] * 3
        + [whole(norms)]
        + weights
        + [STAYS, pl.BlockSpec((heads * width, CHUNK), lambda c, *_: (0, c)), STAYS, STAYS]
        + [whole(aux)],
        [block, block, fixed(1, dim), fixed(1, dim), STAYS, fixed(heads, EXT, feat)]
        + [fixed(dim, part)] * 2,
        (
            streamed((rows, dim), LOW),
            streamed((rows, dim), F32),
            streamed((1, dim), F32),
            streamed((1, dim), F32),
            kept_in_vmem((heads, EXT, rows), LOW),
            streamed((heads, EXT, feat), LOW),
        )
        + (jax.ShapeDtypeStruct((dim, part), LOW),) * 2,
        [pltpu.VMEM((dim, rows), LOW), pltpu.VMEM((heads, EXT, feat), F32)],
        20,
        13,
        (
            spots,
            *apart(hidden),
            *pinned(feed, grad_normed, cot),
            norms,
            *apart(early, early),
            *pinned(att_t),
            *apart(att_c),
            *pinned(denom, phi_q),
            aux,
        ),
        scalars=1,
    )


def attend_back_kernel(
    side,
    carry,
    kept,
    aux,
    mask,
    phi_q,
    phi_k,
    phi_k_nat,
    v_nat,
    v_ext,
    g_ext,
    prefix,
    final,
    entering,
    arriving,
    q_t,
    k_t,
    maps,
    grads,
    d_maps,
    state,
    d_fq,
    d_fk,
):
    step = pl.program_id(0)
    count = pl.num_programs(0)
    heads, feat, unused = phi_q.shape
    width = feat // 2
    part = heads * width // 2
    half = heads // 2
    chunk = count - 1 - step
    rows = at(chunk, CHUNK)
    keep_in = carry[chunk]
    keep = kept[chunk]
    reach = aux[0:1, rows].astype(LOW)
    written = aux[1:2, rows].astype(LOW)
    mask_now = mask[0]

    @pl.when(step == 0)
    def _():
        for head in range(half):
            state[head] = arriving[(1 - side) * half + head].astype(F32)
        d_fq[...] = jnp.zeros_like(d_fq)
        d_fk[...] = jnp.zeros_like(d_fk)

    for local in range(half // 2):
        pair = side * half // 2 + local
        logit_grads = ([], [])
        value_grads = []
        lanes = slice(local * feat, (local + 1) * feat)
        center = center_of(final, entering, pair, 2 * phi_q.shape[2])
        v_pair = (v_nat[:, lanes].astype(F32) - center[:1]).astype(LOW)
        center = center.T
        for one in range(2):
            head = 2 * pair + one
            kept_head = 2 * local + one
            pq = phi_q[head, :, rows]
            pk = phi_k[kept_head]
            scores = nn(phi_k_nat[rows, head * feat : (head + 1) * feat], pq)
            weights = scores.astype(LOW) * mask_now
            ext = g_ext[head, :, rows]
            numer = ext[:width]
            blank = jnp.zeros_like(numer)
            padded = jnp.concatenate([numer, blank] if one == 0 else [blank, numer], axis=0)
            gw = nn(v_pair, padded)
            gw = (gw + ext[width : width + 1].astype(F32)).astype(LOW) * mask_now
            middle_v = center[one * width : (one + 1) * width, :]
            before = prefix[0, kept_head] + keep_in * entering[(head + heads // 2) % heads]
            before = jnp.concatenate(
                [before[:width] - middle_v * before[width : width + 1], before[width:]], axis=0
            ).astype(LOW)
            value = v_ext[head, :, rows]
            value = jnp.concatenate(
                [
                    (
                        value[:width].astype(F32) - jnp.concatenate([middle_v] * (CHUNK // feat), axis=1)
                    ).astype(LOW),
                    value[width:],
                ],
                axis=0,
            )
            after = state[kept_head].astype(LOW)
            reached = ext * reach
            g_phi_q = nn(pk, gw) + tn(before, reached)
            g_phi_k = nt(pq, gw) + tn(after, value * written)
            g_value = nt(numer, weights) + nn(after[:width], pk * written)
            value_grads.append(g_value.astype(LOW))
            state[kept_head] = keep * state[kept_head] + nt(reached, pq)
            logit_grads[0].append(softmax_pair_back(pq, g_phi_q).astype(LOW))
            logit_grads[1].append(softmax_pair_back(pk, g_phi_k).astype(LOW))
        place = slice(local * feat, (local + 1) * feat)
        base = local * feat
        for index, (both, kind, source, d_fmap) in enumerate(
            ((logit_grads[0], 0, q_t, d_fq), (logit_grads[1], 2, k_t, d_fk))
        ):
            both = jnp.concatenate(both, axis=0)
            start = base + index * part
            grads[start : start + feat, rows] = nn(maps[kind, pair], both).astype(LOW)
            d_fmap[local] += nt(source[place, :], both)
        start = base + 2 * part
        grads[start : start + feat, rows] = jnp.concatenate(value_grads, axis=0)

    @pl.when(step == count - 1)
    def _():
        first = lax.broadcasted_iota(jnp.int32, (width, feat), 1) < width
        for kind, source in enumerate((d_fq, d_fk)):
            for local in range(half // 2):
                block = source[local]
                d_maps[kind, local] = jnp.where(first, block[:width], block[width:])


def attend_back(
    side, aux, mask, phi_q, phi_k, phi_k_nat, v_nat, v_ext, g_ext, prefix, final, entering, arriving, q_t, k_t, maps, carry, kept
):
    heads, feat, rows = phi_q.shape
    width = feat // 2
    half = heads // 2
    count = rows // CHUNK
    lanes = pl.BlockSpec((half * width, CHUNK), lambda c, *_: (side, count - 1 - c))
    return call(
        functools.partial(attend_back_kernel, side),
        "attend_back",
        (rows // CHUNK,),
        [
            whole(aux),
            pl.BlockSpec((1, CHUNK, CHUNK), lambda c, *_: (count - 1 - c, 0, 0)),
            STAYS,
            pl.BlockSpec((half, feat, CHUNK), lambda c, *_: (side, 0, count - 1 - c)),
            STAYS,
            pl.BlockSpec((CHUNK, half * width), lambda c, *_: (count - 1 - c, side)),
            STAYS,
            STAYS,
            pl.BlockSpec((1, half, EXT, feat), lambda c, *_: (count - 1 - c, side, 0, 0)),
            whole(final),
            whole(entering),
            whole(arriving),
            lanes,
            lanes,
            STAYS,
        ],
        [STAYS, fixed(2, half // 2, width, feat)],
        (kept_in_vmem((3 * half * width, rows), LOW), streamed((2, half // 2, width, feat), F32)),
        [pltpu.VMEM((half, EXT, feat), F32)] + [pltpu.VMEM((half // 2, feat, feat), F32)] * 2,
        10,
        14,
        (
            carry,
            kept,
            aux,
            *apart(mask),
            *pinned(phi_q),
            *apart(phi_k),
            *pinned(phi_k_nat),
            *apart(v_nat),
            *pinned(v_ext, g_ext),
            *apart(prefix, final, entering, arriving, q_t, k_t),
            *pinned(maps),
        ),
        scalars=2,
    )


def weight_kernel(normed_t, grads, out):
    out[...] = nt(normed_t[...], grads[...]).astype(LOW)


def weight_grads(normed_t, grads):
    dim, rows = normed_t.shape
    size = grads.shape[0]
    return call(
        weight_kernel,
        "weight_grads",
        (1,),
        [whole(normed_t), STAYS],
        fixed(dim, size),
        jax.ShapeDtypeStruct((dim, size), LOW),
        [],
        8,
        4,
        (*apart(normed_t), *pinned(grads)),
    )


def first_kernel(tokens, norms, grad_hidden, wa_own, wb_own, wa_oth, wb_oth, grads_own, grads_oth, out, d_gain, d_shift):
    step = pl.program_id(0)
    rows = at(step, CHUNK)
    total = None
    for wa, wb, grads in ((wa_own, wb_own, grads_own), (wa_oth, wb_oth, grads_oth)):
        cut = wa.shape[1]
        term = nn(wa[...], grads[:cut, rows]) + nn(wb[...], grads[cut:, rows])
        total = term if total is None else total + term
    grad = total.T
    xhat, rstd = norm_parts(tokens[...].astype(F32))
    out[...] = (grad_hidden[...] + norm_back(grad, xhat, rstd, norms[0:1, :])).astype(LOW)

    @pl.when(step == 0)
    def _():
        d_gain[...] = jnp.zeros_like(d_gain)
        d_shift[...] = jnp.zeros_like(d_shift)

    d_gain[...] += jnp.sum(grad * xhat, axis=0, keepdims=True)
    d_shift[...] += jnp.sum(grad, axis=0, keepdims=True)


def first_back(tokens, norms, grad_hidden, weights, grads):
    rows, dim = tokens.shape
    block = pl.BlockSpec((CHUNK, dim), lambda c: (c, 0))
    return call(
        first_kernel,
        "first_back",
        (rows // CHUNK,),
        [block, whole(norms), block] + [whole(w) for w in weights] + [STAYS] * 2,
        [block, fixed(1, dim), fixed(1, dim)],
        (
            streamed((rows, dim), LOW),
            streamed((1, dim), F32),
            streamed((1, dim), F32),
        ),
        [],
        16,
        9,
        (*apart(tokens), norms, *apart(grad_hidden), *weights, *pinned(*grads)),
    )


SWAP = [(0, 1), (1, 0)]


def swap(piece):
    return lax.ppermute(piece, "mp", SWAP)


def flip(piece, bit, size):
    return lax.ppermute(piece, "dp", [(i, i ^ bit) for i in range(size)])


def turn(piece, by, size):
    return lax.ppermute(piece, "dp", [(i, (i + by) % size) for i in range(size)])


def after(value, *others):
    return lax.optimization_barrier((value, *others))[0]


class Places:
    def __init__(self, size):
        self.size = size
        self.deep = size // 4
        place = lax.axis_index("dp")
        self.spots = jnp.stack([place % 2, (place // 2) % 2, place // 4, lax.axis_index("mp")])

    def flip(self, value, axis):
        return flip(value, 1 if axis == "x" else 2, self.size)


def line_kernel(cut, spots, *refs):
    deep = len(refs) - 2
    for s in range(deep):
        spot = lax.rem(spots[2] + deep - s, deep)
        refs[-2][spot] = refs[s][:, :cut]
        refs[-1][spot] = refs[s][:, cut:]


def gather_line(shard, cut, at, *others):
    pieces = [shard] + [turn(shard, 4 * s, at.size) for s in range(1, at.deep)]
    if others:
        pieces[1] = after(pieces[1], *others)
    rows, columns = shard.shape
    shapes = [(at.deep, rows, cut), (at.deep, rows, columns - cut)]
    return call(
        functools.partial(line_kernel, cut),
        "line",
        (1,),
        [whole(p) for p in pieces],
        [fixed(*shape) for shape in shapes],
        tuple(jax.ShapeDtypeStruct(shape, LOW) for shape in shapes),
        [],
        6,
        0,
        (at.spots, *pieces),
        scalars=1,
    )


def pair_kernel(axes, dims, spots, *refs):
    for index, (axis, dim) in enumerate(zip(axes, dims)):
        mine, theirs, out = refs[2 * index], refs[2 * index + 1], refs[4 + index]
        bit = spots[0 if axis == "x" else 1]
        for source, place in ((mine, bit), (theirs, 1 - bit)):
            if dim == 1:
                out[:, pl.ds(place, 1)] = source[...][:, None]
            else:
                out[:, :, pl.ds(place, 1)] = source[...][:, :, None]


def first_by(shape):
    tail = (0,) * (len(shape) - 1)
    return pl.BlockSpec((1, *shape[1:]), lambda d, *_: (d, *tail))


def gather_pair(values, axes, at, *others, kind=jax.ShapeDtypeStruct):
    moved = [at.flip(v, axis) for v, axis in zip(values, axes)]
    if others:
        moved[0] = after(moved[0], *others)
    dims = [v.ndim - 2 if axis == "x" else 1 for v, axis in zip(values, axes)]
    shapes = [(*v.shape[:d], 2, *v.shape[d:]) for v, d in zip(values, dims)]
    return call(
        functools.partial(pair_kernel, axes, dims),
        "pair",
        (at.deep,),
        [first_by(v.shape) for v in values for unused in (0, 1)],
        [first_by(shape) for shape in shapes],
        tuple(kind(shape, LOW) for shape in shapes),
        [],
        8,
        0,
        (at.spots, values[0], moved[0], values[1], moved[1]),
        scalars=1,
    )


def first_fold_kernel(axes, cuts, spots, *refs):
    outs = refs[-4:]
    for index, axis in enumerate(axes):
        bit = spots[0 if axis == "x" else 1]
        sent, kept = outs[2 * index : 2 * index + 2]
        start = 0
        for segment, cut in enumerate(cuts):
            pair = refs[2 * segment : 2 * segment + 2]
            columns = slice(0, cut) if index == 0 else slice(cut, pair[0].shape[-1])
            size = columns.stop - columns.start
            for out, place in ((sent, 1 - bit), (kept, bit)):
                if axis == "x":
                    terms = [r[:, :, pl.ds(place, 1), :, columns].astype(F32) for r in pair]
                else:
                    terms = [r[:, pl.ds(place, 1), :, :, columns].astype(F32) for r in pair]
                total = (terms[0] + terms[1]).astype(LOW)
                out[..., start : start + size] = total.reshape(*out.shape[:-1], size)
            start += size


def fold_kernel(axes, spots, *refs):
    for index, axis in enumerate(axes):
        bit = spots[0 if axis == "x" else 1]
        sent, kept = refs[4 + 2 * index : 6 + 2 * index]
        for out, place in ((sent, 1 - bit), (kept, bit)):
            terms = [r[:, pl.ds(place, 1)].astype(F32) for r in refs[2 * index : 2 * index + 2]]
            out[...] = (terms[0] + terms[1]).astype(LOW).reshape(out.shape)


def spread_kernel(spots, a_kept, a_sent, b_kept, b_sent, *outs):
    deep = len(outs)
    cut = a_kept.shape[-1]
    for s, out in enumerate(outs):
        spot = lax.rem(spots[2] + s, deep)
        out[:, :cut] = (a_kept[spot].astype(F32) + a_sent[spot].astype(F32)).astype(LOW)
        out[:, cut:] = (b_kept[spot].astype(F32) + b_sent[spot].astype(F32)).astype(LOW)


class Scatter:
    def __init__(self, segments, at):
        self.at = at
        self.cuts = [cut for own, oth, cut in segments]
        self.cut = sum(self.cuts)
        self.terms = [[own, swap(oth)] for own, oth, cut in segments]
        if at.size % 4 == 0:
            split = lambda v: v.reshape(at.deep, 2, 2, v.shape[0] // at.size, v.shape[1])
            self.terms = [[split(v) for v in pair] for pair in self.terms]

    def wait_for(self, *others):
        self.terms[0][1] = after(self.terms[0][1], *others)

    def fold(self, axes):
        at = self.at
        flats = [v for pair in self.terms for v in pair]
        if at.size % 4:
            return flats[0]
        if self.cuts:
            columns = sum(pair[0].shape[-1] for pair in self.terms)
            head = flats[0].shape[:2]
            rows = flats[0].shape[3]
            lefts = [(*head, rows, self.cut), (*head, rows, columns - self.cut)]
            kernel = functools.partial(first_fold_kernel, axes, tuple(self.cuts))
        else:
            lefts = [(v.shape[0], *v.shape[2:]) for v in flats[::2]]
            kernel = functools.partial(fold_kernel, axes)
        outs = [left for left in lefts for unused in (0, 1)]
        a_sent, a_kept, b_sent, b_kept = call(
            kernel,
            "fold",
            (at.deep,),
            [first_by(v.shape) for v in flats],
            [first_by(left) for left in outs],
            tuple(jax.ShapeDtypeStruct(left, LOW) for left in outs),
            [],
            12,
            0,
            (at.spots, *flats),
            scalars=1,
        )
        self.cuts = []
        self.terms = [[a_kept, at.flip(a_sent, axes[0])], [b_kept, at.flip(b_sent, axes[1])]]
        return a_kept

    def spread(self):
        at = self.at
        if at.size % 4:
            return self.terms[0][0]
        a, b = self.terms
        shape = (a[0].shape[1], self.cut + b[0].shape[-1])
        own, *sends = call(
            spread_kernel,
            "spread",
            (1,),
            [whole(v) for v in (*a, *b)],
            [fixed(*shape)] * at.deep,
            (jax.ShapeDtypeStruct(shape, LOW),) * at.deep,
            [],
            8,
            0,
            (at.spots, *a, *b),
            scalars=1,
        )
        self.parts = [own] + [turn(p, 4 * s, at.size) for s, p in enumerate(sends, 1)]
        return own

    def end(self, *others):
        if self.at.size % 4:
            sums = [own.astype(F32) + moved.astype(F32) for own, moved in self.terms]
            total = [t[:, :cut] for t, cut in zip(sums, self.cuts)] + [t[:, cut:] for t, cut in zip(sums, self.cuts)]
            total = lax.psum_scatter(jnp.concatenate(total, axis=1), "dp", scatter_dimension=0, tiled=True)
        else:
            if others:
                self.parts[1] = after(self.parts[1], *others)
            total = sum(p.astype(F32) for p in self.parts)
        return total


def add_along(value, steps, size):
    for step in steps:
        if step < size:
            value = value.astype(LOW)
            value = value.astype(F32) + flip(value, step, size).astype(F32)
    return value


def per_device(
    size,
    tokens,
    norm1_gain,
    norm1_shift,
    w_query,
    w_key,
    w_value,
    w_out,
    fmap_query,
    fmap_key,
    norm2_gain,
    norm2_shift,
    w_fc,
    w_down,
    lengths,
    cotangent,
):
    rows, dim = tokens.shape
    heads = 2 * fmap_query.shape[0]
    width = fmap_query.shape[1]
    feat = 2 * width
    part = w_query.shape[1]
    count = rows // CHUNK
    core = lax.axis_index("mp")

    ends = jnp.cumsum(lengths[0])
    places = core * rows - 1 + jnp.arange(rows + 1, dtype=jnp.int32)
    numbers = jnp.sum((ends[None, :] <= places[:, None]).astype(jnp.int32), axis=1)
    numbers = jnp.where(places < 0, -1, numbers)
    segment = numbers[1:]
    living = places[1:] < ends[-1]
    blocks = segment.reshape(count, CHUNK)
    last = blocks[:, -1]
    before = jnp.concatenate([numbers[:1], last[:-1]])
    kept = (last == before).astype(F32)
    carry = ((before == numbers[0]) & (core > 0)).astype(F32)
    reach = (blocks == before[:, None]).reshape(rows) & living
    written = (blocks == last[:, None]).reshape(rows)
    reach_in = (segment == numbers[0]) & living
    aux = jnp.stack([reach, written, reach_in, ~living] + [jnp.zeros_like(living)] * 4).astype(F32)
    order = jnp.arange(CHUNK, dtype=jnp.int32)
    mask = (
        (blocks[:, :, None] == blocks[:, None, :])
        & (order[:, None] <= order[None, :])
        & living.reshape(count, 1, CHUNK)
    ).astype(LOW)

    norms = jnp.stack([norm1_gain, norm1_shift, norm2_gain, norm2_shift])

    where = Places(size)
    staged = size % 4 == 0
    units = w_fc.shape[1] // 2
    cut = (3 * part // feat + 1) // 2 * feat
    cut_out = (part // feat + 1) // 2 * feat
    shard_qkv = jnp.concatenate([w_query, w_key, w_value], axis=1)
    shard_early = jnp.concatenate([w_fc[:, :units], w_down[:, :units], w_out], axis=1)
    shard_late = jnp.concatenate([w_fc[:, units:], w_down[:, units:]], axis=1)
    early = lax.all_gather(shard_early, ("dp", "mp"), axis=0)
    early = early.reshape(size, 2, *shard_early.shape)
    if shard_early.shape[0] % 16:
        early = early.swapaxes(0, 1).reshape(1, 2, dim, -1)
    fq_oth, fk_oth = swap(fmap_query), swap(fmap_key)
    ready = lax.optimization_barrier((shard_late, norms, aux, mask, kept, carry, where.spots))
    shard_late, norms, aux, mask, kept, carry, spots = ready
    where.spots = spots
    if staged:
        qkv = gather_line(shard_qkv, cut, where)
        qkv = gather_pair(qkv, "xy", where)
        shard_late, tokens = after(shard_late, qkv[0]), after(tokens, qkv[0])
    normed1, normed1_t, cot, cot_t, maps = prepare(
        tokens, cotangent, norms, fmap_query, fq_oth, fmap_key, fk_oth
    )
    if staged:
        qkv = tuple(map(flat, gather_pair(qkv, "yx", where, maps)))
    else:
        qkv, late = (
            tuple(lax.all_gather(s, "dp", axis=0, tiled=True) for s in shards)
            for shards in (
                (shard_qkv[:, :cut], shard_qkv[:, cut:]),
                (shard_late[:, :units], shard_late[:, units:]),
            )
        )
    qkv = (*qkv, *map(swap, qkv))
    q_t, k_t, v_nat, v_ext, phi_q, phi_k, phi_k_nat, prefix, final = project(
        normed1, *qkv, maps, aux, kept, heads, width
    )
    if staged:
        late = gather_line(shard_late, units, where, final)
        final = after(final, late[0])
    entering = swap(final)
    att_t, att_c, denom = attend(aux, mask, phi_q, phi_k_nat, v_ext, prefix, final, entering, carry)
    if staged:
        late = gather_pair(late, "xy", where, denom)
        att_t = after(att_t, late[0])
    hidden, normed2, normed2_t = mix(spots, tokens, norms, early, units, att_t)
    feed_part = functools.partial(feed_forward, spots, normed2, normed2_t, cot, cot_t)
    early_specs = [[gathered(early, units, index, side) for index in (0, 1)] for side in (0, 1)]
    feed, grad_normed, *d_early_oth = feed_part(apart(early, early), early_specs[1], units, None)
    if staged:
        late = tuple(map(flat, gather_pair(late, "yx", where, d_early_oth[0], kind=streamed)))
        feed = after(feed, late[0])
    feed, grad_normed, *d_early_own = feed_part(
        apart(early, early), early_specs[0], units, (feed, grad_normed)
    )
    sums_early = Scatter([(*d_early_own, *d_early_oth, units)], where)
    late_oth = tuple(map(swap, late))
    feed = after(feed, sums_early.fold("xy"))
    feed, grad_normed, d_late_own, d_late_oth = feed_part(
        (*late, *late_oth), [whole(w) for w in late] * 2, units, (feed, grad_normed)
    )
    sums_early.wait_for(d_late_oth)
    hidden = after(hidden, sums_early.fold("yx"))
    mixed, grad_hidden, d_gain2, d_shift2, g_ext, leaving, d_out_own, d_out_oth = middle(
        spots, hidden, feed, grad_normed, cot, norms, early, units, att_t, att_c, denom, phi_q, aux
    )
    sums_early.wait_for(d_gain2)
    leaving = after(leaving, sums_early.spread())
    arriving = lax.ppermute(leaving, "mp", [(1, 0)])
    sums_late = Scatter([(d_late_own, d_late_oth, units), (d_out_own, d_out_oth, cut_out)], where)
    back = functools.partial(
        attend_back, carry=carry, kept=kept, prefix=prefix, final=final, entering=entering, q_t=q_t, k_t=k_t, maps=maps
    )
    back_inputs = (aux, mask, phi_q, phi_k, phi_k_nat, v_nat, v_ext, g_ext)
    lanes = lambda v: v.reshape(-1, feat)
    grads_oth, maps_oth = back(1, *back_inputs, arriving=arriving)
    sums_late.wait_for(maps_oth)
    grads_oth = after(grads_oth, sums_late.fold("xy"))
    total_early = sums_early.end(maps_oth)
    maps_oth = swap(maps_oth)
    d_qkv_oth = weight_grads(normed1_t, grads_oth)
    arriving = after(arriving, d_qkv_oth, total_early)
    grads_own, maps_own = back(0, *back_inputs, arriving=arriving)
    sums_late.wait_for(maps_own)
    grads_own = after(grads_own, sums_late.fold("yx"))
    map_grads = add_along(lanes(maps_own + maps_oth), [1], size)
    d_qkv_own = weight_grads(normed1_t, grads_own)
    sums_qkv = Scatter([(d_qkv_own, d_qkv_oth, cut)], where)
    grad_hidden = after(grad_hidden, sums_qkv.fold("xy"))
    sums_late.wait_for(d_qkv_own)
    grad_hidden = after(grad_hidden, sums_late.spread())
    map_grads = add_along(after(map_grads, d_qkv_own), [2], size)
    grad_tokens, d_gain1, d_shift1 = first_back(tokens, norms, grad_hidden, qkv, (grads_own, grads_oth))
    sums_qkv.wait_for(d_gain1)
    norm_grads = jnp.concatenate([d_gain1, d_shift1, d_gain2, d_shift2], axis=0)
    norm_grads = lanes(after(norm_grads, sums_qkv.fold("yx")))
    norm_grads = add_along(norm_grads + swap(norm_grads), [1, 2], size)
    small = jnp.concatenate([map_grads, norm_grads], axis=0)
    small = add_along(after(small, sums_qkv.spread()), [4 << i for i in range(size.bit_length() - 3)], size)
    map_grads = small[: map_grads.shape[0]].reshape(2, heads // 4, width, 2, width)
    map_grads = map_grads.swapaxes(2, 3).reshape(2, heads // 2, width, width)
    norm_grads = small[-norm_grads.shape[0] :].reshape(4, dim)
    total_late = sums_late.end()
    grad_qkv = sums_qkv.end()
    cut_late = units + cut_out
    return (
        mixed,
        grad_tokens,
        norm_grads[0],
        norm_grads[1],
        grad_qkv[:, :part],
        grad_qkv[:, part : 2 * part],
        grad_qkv[:, 2 * part :],
        jnp.concatenate([total_late[:, units:cut_late], total_late[:, cut_late + units :]], axis=1),
        map_grads[0],
        map_grads[1],
        norm_grads[2],
        norm_grads[3],
        jnp.concatenate([total_early[:, :units], total_late[:, :units]], axis=1),
        jnp.concatenate([total_early[:, units:], total_late[:, cut_late : cut_late + units]], axis=1),
    )


def solution(mesh):
    placed = (
        P(("dp", "mp"), None),
        P(),
        P(),
        P("dp", "mp"),
        P("dp", "mp"),
        P("dp", "mp"),
        P("dp", "mp"),
        P("mp", None, None),
        P("mp", None, None),
        P(),
        P(),
        P("dp", "mp"),
        P("dp", "mp"),
        P("dp", None),
        P(("dp", "mp"), None),
    )
    return jax.shard_map(
        functools.partial(per_device, mesh.shape["dp"]),
        mesh=mesh,
        in_specs=placed,
        out_specs=(
            P(("dp", "mp"), None),
            P(("dp", "mp"), None),
            P(),
            P(),
            P("dp", "mp"),
            P("dp", "mp"),
            P("dp", "mp"),
            P("dp", "mp"),
            P("mp", None, None),
            P("mp", None, None),
            P(),
            P(),
            P("dp", "mp"),
            P("dp", "mp"),
        ),
        check_vma=False,
    )
```

time: 2180 us -> 306 us (0.14)
  waiting for transfers between devices: 983 us -> 52.4 us
  matrix products: 439 us -> 0 us
  local copies, waits for them, and re-layouts: 416 us -> 15.7 us
  blocking collectives: 215 us -> 0 us
  Pallas kernels: 0 us -> 149 us
  other arithmetic: 86.4 us -> 9.89 us
  starting transfers between devices: 0.73 us -> 60.7 us
    reduce_scatter x9 -> x0, waiting for transfers between devices: 673 us -> none  [the longest x1 143 us: per_device(): lax.psum_scatter(grad_fc, 'dp', scatter_dimension=0, tiled=True)]
    dot_general x94 -> x0, matrix products: 423 us -> none  [the longest x16 126 us: block_core(): scores = jnp.einsum('thf,shf->hts', phi_q, phi_k, precision=HIGH)]
    dynamic_update_slice x16 -> x0, local copies, waits for them, and re-layouts: 265 us -> none  [attend(): lax.scan(jax.checkpoint(block_core), initial, (phi_q, phi_k, blocked, seg...]
    all_gather x4 -> x0, blocking collectives: 175 us -> none  [the longest x1 48.5 us: per_device(): lax.all_gather(w_query, 'dp', axis=0, tiled=True)]
    pallas_call x0 -> x28, Pallas kernels: none -> 149 us  [call(): pl.pallas_call(kernel, grid_spec=pltpu.PrefetchScalarGridSpec(num_scalar_...]
    all_gather x6 -> x1, waiting for transfers between devices: 145 us -> 5.5 us  [per_device(): early = lax.all_gather(shard_early, ('dp', 'mp'), axis=0)]
    psum x1 -> x0, waiting for transfers between devices: 112 us -> none  [per_device(): lax.psum((grad_fmap_query, grad_fmap_key), 'dp')]
    ppermute x0 -> x55, starting transfers between devices: none -> 60.7 us  [the longest x26 32 us: flip(): return lax.ppermute(piece, 'dp', [(i, i ^ bit) for i in range(size)])]
  transfers between devices with their start and end apart: 17 -> 56, of which waited for: 14 -> 18; matrix products, arithmetic and copies ran while one was open for 4% -> 6% of each run, Pallas kernels for 0% -> 48%
where the time goes in v2:
time: 306 us; the launch traced here: 303 us
  Pallas kernels  149 us (49%)
  starting transfers between devices  60.7 us (20%)
  waiting for transfers between devices  52.4 us (17%)
  local copies, waits for them, and re-layouts  15.7 us (5%)
  between operations  15.2 us (5%)
  other arithmetic  9.89 us (3%)
    pallas_call x28, Pallas kernels, call(): pl.pallas_call(kernel, grid_spec=pltpu.PrefetchScalarGridSpec(num_scalar_...  149 us
    ppermute x26, starting transfers between devices, flip(): return lax.ppermute(piece, 'dp', [(i, i ^ bit) for i in range(size)])  32 us
    ppermute x26, waiting for transfers between devices, flip(): return lax.ppermute(piece, 'dp', [(i, i ^ bit) for i in range(size)])  31 us
    ppermute x15, starting transfers between devices, turn(): lax.ppermute(piece, 'dp', [(i, (i + by) % size) for i in range(size)])  23.9 us
    ppermute x15, waiting for transfers between devices, turn(): lax.ppermute(piece, 'dp', [(i, (i + by) % size) for i in range(size)])  14 us
    unnamed x78, local copies, waits for them, and re-layouts  6.45 us
  transfers between devices with their start and end apart: 56, of which 18 were waited for; matrix products, arithmetic and copies ran while one was open for 6% of the time, Pallas kernels for 48%

profile of v2, /device:TPU:0, one launch (start us, length us, event | category | flops | bytes accessed | tf_op | source)
XLA Modules:
  0.0 302.6 jit_solution(9295058844687015138)
XLA Ops:
  9.6 5.0 %collective-permute-start.2 = (bf16[48,1152]{1,0:T(8,128)(2,1)S(1)}, bf16[48,1152]{1,0:T(8,128)(2,1)S(1)}, u32[]{:S(2)}, u32[]{:S(2)}) collective-permute-start(bf16[48,1152]{1,0:T(8,128)(2,1)S(1)} %constant_dynamic-update-slice_fusion.refs_0_), channel_id=1, source_target_pairs={{0,24},{2,26},{4,28},{6,30},{8,0},{10,2},{12,4},{14,6},{16,8},{18,... | collective-permute-start | bytes 331784 | tf_op jit(solution)/shard_map/ppermute | solution.py:804
  32.0 3.6 %collective-permute-done.4.refs_3_ = bf16[4,48,512]{2,1,0:T(8,128)(2,1)S(1)} collective-permute-done((bf16[4,48,512]{2,1,0:T(8,128)(2,1)S(1)}, bf16[4,48,512]{2,1,0:T(8,128)(2,1)S(1)}, u32[]{:S(2)}, u32[]{:S(2)}) %collective-permute-start.4) | collective-permute-done | bytes 196640 | tf_op jit(solution)/shard_map/ppermute | solution.py:800
  39.4 5.2 %prepare.1 = (bf16[1024,768]{1,0:T(8,128)(2,1)S(1)}, bf16[768,1024]{1,0:T(8,128)(2,1)}, bf16[1024,768]{1,0:T(8,128)(2,1)S(1)}, bf16[768,1024]{1,0:T(8,128)(2,1)S(1)}, bf16[4,6,128,128]{3,2,1,0:T(8,128)(2,1)S(1)}) custom-call(bf16[1024,768]{1,0:T(8,128)(2,1)} %tokens.2, bf16[1024,768]{1,0:T(8,128)(2,1)} %cot.1, f32[4,768]{1,0:T(4,128)S(1)} %pad_maximum_fusion.6.norms, ...), custom_call_target="tpu_custom_call" | custom-call | flops 15000000512 | bytes 1024 | tf_op jit(solution)/shard_map/prepare/pallas_call | solution.py:106
  45.9 6.5 %collective-permute-done.7.refs_1_ = bf16[4,2,48,640]{3,2,1,0:T(8,128)(2,1)S(1)} collective-permute-done((bf16[4,2,48,640]{3,2,1,0:T(8,128)(2,1)S(1)}, bf16[4,2,48,640]{3,2,1,0:T(8,128)(2,1)S(1)}, u32[]{:S(2)}, u32[]{:S(2)}) %collective-permute-start.7) | collective-permute-done | bytes 491552 | tf_op jit(solution)/shard_map/ppermute | solution.py:800
  54.0 3.5 %collective-permute-start.13 = (bf16[48,1536]{1,0:T(8,128)(2,1)S(1)}, bf16[48,1536]{1,0:T(8,128)(2,1)S(1)}, u32[]{:S(2)}, u32[]{:S(2)}) collective-permute-start(bf16[48,1536]{1,0:T(8,128)(2,1)S(1)} %pad_maximum_fusion.4.refs_0_), channel_id=1, source_target_pairs={{0,24},{2,26},{4,28},{6,30},{8,0},{10,2},{12,4},{14,6},{16,8},{18,... | collective-permute-start | bytes 442376 | tf_op jit(solution)/shard_map/ppermute | solution.py:804
  58.9 14.2 %project.1 = (bf16[768,1024]{1,0:T(8,128)(2,1)}, bf16[768,1024]{1,0:T(8,128)(2,1)}, bf16[1024,768]{1,0:T(8,128)(2,1)}, bf16[12,80,1024]{2,1,0:T(8,128)(2,1)S(1)}...) custom-call(f32[4]{0:T(128)S(1)} %compare_convert_fusion.kept, ...), custom_call_target="tpu_custom_call" | custom-call | flops 41999998976 | bytes 1024 | tf_op jit(solution)/shard_map/project/pallas_call | solution.py:106
  76.9 13.6 %attend.1 = (bf16[768,1024]{1,0:T(8,128)(2,1)S(1)}, bf16[768,1024]{1,0:T(8,128)(2,1)}, f32[16,1024]{1,0:T(8,128)S(1)}) custom-call(f32[4]{0:T(128)S(1)} %get-tuple-element.147.carry, f32[8,1024]{1,0:T(8,128)S(1)} %convert_element_type.109.aux, bf16[4,256,256]{2,1,0:T(8,128)(2,1)} %and_convert_fusion.mask, ...), custom_call_target="tpu_custom_call" | custom-call | flops 41999998976 | bytes 1024 | tf_op jit(solution)/shard_map/attend/pallas_call | solution.py:106
  94.5 5.5 %all-gather.3.cloned.1.call-done = bf16[1536,1920]{1,0:T(8,128)(2,1)} async-done(((bf16[48,1920]{1,0:T(8,128)(2,1)}), bf16[1536,1920]{1,0:T(8,128)(2,1)}) %all-gather.3.cloned.1.call-update) | async-done | bytes 5898256 | tf_op jit(solution)/shard_map/all_gather | solution.py:1071
  101.4 6.8 %mix.1 = (f32[1024,768]{1,0:T(8,128)}, bf16[1024,768]{1,0:T(8,128)(2,1)S(1)}, bf16[768,1024]{1,0:T(8,128)(2,1)S(1)}) custom-call(s32[4]{0:T(128)S(1)} %pad_add_fusion.1.spots, bf16[1024,768]{1,0:T(8,128)(2,1)} %tokens.2, f32[4,768]{1,0:T(4,128)S(1)} %pad_maximum_fusion.6.norms, bf16[16,2,48,1920]{3,2,1,0:T(8,128)(2,1)} %bitcast.66, ...), custom_call_target="tpu_custom_call" | custom-call | flops 20999999488 | bytes 1024 | tf_op jit(solution)/shard_map/mix/pallas_call | solution.py:106
  108.2 10.1 %feed.3 = (f32[1024,768]{1,0:T(8,128)S(1)}, f32[1024,768]{1,0:T(8,128)S(1)}, bf16[768,1536]{1,0:T(8,128)(2,1)S(1)}) custom-call(s32[4]{0:T(128)S(1)} %pad_add_fusion.1.spots, bf16[1024,768]{1,0:T(8,128)(2,1)S(1)} %get-tuple-element.174.normed, bf16[768,1024]{1,0:T(8,128)(2,1)S(1)} %get-tuple-element.175.normed_t, bf16[1024,768]{1,0:T(8,128)(2,1)S(1)} %copy-done.17, ...), custom_call_target="tpu_custom_call" | custom-call | flops 27000000512 | bytes 1024 | tf_op jit(solution)/shard_map/feed/pallas_call | solution.py:106
  118.6 3.1 %pair.7 = (bf16[4,2,2,48,768]{4,3,2,1,0:T(8,128)(2,1)}, bf16[4,2,2,48,768]{4,3,2,1,0:T(8,128)(2,1)}) custom-call(s32[4]{0:T(128)S(1)} %pad_add_fusion.1.spots, bf16[4,2,48,768]{3,2,1,0:T(8,128)(2,1)S(1)} %get-tuple-element.171.refs_0_, bf16[4,2,48,768]{3,2,1,0:T(8,128)(2,1)S(1)} %collective-permute-done.17.refs_1_, ...), custom_call_target="tpu_custom_call" | custom-call | bytes 1024 | tf_op jit(solution)/shard_map/pair/pallas_call | solution.py:106
  122.3 10.1 %feed.4 = (f32[1024,768]{1,0:T(8,128)S(1)}, f32[1024,768]{1,0:T(8,128)S(1)}, bf16[768,1536]{1,0:T(8,128)(2,1)S(1)}) custom-call(s32[4]{0:T(128)S(1)} %pad_add_fusion.1.spots, bf16[1024,768]{1,0:T(8,128)(2,1)S(1)} %get-tuple-element.174.normed, bf16[768,1024]{1,0:T(8,128)(2,1)S(1)} %get-tuple-element.175.normed_t, ...), custom_call_target="tpu_custom_call", output_to_operand_aliasing={{0}: (7, {}), {1}: (8, {})} | custom-call | flops 27000000512 | bytes 1024 | tf_op jit(solution)/shard_map/feed/pallas_call | solution.py:106
  135.8 16.4 %feed.5 = (f32[1024,768]{1,0:T(8,128)S(1)}, f32[1024,768]{1,0:T(8,128)S(1)}, bf16[768,1536]{1,0:T(8,128)(2,1)S(1)}, bf16[768,1536]{1,0:T(8,128)(2,1)S(1)}) custom-call(s32[4]{0:T(128)S(1)} %pad_add_fusion.1.spots, bf16[1024,768]{1,0:T(8,128)(2,1)S(1)} %get-tuple-element.174.normed, ...), custom_call_target="tpu_custom_call", output_to_operand_aliasing={{0}: (9, {}), {1}: (10, {})} | custom-call | flops 54000001024 | bytes 1024 | tf_op jit(solution)/shard_map/feed/pallas_call | solution.py:106
  155.2 12.8 %middle.1 = (bf16[1024,768]{1,0:T(8,128)(2,1)}, f32[1024,768]{1,0:T(8,128)}, f32[1,768]{1,0:T(1,128)}, f32[1,768]{1,0:T(1,128)}, bf16[12,80,1024]{2,1,0:T(8,128)...) custom-call(s32[4]{0:T(128)S(1)} %pad_add_fusion.1.spots, ...), custom_call_target="tpu_custom_call" | custom-call | flops 38999998464 | bytes 1024 | tf_op jit(solution)/shard_map/middle/pallas_call | solution.py:106
  171.3 2.0 collective-permute-start.29
  173.7 2.9 collective-permute-start.31
  176.6 14.2 %attend_back.2 = (bf16[1152,1024]{1,0:T(8,128)(2,1)S(1)}, f32[2,3,64,128]{3,2,1,0:T(8,128)}) custom-call(f32[4]{0:T(128)S(1)} %copy-done.1, f32[4]{0:T(128)S(1)} %copy-done.15, f32[8,1024]{1,0:T(8,128)S(1)} %convert_element_type.109.aux, bf16[4,256,256]{2,1,0:T(8,128)(2,1)} %and_convert_fusion.mask, bf16[12,128,1024]{2,1,0:T(8,128)(2,1)S(1)} %copy-done.26, ...), custom_call_target="tpu_custom_call" | custom-call | flops 41999998976 | bytes 1024 | tf_op jit(solution)/shard_map/attend_back/pallas_call | solution.py:106
  194.5 3.8 %weight_grads.2 = bf16[768,1152]{1,0:T(8,128)(2,1)S(1)} custom-call(bf16[768,1024]{1,0:T(8,128)(2,1)} %get-tuple-element.203.normed_t, bf16[1152,1024]{1,0:T(8,128)(2,1)S(1)} %get-tuple-element.224.grads.grads_oth), custom_call_target="tpu_custom_call" | custom-call | flops 12000000000 | bytes 1024 | tf_op jit(solution)/shard_map/weight_grads/pallas_call | solution.py:106
  198.3 14.3 %attend_back.3 = (bf16[1152,1024]{1,0:T(8,128)(2,1)S(1)}, f32[2,3,64,128]{3,2,1,0:T(8,128)}) custom-call(f32[4]{0:T(128)S(1)} %copy-done.1, f32[4]{0:T(128)S(1)} %copy-done.15, f32[8,1024]{1,0:T(8,128)S(1)} %convert_element_type.109.aux, bf16[4,256,256]{2,1,0:T(8,128)(2,1)} %and_convert_fusion.mask, bf16[12,128,1024]{2,1,0:T(8,128)(2,1)S(1)} %copy-done.26, ...), custom_call_target="tpu_custom_call" | custom-call | flops 41999998976 | bytes 1024 | tf_op jit(solution)/shard_map/attend_back/pallas_call | solution.py:106
  215.0 3.1 %collective-permute-done.38 = bf16[384,128]{1,0:T(8,128)(2,1)S(1)} collective-permute-done((bf16[384,128]{1,0:T(8,128)(2,1)S(1)}, bf16[384,128]{1,0:T(8,128)(2,1)S(1)}, u32[]{:S(2)}, u32[]{:S(2)}) %collective-permute-start.38) | collective-permute-done | bytes 98336 | tf_op jit(solution)/shard_map/ppermute | solution.py:800
  221.3 3.7 %weight_grads.3 = bf16[768,1152]{1,0:T(8,128)(2,1)S(1)} custom-call(bf16[768,1024]{1,0:T(8,128)(2,1)} %get-tuple-element.203.normed_t, bf16[1152,1024]{1,0:T(8,128)(2,1)S(1)} %get-tuple-element.237.grads.grads_own), custom_call_target="tpu_custom_call" | custom-call | flops 12000000000 | bytes 1024 | tf_op jit(solution)/shard_map/weight_grads/pallas_call | solution.py:106
  226.5 4.8 %collective-permute-done.35.a_sent = bf16[4,48,1024]{2,1,0:T(8,128)(2,1)S(1)} collective-permute-done((bf16[4,48,1024]{2,1,0:T(8,128)(2,1)S(1)}, bf16[4,48,1024]{2,1,0:T(8,128)(2,1)S(1)}, u32[]{:S(2)}, u32[]{:S(2)}) %collective-permute-start.35) | collective-permute-done | bytes 393248 | tf_op jit(solution)/shard_map/ppermute | solution.py:800
  233.8 2.1 collective-permute-start.54
  236.0 5.1 %collective-permute-done.52 = bf16[48,1920]{1,0:T(8,128)(2,1)S(1)} collective-permute-done((bf16[48,1920]{1,0:T(8,128)(2,1)S(1)}, bf16[48,1920]{1,0:T(8,128)(2,1)S(1)}, u32[]{:S(2)}, u32[]{:S(2)}) %collective-permute-start.52) | collective-permute-done | bytes 184352 | tf_op jit(solution)/shard_map/ppermute | solution.py:804
  241.0 4.0 %collective-permute-done.53 = bf16[48,1920]{1,0:T(8,128)(2,1)S(1)} collective-permute-done((bf16[48,1920]{1,0:T(8,128)(2,1)S(1)}, bf16[48,1920]{1,0:T(8,128)(2,1)S(1)}, u32[]{:S(2)}, u32[]{:S(2)}) %collective-permute-start.53) | collective-permute-done | bytes 184352 | tf_op jit(solution)/shard_map/ppermute | solution.py:804
  248.3 8.9 %first_back.1 = (bf16[1024,768]{1,0:T(8,128)(2,1)}, f32[1,768]{1,0:T(1,128)}, f32[1,768]{1,0:T(1,128)}) custom-call(bf16[1024,768]{1,0:T(8,128)(2,1)} %tokens.2, f32[4,768]{1,0:T(4,128)S(1)} %pad_maximum_fusion.6.norms, f32[1024,768]{1,0:T(8,128)} %get-tuple-element.245.grad_hidden, bf16[768,640]{1,0:T(8,128)(2,1)S(1)} %bitcast.55, ...), custom_call_target="tpu_custom_call" | custom-call | flops 27000000512 | bytes 1024 | tf_op jit(solution)/shard_map/first_back/pallas_call | solution.py:106
  267.9 3.7 %collective-permute-done.46.b_sent = bf16[4,48,512]{2,1,0:T(8,128)(2,1)S(1)} collective-permute-done((bf16[4,48,512]{2,1,0:T(8,128)(2,1)S(1)}, bf16[4,48,512]{2,1,0:T(8,128)(2,1)S(1)}, u32[]{:S(2)}, u32[]{:S(2)}) %collective-permute-start.46) | collective-permute-done | bytes 196640 | tf_op jit(solution)/shard_map/ppermute | solution.py:800
  273.6 4.5 %collective-permute-start.47 = (bf16[408,128]{1,0:T(8,128)(2,1)S(1)}, bf16[408,128]{1,0:T(8,128)(2,1)S(1)}, u32[]{:S(2)}, u32[]{:S(2)}) collective-permute-start(bf16[408,128]{1,0:T(8,128)(2,1)S(1)} %pad_maximum_fusion.2), channel_id=1, source_target_pairs={{0,8},{2,10},{4,12},{6,14},{8,0},{10,2},{12,4},{14,6},{16,24},{18,... | collective-permute-start | bytes 313352 | tf_op jit(solution)/shard_map/ppermute | solution.py:800
  279.7 2.8 collective-permute-start.51
  284.6 1.9 collective-permute-done.49
  286.6 2.9 collective-permute-done.50
  290.2 3.6 %collective-permute-done.48 = bf16[408,128]{1,0:T(8,128)(2,1)S(1)} collective-permute-done((bf16[408,128]{1,0:T(8,128)(2,1)S(1)}, bf16[408,128]{1,0:T(8,128)(2,1)S(1)}, u32[]{:S(2)}, u32[]{:S(2)}) %collective-permute-start.48) | collective-permute-done | bytes 104480 | tf_op jit(solution)/shard_map/ppermute | solution.py:800
  (250 shorter events, 82.6 us)
Async XLA Ops:
  7.2 92.8 %all-gather.3.cloned.1.call-start = ((), (), s32[]{:S(2)}) async-start(), calls=%async_computation | async-start | bytes 6082560 | tf_op jit(solution)/shard_map/all_gather | solution.py:1071
  9.6 18.2 %collective-permute-start.2 = (bf16[48,1152]{1,0:T(8,128)(2,1)S(1)}, bf16[48,1152]{1,0:T(8,128)(2,1)S(1)}, u32[]{:S(2)}, u32[]{:S(2)}) collective-permute-start(bf16[48,1152]{1,0:T(8,128)(2,1)S(1)} %constant_dynamic-update-slice_fusion.refs_0_), channel_id=1, source_target_pairs={{0,24},{2,26},{4,28},{6,30},{8,0},{10,2},{12,4},{14,6},{16,8},{18,... | collective-permute-start | bytes 331784 | tf_op jit(solution)/shard_map/ppermute | solution.py:804
  14.7 13.2 %collective-permute-start.1 = (bf16[48,1152]{1,0:T(8,128)(2,1)S(1)}, bf16[48,1152]{1,0:T(8,128)(2,1)S(1)}, u32[]{:S(2)}, u32[]{:S(2)}) collective-permute-start(bf16[48,1152]{1,0:T(8,128)(2,1)S(1)} %constant_dynamic-update-slice_fusion.refs_0_), channel_id=1, source_target_pairs={{0,16},{2,18},{4,20},{6,22},{8,24},{10,26},{12,28},{14,30},{16,0},... | collective-permute-start | bytes 331784 | tf_op jit(solution)/shard_map/ppermute | solution.py:804
  14.7 13.2 %collective-permute-start = (bf16[48,1152]{1,0:T(8,128)(2,1)S(1)}, bf16[48,1152]{1,0:T(8,128)(2,1)S(1)}, u32[]{:S(2)}, u32[]{:S(2)}) collective-permute-start(bf16[48,1152]{1,0:T(8,128)(2,1)S(1)} %constant_dynamic-update-slice_fusion.refs_0_), channel_id=1, source_target_pairs={{0,8},{2,10},{4,12},{6,14},{8,16},{10,18},{12,20},{14,22},{16,24},... | collective-permute-start | bytes 331784 | tf_op jit(solution)/shard_map/ppermute | solution.py:804
  37.2 15.2 %collective-permute-start.7 = (bf16[4,2,48,640]{3,2,1,0:T(8,128)(2,1)S(1)}, bf16[4,2,48,640]{3,2,1,0:T(8,128)(2,1)S(1)}, u32[]{:S(2)}, u32[]{:S(2)}) collective-permute-start(bf16[4,2,48,640]{3,2,1,0:T(8,128)(2,1)S(1)} %get-tuple-element.144.refs_0_), channel_id=1, source_target_pairs={{0,4},{2,6},{4,0},{6,2},{8,12},{10,14},{12,8},{14,10},{16,20},{18,... | collective-permute-start | bytes 1474568 | tf_op jit(solution)/shard_map/ppermute | solution.py:800
  38.8 13.9 %collective-permute-start.8 = (bf16[4,2,48,512]{3,2,1,0:T(8,128)(2,1)S(1)}, bf16[4,2,48,512]{3,2,1,0:T(8,128)(2,1)S(1)}, u32[]{:S(2)}, u32[]{:S(2)}) collective-permute-start(bf16[4,2,48,512]{3,2,1,0:T(8,128)(2,1)S(1)} %get-tuple-element.154.refs_2_), channel_id=1, source_target_pairs={{0,2},{2,0},{4,6},{6,4},{8,10},{10,8},{12,14},{14,12},{16,18},{18,... | collective-permute-start | bytes 1179656 | tf_op jit(solution)/shard_map/ppermute | solution.py:800
  54.0 19.3 %collective-permute-start.13 = (bf16[48,1536]{1,0:T(8,128)(2,1)S(1)}, bf16[48,1536]{1,0:T(8,128)(2,1)S(1)}, u32[]{:S(2)}, u32[]{:S(2)}) collective-permute-start(bf16[48,1536]{1,0:T(8,128)(2,1)S(1)} %pad_maximum_fusion.4.refs_0_), channel_id=1, source_target_pairs={{0,24},{2,26},{4,28},{6,30},{8,0},{10,2},{12,4},{14,6},{16,8},{18,... | collective-permute-start | bytes 442376 | tf_op jit(solution)/shard_map/ppermute | solution.py:804
  57.5 15.8 %collective-permute-start.12 = (bf16[48,1536]{1,0:T(8,128)(2,1)S(1)}, bf16[48,1536]{1,0:T(8,128)(2,1)S(1)}, u32[]{:S(2)}, u32[]{:S(2)}) collective-permute-start(bf16[48,1536]{1,0:T(8,128)(2,1)S(1)} %pad_maximum_fusion.4.refs_0_), channel_id=1, source_target_pairs={{0,16},{2,18},{4,20},{6,22},{8,24},{10,26},{12,28},{14,30},{16,0},... | collective-permute-start | bytes 442376 | tf_op jit(solution)/shard_map/ppermute | solution.py:804
  57.5 15.8 %collective-permute-start.11 = (bf16[48,1536]{1,0:T(8,128)(2,1)S(1)}, bf16[48,1536]{1,0:T(8,128)(2,1)S(1)}, u32[]{:S(2)}, u32[]{:S(2)}) collective-permute-start(bf16[48,1536]{1,0:T(8,128)(2,1)S(1)} %pad_maximum_fusion.4.refs_0_), channel_id=1, source_target_pairs={{0,8},{2,10},{4,12},{6,14},{8,16},{10,18},{12,20},{14,22},{16,24},... | collective-permute-start | bytes 442376 | tf_op jit(solution)/shard_map/ppermute | solution.py:804
  74.0 17.7 %collective-permute-start.15 = (bf16[4,48,768]{2,1,0:T(8,128)(2,1)S(1)}, bf16[4,48,768]{2,1,0:T(8,128)(2,1)S(1)}, u32[]{:S(2)}, u32[]{:S(2)}) collective-permute-start(bf16[4,48,768]{2,1,0:T(8,128)(2,1)S(1)} %get-tuple-element.165.refs_0_), channel_id=1, source_target_pairs={{0,2},{2,0},{4,6},{6,4},{8,10},{10,8},{12,14},{14,12},{16,18},{18,... | collective-permute-start | bytes 884744 | tf_op jit(solution)/shard_map/ppermute | solution.py:800
  74.4 17.3 %collective-permute-start.16 = (bf16[4,48,768]{2,1,0:T(8,128)(2,1)S(1)}, bf16[4,48,768]{2,1,0:T(8,128)(2,1)S(1)}, u32[]{:S(2)}, u32[]{:S(2)}) collective-permute-start(bf16[4,48,768]{2,1,0:T(8,128)(2,1)S(1)} %get-tuple-element.170.refs_2_), channel_id=1, source_target_pairs={{0,4},{2,6},{4,0},{6,2},{8,12},{10,14},{12,8},{14,10},{16,20},{18,... | collective-permute-start | bytes 884744 | tf_op jit(solution)/shard_map/ppermute | solution.py:800
  92.4 26.2 %collective-permute-start.17 = (bf16[4,2,48,768]{3,2,1,0:T(8,128)(2,1)S(1)}, bf16[4,2,48,768]{3,2,1,0:T(8,128)(2,1)S(1)}, u32[]{:S(2)}, u32[]{:S(2)}) collective-permute-start(bf16[4,2,48,768]{3,2,1,0:T(8,128)(2,1)S(1)} %get-tuple-element.171.refs_0_), channel_id=1, source_target_pairs={{0,4},{2,6},{4,0},{6,2},{8,12},{10,14},{12,8},{14,10},{16,20},{18,... | collective-permute-start | bytes 1769480 | tf_op jit(solution)/shard_map/ppermute | solution.py:800
  93.7 24.9 %collective-permute-start.18 = (bf16[4,2,48,768]{3,2,1,0:T(8,128)(2,1)S(1)}, bf16[4,2,48,768]{3,2,1,0:T(8,128)(2,1)S(1)}, u32[]{:S(2)}, u32[]{:S(2)}) collective-permute-start(bf16[4,2,48,768]{3,2,1,0:T(8,128)(2,1)S(1)} %get-tuple-element.181.refs_2_), channel_id=1, source_target_pairs={{0,2},{2,0},{4,6},{6,4},{8,10},{10,8},{12,14},{14,12},{16,18},{18,... | collective-permute-start | bytes 1769480 | tf_op jit(solution)/shard_map/ppermute | solution.py:800
  118.3 14.1 %collective-permute-start.19 = (bf16[768,1536]{1,0:T(8,128)(2,1)S(1)}, bf16[768,1536]{1,0:T(8,128)(2,1)S(1)}, u32[]{:S(2)}, u32[]{:S(2)}) collective-permute-start(bf16[768,1536]{1,0:T(8,128)(2,1)S(1)} %get-tuple-element.179), channel_id=1, source_target_pairs={{0,1},{1,0},{2,3},{3,2},{4,5},{5,4},{6,7},{7,6},{8,9},{9,8},{10,11... | collective-permute-start | bytes 7077896 | tf_op jit(solution)/shard_map/ppermute | solution.py:796
  121.7 14.0 %collective-permute-start.21 = (bf16[768,768]{1,0:T(8,128)(2,1)}, bf16[768,768]{1,0:T(8,128)(2,1)S(1)}, u32[]{:S(2)}, u32[]{:S(2)}) collective-permute-start(bf16[768,768]{1,0:T(8,128)(2,1)} %bitcast.49), channel_id=1, source_target_pairs={{0,1},{1,0},{2,3},{3,2},{4,5},{5,4},{6,7},{7,6},{8,9},{9,8},{10,11... | collective-permute-start | bytes 3538952 | tf_op jit(solution)/shard_map/ppermute | solution.py:796
  122.0 13.7 %collective-permute-start.22 = (bf16[768,768]{1,0:T(8,128)(2,1)}, bf16[768,768]{1,0:T(8,128)(2,1)S(1)}, u32[]{:S(2)}, u32[]{:S(2)}) collective-permute-start(bf16[768,768]{1,0:T(8,128)(2,1)} %bitcast.51), channel_id=1, source_target_pairs={{0,1},{1,0},{2,3},{3,2},{4,5},{5,4},{6,7},{7,6},{8,9},{9,8},{10,11... | collective-permute-start | bytes 3538952 | tf_op jit(solution)/shard_map/ppermute | solution.py:796
  133.6 18.5 %collective-permute-start.20 = (bf16[4,2,48,768]{3,2,1,0:T(8,128)(2,1)S(1)}, bf16[4,2,48,768]{3,2,1,0:T(8,128)(2,1)S(1)}, u32[]{:S(2)}, u32[]{:S(2)}) collective-permute-start(bf16[4,2,48,768]{3,2,1,0:T(8,128)(2,1)S(1)} %get-tuple-element.187), channel_id=1, source_target_pairs={{0,2},{2,0},{4,6},{6,4},{8,10},{10,8},{12,14},{14,12},{16,18},{18,... | collective-permute-start | bytes 1769480 | tf_op jit(solution)/shard_map/ppermute | solution.py:800
  135.1 17.1 %collective-permute-start.23 = (bf16[4,2,48,768]{3,2,1,0:T(8,128)(2,1)S(1)}, bf16[4,2,48,768]{3,2,1,0:T(8,128)(2,1)S(1)}, u32[]{:S(2)}, u32[]{:S(2)}) collective-permute-start(bf16[4,2,48,768]{3,2,1,0:T(8,128)(2,1)S(1)} %get-tuple-element.195), channel_id=1, source_target_pairs={{0,4},{2,6},{4,0},{6,2},{8,12},{10,14},{12,8},{14,10},{16,20},{18,... | collective-permute-start | bytes 1769480 | tf_op jit(solution)/shard_map/ppermute | solution.py:800
  153.1 14.9 %collective-permute-start.24 = (bf16[4,48,768]{2,1,0:T(8,128)(2,1)S(1)}, bf16[4,48,768]{2,1,0:T(8,128)(2,1)S(1)}, u32[]{:S(2)}, u32[]{:S(2)}) collective-permute-start(bf16[4,48,768]{2,1,0:T(8,128)(2,1)S(1)} %get-tuple-element.208), channel_id=1, source_target_pairs={{0,4},{2,6},{4,0},{6,2},{8,12},{10,14},{12,8},{14,10},{16,20},{18,... | collective-permute-start | bytes 884744 | tf_op jit(solution)/shard_map/ppermute | solution.py:800
  154.5 13.5 %collective-permute-start.25 = (bf16[4,48,768]{2,1,0:T(8,128)(2,1)S(1)}, bf16[4,48,768]{2,1,0:T(8,128)(2,1)S(1)}, u32[]{:S(2)}, u32[]{:S(2)}) collective-permute-start(bf16[4,48,768]{2,1,0:T(8,128)(2,1)S(1)} %get-tuple-element.212), channel_id=1, source_target_pairs={{0,2},{2,0},{4,6},{6,4},{8,10},{10,8},{12,14},{14,12},{16,18},{18,... | collective-permute-start | bytes 884744 | tf_op jit(solution)/shard_map/ppermute | solution.py:800
  170.0 20.9 %collective-permute-start.27 = (bf16[768,1536]{1,0:T(8,128)(2,1)S(1)}, bf16[768,1536]{1,0:T(8,128)(2,1)S(1)}, u32[]{:S(2)}, u32[]{:S(2)}) collective-permute-start(bf16[768,1536]{1,0:T(8,128)(2,1)S(1)} %get-tuple-element.192), channel_id=1, source_target_pairs={{0,1},{1,0},{2,3},{3,2},{4,5},{5,4},{6,7},{7,6},{8,9},{9,8},{10,11... | collective-permute-start | bytes 7077896 | tf_op jit(solution)/shard_map/ppermute | solution.py:796
  171.2 19.8 %collective-permute-start.28 = (bf16[768,384]{1,0:T(8,128)(2,1)S(1)}, bf16[768,384]{1,0:T(8,128)(2,1)S(1)}, u32[]{:S(2)}, u32[]{:S(2)}) collective-permute-start(bf16[768,384]{1,0:T(8,128)(2,1)S(1)} %get-tuple-element.222), channel_id=1, source_target_pairs={{0,1},{1,0},{2,3},{3,2},{4,5},{5,4},{6,7},{7,6},{8,9},{9,8},{10,11... | collective-permute-start | bytes 1769480 | tf_op jit(solution)/shard_map/ppermute | solution.py:796
  171.3 19.5 %collective-permute-start.29 = (bf16[48,1536]{1,0:T(8,128)(2,1)S(1)}, bf16[48,1536]{1,0:T(8,128)(2,1)S(1)}, u32[]{:S(2)}, u32[]{:S(2)}) collective-permute-start(bf16[48,1536]{1,0:T(8,128)(2,1)S(1)} %get-tuple-element.225), channel_id=1, source_target_pairs={{0,8},{2,10},{4,12},{6,14},{8,16},{10,18},{12,20},{14,22},{16,24},... | collective-permute-start | bytes 442376 | tf_op jit(solution)/shard_map/ppermute | solution.py:804
  173.4 17.5 %collective-permute-start.30 = (bf16[48,1536]{1,0:T(8,128)(2,1)S(1)}, bf16[48,1536]{1,0:T(8,128)(2,1)S(1)}, u32[]{:S(2)}, u32[]{:S(2)}) collective-permute-start(bf16[48,1536]{1,0:T(8,128)(2,1)S(1)} %get-tuple-element.227), channel_id=1, source_target_pairs={{0,16},{2,18},{4,20},{6,22},{8,24},{10,26},{12,28},{14,30},{16,0},... | collective-permute-start | bytes 442376 | tf_op jit(solution)/shard_map/ppermute | solution.py:804
  173.7 17.2 %collective-permute-start.31 = (bf16[48,1536]{1,0:T(8,128)(2,1)S(1)}, bf16[48,1536]{1,0:T(8,128)(2,1)S(1)}, u32[]{:S(2)}, u32[]{:S(2)}) collective-permute-start(bf16[48,1536]{1,0:T(8,128)(2,1)S(1)} %get-tuple-element.228), channel_id=1, source_target_pairs={{0,24},{2,26},{4,28},{6,30},{8,0},{10,2},{12,4},{14,6},{16,8},{18,... | collective-permute-start | bytes 442376 | tf_op jit(solution)/shard_map/ppermute | solution.py:804
  190.8 21.7 %collective-permute-start.37 = (f32[2,3,64,128]{3,2,1,0:T(8,128)}, f32[2,3,64,128]{3,2,1,0:T(8,128)S(1)}, u32[]{:S(2)}, u32[]{:S(2)}) collective-permute-start(f32[2,3,64,128]{3,2,1,0:T(8,128)} %get-tuple-element.219), channel_id=1, source_target_pairs={{0,1},{1,0},{2,3},{3,2},{4,5},{5,4},{6,7},{7,6},{8,9},{9,8},{10,11... | collective-permute-start | bytes 589832 | tf_op jit(solution)/shard_map/ppermute | solution.py:796
  192.4 25.9 %collective-permute-start.33 = (bf16[4,2,48,896]{3,2,1,0:T(8,128)(2,1)S(1)}, bf16[4,2,48,896]{3,2,1,0:T(8,128)(2,1)S(1)}, u32[]{:S(2)}, u32[]{:S(2)}) collective-permute-start(bf16[4,2,48,896]{3,2,1,0:T(8,128)(2,1)S(1)} %get-tuple-element.235), channel_id=1, source_target_pairs={{0,4},{2,6},{4,0},{6,2},{8,12},{10,14},{12,8},{14,10},{16,20},{18,... | collective-permute-start | bytes 2064392 | tf_op jit(solution)/shard_map/ppermute | solution.py:800
  193.9 24.3 %collective-permute-start.32 = (bf16[4,2,48,1024]{3,2,1,0:T(8,128)(2,1)S(1)}, bf16[4,2,48,1024]{3,2,1,0:T(8,128)(2,1)S(1)}, u32[]{:S(2)}, u32[]{:S(2)}) collective-permute-start(bf16[4,2,48,1024]{3,2,1,0:T(8,128)(2,1)S(1)} %get-tuple-element.231), channel_id=1, source_target_pairs={{0,2},{2,0},{4,6},{6,4},{8,10},{10,8},{12,14},{14,12},{16,18},{18,... | collective-permute-start | bytes 2359304 | tf_op jit(solution)/shard_map/ppermute | solution.py:800
  215.0 30.2 %collective-permute-start.34 = (bf16[768,1152]{1,0:T(8,128)(2,1)S(1)}, bf16[768,1152]{1,0:T(8,128)(2,1)S(1)}, u32[]{:S(2)}, u32[]{:S(2)}) collective-permute-start(bf16[768,1152]{1,0:T(8,128)(2,1)S(1)} %weight_grads.2), channel_id=1, source_target_pairs={{0,1},{1,0},{2,3},{3,2},{4,5},{5,4},{6,7},{7,6},{8,9},{9,8},{10,11... | collective-permute-start | bytes 5308424 | tf_op jit(solution)/shard_map/ppermute | solution.py:796
  219.2 12.1 %collective-permute-start.36 = (bf16[4,48,896]{2,1,0:T(8,128)(2,1)S(1)}, bf16[4,48,896]{2,1,0:T(8,128)(2,1)S(1)}, u32[]{:S(2)}, u32[]{:S(2)}) collective-permute-start(bf16[4,48,896]{2,1,0:T(8,128)(2,1)S(1)} %get-tuple-element.243), channel_id=1, source_target_pairs={{0,2},{2,0},{4,6},{6,4},{8,10},{10,8},{12,14},{14,12},{16,18},{18,... | collective-permute-start | bytes 1032200 | tf_op jit(solution)/shard_map/ppermute | solution.py:800
  232.1 13.0 %collective-permute-start.53 = (bf16[48,1920]{1,0:T(8,128)(2,1)S(1)}, bf16[48,1920]{1,0:T(8,128)(2,1)S(1)}, u32[]{:S(2)}, u32[]{:S(2)}) collective-permute-start(bf16[48,1920]{1,0:T(8,128)(2,1)S(1)} %get-tuple-element.266), channel_id=1, source_target_pairs={{0,16},{2,18},{4,20},{6,22},{8,24},{10,26},{12,28},{14,30},{16,0},... | collective-permute-start | bytes 552968 | tf_op jit(solution)/shard_map/ppermute | solution.py:804
  246.3 11.6 %collective-permute-start.41 = (bf16[4,2,48,512]{3,2,1,0:T(8,128)(2,1)S(1)}, bf16[4,2,48,512]{3,2,1,0:T(8,128)(2,1)S(1)}, u32[]{:S(2)}, u32[]{:S(2)}) collective-permute-start(bf16[4,2,48,512]{3,2,1,0:T(8,128)(2,1)S(1)} %get-tuple-element.254), channel_id=1, source_target_pairs={{0,4},{2,6},{4,0},{6,2},{8,12},{10,14},{12,8},{14,10},{16,20},{18,... | collective-permute-start | bytes 1179656 | tf_op jit(solution)/shard_map/ppermute | solution.py:800
  (60 other events, 668.8 us)
Sparse Core Ops, SparseCore 0:
  18.3 81.6 all-gather.2

commit v3 on v2

--- a/solution.py
+++ b/solution.py
@@ -118,6 +118,32 @@
         cost_estimate=pl.CostEstimate(flops=micros * PACE, bytes_accessed=1024, transcendentals=0),
         name=name,
     )(*args)
+
+
+def pack_kernel(groups, *refs):
+    outs = refs[len(refs) - len(groups) :]
+    for out, group in zip(outs, groups):
+        start = 0
+        for index, first, size in group:
+            out[:, start : start + size] = refs[index][:, first : first + size]
+            start += size
+
+
+def pack(arrays, groups):
+    rows = arrays[0].shape[0]
+    shapes = [(rows, sum(size for unused, first, size in group)) for group in groups]
+    return call(
+        functools.partial(pack_kernel, groups),
+        "pack",
+        (1,),
+        [whole(a) for a in arrays],
+        [fixed(*shape) for shape in shapes],
+        tuple(jax.ShapeDtypeStruct(shape, LOW) for shape in shapes),
+        [],
+        8,
+        1,
+        apart(*arrays),
+    )
 
 
 def prepare_kernel(
@@ -205,36 +231,41 @@
 
     prefix[0] = state[:heads]
     keep = kept[step]
-    for side, (wa, wb) in enumerate(((wa_own, wb_own), (wa_oth, wb_oth))):
-        made = jnp.concatenate([nn(normed_now, wa[...]), nn(normed_now, wb[...])], axis=1).astype(LOW)
-        part = made.shape[1] // 3
-        values = made[:, 2 * part :]
+    halves = ((wa_own, wb_own), (wa_oth, wb_oth))
+    made = [jnp.concatenate([nn(normed_now, w[...]) for w in half], axis=1).astype(LOW) for half in halves]
+    part = made[0].shape[1] // 3
+    pairs = part // feat
+    for side in range(2):
+        values = made[side][:, 2 * part :]
         v_nat[:, side * part : (side + 1) * part] = values
-        for pair in range(part // feat):
-            place = side * part + pair * feat
-            index = place // feat
-            lanes = slice(pair * feat, (pair + 1) * feat)
-            q = made[:, :part][:, lanes].T
-            k = made[:, part : 2 * part][:, lanes].T
-            v = values[:, lanes].T
+        turned = [
+            [made[side][:, kind * part + p * feat : kind * part + (p + 1) * feat].T for p in range(pairs)]
+            for kind in range(3)
+        ]
+        indices = [side * pairs + p for p in range(pairs)]
+        logits = [
+            [nn(maps[2 * kind + 1, index], piece) for index, piece in zip(indices, turned[kind])]
+            for kind in range(2)
+        ]
+        for p, index in enumerate(indices):
+            place = slice(index * feat, (index + 1) * feat)
+            q_t[place, :] = turned[0][p]
+            k_t[place, :] = turned[1][p]
             state[heads, index : index + 1, :] += jnp.sum(
-                values[:, lanes].astype(F32), axis=0, keepdims=True
+                values[:, p * feat : (p + 1) * feat].astype(F32), axis=0, keepdims=True
             )
-            q_t[place : place + feat, :] = q
-            k_t[place : place + feat, :] = k
-            q_logits = nn(maps[1, index], q)
-            k_logits = nn(maps[3, index], k)
-            for one in range(2):
-                head = 2 * index + one
-                inside = slice(one * width, (one + 1) * width)
-                feat_q = softmax_pair(q_logits[inside])
-                feat_k = softmax_pair(k_logits[inside])
-                phi_q[head, :, rows] = feat_q
-                phi_k[head] = feat_k
-                phi_k_nat[rows, head * feat : (head + 1) * feat] = feat_k.T
-                value = jnp.concatenate([v[inside], tail], axis=0)
-                v_ext[head, :, rows] = value
-                state[head] = keep * state[head] + nt(value, feat_k * written)
+        inside = [slice(one * width, (one + 1) * width) for one in range(2)]
+        feats_q = [softmax_pair(piece[lines]) for piece in logits[0] for lines in inside]
+        feats_k = [softmax_pair(piece[lines]) for piece in logits[1] for lines in inside]
+        extended = [jnp.concatenate([piece[lines], tail], axis=0) for piece in turned[2] for lines in inside]
+        more = [nt(value, feat_k * written) for value, feat_k in zip(extended, feats_k)]
+        for local in range(2 * pairs):
+            head = 2 * side * pairs + local
+            phi_q[head, :, rows] = feats_q[local]
+            phi_k[head] = feats_k[local]
+            phi_k_nat[rows, head * feat : (head + 1) * feat] = feats_k[local].T
+            v_ext[head, :, rows] = extended[local]
+            state[head] = keep * state[head] + more[local]
     final[...] = state[...]
 
 
@@ -306,21 +337,29 @@
     padding = aux[3:4, rows]
     keep = carry[step]
     mask_now = mask[0]
-    for head in range(heads):
-        if head % 2 == 0:
-            center = center_of(final, entering, head // 2, 2 * att_t.shape[1]).T
-        pq = phi_q[head, :, rows]
-        scores = nn(phi_k_nat[rows, head * feat : (head + 1) * feat], pq)
-        weights = scores.astype(LOW) * mask_now
-        state = (prefix[0, head] + keep * entering[(head + heads // 2) % heads]).astype(LOW)
-        numer = nn(v_ext[head, :, rows], weights) + reach * nn(state, pq)
-        below = numer[width : width + 1] + padding
-        denom[head : head + 1, rows] = below
-        place = slice(head * width, (head + 1) * width)
-        att = numer[:width] * (1.0 / below)
-        att_t[place, rows] = att.astype(LOW)
-        near = center[head % 2 * width : (head % 2 + 1) * width, :]
-        att_c[place, :] = (att - jnp.concatenate([near] * (CHUNK // feat), axis=1)).astype(LOW)
+    half = heads // 2
+    centers = [center_of(final, entering, pair, 2 * att_t.shape[1]).T for pair in range(half)]
+    for side in range(2):
+        group = range(side * half, (side + 1) * half)
+        pqs = [phi_q[head, :, rows] for head in group]
+        states = [(prefix[0, head] + keep * entering[(head + half) % heads]).astype(LOW) for head in group]
+        scores = [
+            nn(phi_k_nat[rows, head * feat : (head + 1) * feat], pq) for head, pq in zip(group, pqs)
+        ]
+        inter = [nn(state, pq) for state, pq in zip(states, pqs)]
+        weights = [score.astype(LOW) * mask_now for score in scores]
+        numers = [
+            nn(v_ext[head, :, rows], weight) + reach * more
+            for head, weight, more in zip(group, weights, inter)
+        ]
+        for head, numer in zip(group, numers):
+            below = numer[width : width + 1] + padding
+            denom[head : head + 1, rows] = below
+            place = slice(head * width, (head + 1) * width)
+            att = numer[:width] * (1.0 / below)
+            att_t[place, rows] = att.astype(LOW)
+            near = centers[head // 2][head % 2 * width : (head % 2 + 1) * width, :]
+            att_c[place, :] = (att - jnp.concatenate([near] * (CHUNK // feat), axis=1)).astype(LOW)
 
 
 def attend(aux, mask, phi_q, phi_k_nat, v_ext, prefix, final, entering, carry):
@@ -489,23 +528,25 @@
     branch_t[:, rows] = low.T
     reach = aux[2:3, rows].astype(LOW)
     first = lax.broadcasted_iota(jnp.int32, (16, CHUNK), 0) == 0
-    pair = 0
-    for weights in (w_own, w_oth):
-        grad_att = nn(low, flat(weights[...]))
-        for inner in range(weights.shape[-1] // feat):
-            turned = grad_att[:, inner * feat : (inner + 1) * feat].T
-            for one in range(2):
-                head = 2 * pair + one
-                ga = turned[one * width : (one + 1) * width]
-                inverse = 1.0 / denom[head : head + 1, rows]
-                centered = att_c[head * width : (head + 1) * width, :].astype(F32)
-                gd = -jnp.sum(ga * centered, axis=0, keepdims=True) * inverse
-                ext = jnp.concatenate(
-                    [(ga * inverse).astype(LOW), jnp.where(first, gd, 0.0).astype(LOW)], axis=0
-                )
-                g_ext[head, :, rows] = ext
-                state[head] += nt(ext * reach, phi_q[head, :, rows])
-            pair += 1
+    grad_att = [nn(low, flat(weights[...])) for weights in (w_own, w_oth)]
+    turned = [
+        piece[:, inner * feat : (inner + 1) * feat].T
+        for piece in grad_att
+        for inner in range(piece.shape[1] // feat)
+    ]
+    exts = []
+    for head in range(heads):
+        ga = turned[head // 2][head % 2 * width : (head % 2 + 1) * width]
+        inverse = 1.0 / denom[head : head + 1, rows]
+        centered = att_c[head * width : (head + 1) * width, :].astype(F32)
+        gd = -jnp.sum(ga * centered, axis=0, keepdims=True) * inverse
+        exts.append(
+            jnp.concatenate([(ga * inverse).astype(LOW), jnp.where(first, gd, 0.0).astype(LOW)], axis=0)
+        )
+    more = [nt(ext * reach, phi_q[head, :, rows]) for head, ext in enumerate(exts)]
+    for head in range(heads):
+        g_ext[head, :, rows] = exts[head]
+        state[head] += more[head]
     leaving[...] = state[...].astype(LOW)
 
     @pl.when(step == count - 1)
@@ -539,8 +580,8 @@
         (
             streamed((rows, dim), LOW),
             streamed((rows, dim), F32),
-            streamed((1, dim), F32),
-            streamed((1, dim), F32),
+            jax.ShapeDtypeStruct((1, dim), F32),
+            jax.ShapeDtypeStruct((1, dim), F32),
             kept_in_vmem((heads, EXT, rows), LOW),
             streamed((heads, EXT, feat), LOW),
         )
@@ -609,62 +650,66 @@
         d_fq[...] = jnp.zeros_like(d_fq)
         d_fk[...] = jnp.zeros_like(d_fk)
 
-    for local in range(half // 2):
-        pair = side * half // 2 + local
-        logit_grads = ([], [])
-        value_grads = []
-        lanes = slice(local * feat, (local + 1) * feat)
-        center = center_of(final, entering, pair, 2 * phi_q.shape[2])
-        v_pair = (v_nat[:, lanes].astype(F32) - center[:1]).astype(LOW)
-        center = center.T
-        for one in range(2):
-            head = 2 * pair + one
-            kept_head = 2 * local + one
-            pq = phi_q[head, :, rows]
-            pk = phi_k[kept_head]
-            scores = nn(phi_k_nat[rows, head * feat : (head + 1) * feat], pq)
-            weights = scores.astype(LOW) * mask_now
-            ext = g_ext[head, :, rows]
-            numer = ext[:width]
-            blank = jnp.zeros_like(numer)
-            padded = jnp.concatenate([numer, blank] if one == 0 else [blank, numer], axis=0)
-            gw = nn(v_pair, padded)
-            gw = (gw + ext[width : width + 1].astype(F32)).astype(LOW) * mask_now
-            middle_v = center[one * width : (one + 1) * width, :]
-            before = prefix[0, kept_head] + keep_in * entering[(head + heads // 2) % heads]
-            before = jnp.concatenate(
-                [before[:width] - middle_v * before[width : width + 1], before[width:]], axis=0
-            ).astype(LOW)
-            value = v_ext[head, :, rows]
-            value = jnp.concatenate(
-                [
-                    (
-                        value[:width].astype(F32) - jnp.concatenate([middle_v] * (CHUNK // feat), axis=1)
-                    ).astype(LOW),
-                    value[width:],
-                ],
-                axis=0,
-            )
-            after = state[kept_head].astype(LOW)
-            reached = ext * reach
-            g_phi_q = nn(pk, gw) + tn(before, reached)
-            g_phi_k = nt(pq, gw) + tn(after, value * written)
-            g_value = nt(numer, weights) + nn(after[:width], pk * written)
-            value_grads.append(g_value.astype(LOW))
-            state[kept_head] = keep * state[kept_head] + nt(reached, pq)
-            logit_grads[0].append(softmax_pair_back(pq, g_phi_q).astype(LOW))
-            logit_grads[1].append(softmax_pair_back(pk, g_phi_k).astype(LOW))
-        place = slice(local * feat, (local + 1) * feat)
-        base = local * feat
-        for index, (both, kind, source, d_fmap) in enumerate(
-            ((logit_grads[0], 0, q_t, d_fq), (logit_grads[1], 2, k_t, d_fk))
-        ):
-            both = jnp.concatenate(both, axis=0)
-            start = base + index * part
-            grads[start : start + feat, rows] = nn(maps[kind, pair], both).astype(LOW)
-            d_fmap[local] += nt(source[place, :], both)
-        start = base + 2 * part
-        grads[start : start + feat, rows] = jnp.concatenate(value_grads, axis=0)
+    locals_ = range(half)
+    pairs = range(half // 2)
+    centers = [center_of(final, entering, side * half // 2 + p, 2 * phi_q.shape[2]) for p in pairs]
+    v_pairs = [
+        (v_nat[:, p * feat : (p + 1) * feat].astype(F32) - centers[p][:1]).astype(LOW) for p in pairs
+    ]
+    columns = [center.T for center in centers]
+    nears = [columns[n // 2][n % 2 * width : (n % 2 + 1) * width, :] for n in locals_]
+    pqs = [phi_q[side * half + n, :, rows] for n in locals_]
+    pks = [phi_k[n] for n in locals_]
+    exts = [g_ext[side * half + n, :, rows] for n in locals_]
+    scores = [
+        nn(phi_k_nat[rows, (side * half + n) * feat : (side * half + n + 1) * feat], pqs[n]) for n in locals_
+    ]
+    blank = jnp.zeros((width, CHUNK), LOW)
+    gws = []
+    for n in locals_:
+        numer = exts[n][:width]
+        padded = jnp.concatenate([numer, blank] if n % 2 == 0 else [blank, numer], axis=0)
+        gws.append(nn(v_pairs[n // 2], padded))
+    weights = [score.astype(LOW) * mask_now for score in scores]
+    gws = [
+        (gw + ext[width : width + 1].astype(F32)).astype(LOW) * mask_now for gw, ext in zip(gws, exts)
+    ]
+    befores, values, afters, reached = [], [], [], []
+    for n in locals_:
+        before = prefix[0, n] + keep_in * entering[(1 - side) * half + n]
+        befores.append(
+            jnp.concatenate([before[:width] - nears[n] * before[width : width + 1], before[width:]], axis=0).astype(LOW)
+        )
+        value = v_ext[side * half + n, :, rows]
+        near = jnp.concatenate([nears[n]] * (CHUNK // feat), axis=1)
+        value = jnp.concatenate([(value[:width].astype(F32) - near).astype(LOW), value[width:]], axis=0)
+        values.append(value * written)
+        afters.append(state[n].astype(LOW))
+        reached.append(exts[n] * reach)
+    g_phi_q = [nn(pks[n], gws[n]) + tn(befores[n], reached[n]) for n in locals_]
+    g_phi_k = [nt(pqs[n], gws[n]) + tn(afters[n], values[n]) for n in locals_]
+    g_values = [
+        nt(exts[n][:width], weights[n]) + nn(afters[n][:width], pks[n] * written) for n in locals_
+    ]
+    more = [nt(reached[n], pqs[n]) for n in locals_]
+    grads_q = [softmax_pair_back(pqs[n], g_phi_q[n]).astype(LOW) for n in locals_]
+    grads_k = [softmax_pair_back(pks[n], g_phi_k[n]).astype(LOW) for n in locals_]
+    for n in locals_:
+        state[n] = keep * state[n] + more[n]
+    both = [[jnp.concatenate(g[2 * p : 2 * p + 2], axis=0) for p in pairs] for g in (grads_q, grads_k)]
+    through = [[nn(maps[2 * kind, side * half // 2 + p], both[kind][p]) for p in pairs] for kind in range(2)]
+    onto = [
+        [nt(source[p * feat : (p + 1) * feat, :], both[kind][p]) for p in pairs]
+        for kind, source in enumerate((q_t, k_t))
+    ]
+    for p in pairs:
+        for kind in range(2):
+            start = kind * part + p * feat
+            grads[start : start + feat, rows] = through[kind][p].astype(LOW)
+        start = 2 * part + p * feat
+        grads[start : start + feat, rows] = jnp.concatenate(g_values[2 * p : 2 * p + 2], axis=0).astype(LOW)
+        d_fq[p] += onto[0][p]
+        d_fk[p] += onto[1][p]
 
     @pl.when(step == count - 1)
     def _():
@@ -742,7 +787,7 @@
         jax.ShapeDtypeStruct((dim, size), LOW),
         [],
         8,
-        4,
+        0,
         (*apart(normed_t), *pinned(grads)),
     )
 
@@ -779,8 +824,8 @@
         [block, fixed(1, dim), fixed(1, dim)],
         (
             streamed((rows, dim), LOW),
-            streamed((1, dim), F32),
-            streamed((1, dim), F32),
+            jax.ShapeDtypeStruct((1, dim), F32),
+            jax.ShapeDtypeStruct((1, dim), F32),
         ),
         [],
         16,
@@ -809,9 +854,10 @@
 
 
 class Places:
-    def __init__(self, size):
+    def __init__(self, size, staged):
         self.size = size
         self.deep = size // 4
+        self.staged = staged
         place = lax.axis_index("dp")
         self.spots = jnp.stack([place % 2, (place // 2) % 2, place // 4, lax.axis_index("mp")])
 
@@ -861,7 +907,7 @@
 
 def first_by(shape):
     tail = (0,) * (len(shape) - 1)
-    return pl.BlockSpec((1, *shape[1:]), lambda d, *_: (d, *tail))
+    return pl.BlockSpec((1, *shape[1:]), lambda d, *_: (jnp.minimum(d, shape[0] - 1), *tail))
 
 
 def gather_pair(values, axes, at, *others, kind=jax.ShapeDtypeStruct):
@@ -885,8 +931,28 @@
     )
 
 
-def first_fold_kernel(axes, cuts, spots, *refs):
+def first_fold_kernel(axes, cuts, deep, spots, *refs):
     outs = refs[-4:]
+    step = pl.program_id(0)
+    if len(refs) == 5 + 2 * len(cuts):
+        rider = refs[-5]
+        rows = outs[0].shape[2]
+
+        @pl.when(step == deep)
+        def _():
+            for index in range(rider.shape[0] // rows):
+                group, place = divmod(index, 2)
+                outs[0][0, place, :, group * 128 : (group + 1) * 128] = rider[index * rows : (index + 1) * rows, :]
+
+        @pl.when(step < deep)
+        def _():
+            first_fold_step(axes, cuts, spots, refs, outs)
+
+    else:
+        first_fold_step(axes, cuts, spots, refs, outs)
+
+
+def first_fold_step(axes, cuts, spots, refs, outs):
     for index, axis in enumerate(axes):
         bit = spots[0 if axis == "x" else 1]
         sent, kept = outs[2 * index : 2 * index + 2]
@@ -929,39 +995,45 @@
         self.cuts = [cut for own, oth, cut in segments]
         self.cut = sum(self.cuts)
         self.terms = [[own, swap(oth)] for own, oth, cut in segments]
-        if at.size % 4 == 0:
+        if at.staged:
             split = lambda v: v.reshape(at.deep, 2, 2, v.shape[0] // at.size, v.shape[1])
             self.terms = [[split(v) for v in pair] for pair in self.terms]
 
     def wait_for(self, *others):
         self.terms[0][1] = after(self.terms[0][1], *others)
 
-    def fold(self, axes):
+    def fold(self, axes, rider=None):
         at = self.at
         flats = [v for pair in self.terms for v in pair]
-        if at.size % 4:
+        if not at.staged:
             return flats[0]
         if self.cuts:
             columns = sum(pair[0].shape[-1] for pair in self.terms)
             head = flats[0].shape[:2]
             rows = flats[0].shape[3]
             lefts = [(*head, rows, self.cut), (*head, rows, columns - self.cut)]
-            kernel = functools.partial(first_fold_kernel, axes, tuple(self.cuts))
+            kernel = functools.partial(first_fold_kernel, axes, tuple(self.cuts), at.deep)
         else:
             lefts = [(v.shape[0], *v.shape[2:]) for v in flats[::2]]
             kernel = functools.partial(fold_kernel, axes)
         outs = [left for left in lefts for unused in (0, 1)]
+        extra = []
+        steps = at.deep
+        if rider is not None:
+            extra = [rider]
+            steps += 1
+            outs[0] = (steps, *outs[0][1:])
         a_sent, a_kept, b_sent, b_kept = call(
             kernel,
             "fold",
-            (at.deep,),
-            [first_by(v.shape) for v in flats],
+            (steps,),
+            [first_by(v.shape) for v in flats] + [whole(v) for v in extra],
             [first_by(left) for left in outs],
             tuple(jax.ShapeDtypeStruct(left, LOW) for left in outs),
             [],
             12,
             0,
-            (at.spots, *flats),
+            (at.spots, *flats, *extra),
             scalars=1,
         )
         self.cuts = []
@@ -970,7 +1042,7 @@
 
     def spread(self):
         at = self.at
-        if at.size % 4:
+        if not at.staged:
             return self.terms[0][0]
         a, b = self.terms
         shape = (a[0].shape[1], self.cut + b[0].shape[-1])
@@ -991,7 +1063,7 @@
         return own
 
     def end(self, *others):
-        if self.at.size % 4:
+        if not self.at.staged:
             sums = [own.astype(F32) + moved.astype(F32) for own, moved in self.terms]
             total = [t[:, :cut] for t, cut in zip(sums, self.cuts)] + [t[:, cut:] for t, cut in zip(sums, self.cuts)]
             total = lax.psum_scatter(jnp.concatenate(total, axis=1), "dp", scatter_dimension=0, tiled=True)
@@ -1000,6 +1072,158 @@
                 self.parts[1] = after(self.parts[1], *others)
             total = sum(p.astype(F32) for p in self.parts)
         return total
+
+
+def ride_kernel(deep, spots, *refs):
+    a_kept, a_moved, b_kept, b_moved, gain1, shift1, gain2, shift2, maps, early = refs[:10]
+    late = refs[10 : 10 + deep]
+    a_sent, a_left, b_sent, b_left, norm_low, maps_low, g_fc, g_down, g_out = refs[10 + deep :]
+    rows = a_left.shape[1]
+    units = early.shape[1] // 2
+    total = late[0][...].astype(F32)
+    for part in late[1:]:
+        total = total + part[...].astype(F32)
+    rest = total.shape[1] - 2 * units
+    cut = units + (rest // 128 + 1) // 2 * 128
+    g_fc[:, :units] = early[:, :units]
+    g_down[:, :units] = early[:, units:]
+    g_fc[:, units:] = total[:, :units]
+    g_down[:, units:] = total[:, cut : cut + units]
+    g_out[:, : cut - units] = total[:, units:cut]
+    g_out[:, cut - units :] = total[:, cut + units :]
+    blank = jnp.zeros((4, gain1.shape[1]), F32)
+    norm_now = jnp.concatenate([gain1[...], shift1[...], gain2[...], shift2[...], blank], axis=0)
+    norm_low[...] = jnp.concatenate([norm_now, jnp.zeros_like(norm_now)], axis=0).astype(LOW)
+    for index in range(maps.shape[0] // rows):
+        group, place = divmod(index, 2)
+        moved = a_moved[deep, place, :, group * 128 : (group + 1) * 128].astype(F32)
+        here = slice(index * rows, (index + 1) * rows)
+        maps_low[here, :] = (maps[here, :].astype(F32) + moved).astype(LOW)
+    for kept, moved, sent, left, bit in (
+        (a_kept, a_moved, a_sent, a_left, spots[1]),
+        (b_kept, b_moved, b_sent, b_left, spots[0]),
+    ):
+        columns = left.shape[2]
+        for out, place in ((sent, 1 - bit), (left, bit)):
+            terms = [r[:deep, pl.ds(place, 1)].astype(F32) for r in (kept, moved)]
+            total = (terms[0] + terms[1]).astype(LOW)
+            if out is left:
+                out[...] = total.reshape(deep, rows, columns)
+            else:
+                out[: deep * rows] = total.reshape(deep * rows, columns)
+        rest = norm_now[:, columns:]
+        rest = jnp.concatenate([rest, jnp.zeros((8, columns - rest.shape[1]), F32)], axis=1)
+        sent[deep * rows :] = jnp.concatenate([norm_now[:, :columns], rest], axis=0).astype(LOW)
+
+
+def last_spread_kernel(spots, a_kept, a_moved, b_kept, b_moved, norm, norm_far, maps, maps_moved, *outs):
+    *parts, maps_low = outs
+    deep, rows, cut = a_kept.shape
+    dim = norm.shape[1]
+    maps_low[...] = (maps[...].astype(F32) + maps_moved[...].astype(F32)).astype(LOW)
+    near = []
+    for moved in (b_moved, a_moved):
+        columns = moved.shape[1]
+        tail = moved[deep * rows :].astype(F32)
+        near.append(jnp.concatenate([tail[:8], tail[8:, : dim - columns]], axis=1))
+    plane = (norm[...].astype(F32)[:8] + near[0]) + (near[1] + norm_far[...].astype(F32)[:8])
+    tail = jnp.concatenate([plane[:, i : i + 128] for i in range(0, dim, 128)], axis=0)
+    for s, out in enumerate(parts):
+        spot = lax.rem(spots[2] + s, deep)
+        place = pl.ds(pl.multiple_of(spot * rows, rows), rows)
+        rest = out.shape[1] - 128
+        out[:, :cut] = (a_kept[spot].astype(F32) + a_moved[place].astype(F32)).astype(LOW)
+        out[:, cut:rest] = (b_kept[spot].astype(F32) + b_moved[place].astype(F32)).astype(LOW)
+        out[:, rest:] = tail.astype(LOW)
+
+
+def finish_kernel(spots, *refs):
+    deep = len(refs) - 9
+    parts = refs[:deep]
+    maps, maps_moved, g_query, g_key, g_value, norms, map_q, map_k, held = refs[deep:]
+    rows, part = g_query.shape
+    total = None
+    for s, ref in enumerate(parts):
+        value = ref[...].astype(F32)
+        held[lax.rem(spots[2] + deep - s, deep)] = value[:, 3 * part :]
+        total = value if total is None else total + value
+    for index, out in enumerate((g_query, g_key, g_value)):
+        out[...] = total[:, index * part : (index + 1) * part]
+    together = held[0]
+    for spot in range(1, deep):
+        together = together + held[spot]
+    for index in range(rows // 8):
+        norms[:, index * 128 : (index + 1) * 128] = together[index * 8 : (index + 1) * 8]
+    width = map_q.shape[1]
+    both = maps[...].astype(F32) + maps_moved[...].astype(F32)
+    heads = map_q.shape[0]
+    for kind, out in enumerate((map_q, map_k)):
+        for pair in range(heads // 2):
+            start = (kind * heads // 2 + pair) * width
+            block = both[start : start + width]
+            out[2 * pair] = block[:, :width]
+            out[2 * pair + 1] = block[:, width:]
+
+
+def finish_last(sums, norm, map_grads, early, late, part, heads, width, at):
+    small = lambda shape, kind: jax.ShapeDtypeStruct(shape, kind)
+    (a_kept, a_moved), (b_kept, b_moved) = sums.terms
+    deep, unused, rows, cut = a_kept.shape
+    rest = b_kept.shape[3]
+    dim = norm[0].shape[1]
+    units = early.shape[1]
+    ins = (a_kept, a_moved, b_kept, b_moved, *norm, map_grads, early, *late)
+    outs = (
+        small((deep * rows + 16, cut), LOW),
+        small((deep, rows, cut), LOW),
+        small((deep * rows + 16, rest), LOW),
+        small((deep, rows, rest), LOW),
+        small((16, dim), LOW),
+        small(map_grads.shape, LOW),
+        small((rows, units), F32),
+        small((rows, units), F32),
+        small((rows, part), F32),
+    )
+
+    def run(kernel, name, ins, outs, scratch):
+        return call(
+            kernel,
+            name,
+            (1,),
+            [whole(v) for v in ins],
+            [fixed(*out.shape) for out in outs],
+            outs,
+            scratch,
+            12,
+            0,
+            (at.spots, *ins),
+            scalars=1,
+        )
+
+    kernel = functools.partial(ride_kernel, deep)
+    a_sent, a_kept, b_sent, b_kept, norm_low, maps, *done = run(kernel, "ride", ins, outs, [])
+    across = [(i, i ^ 3) for i in range(at.size)]
+    ins = (
+        a_kept,
+        at.flip(a_sent, "y"),
+        b_kept,
+        at.flip(b_sent, "x"),
+        norm_low,
+        lax.ppermute(norm_low, "dp", across),
+        maps,
+        flip(maps, 4 << (at.size.bit_length() - 4), at.size),
+    )
+    ins = lax.optimization_barrier(ins)
+    outs = (small((rows, cut + rest + 128), LOW),) * deep + (small(map_grads.shape, LOW),)
+    own, *sends, maps = run(last_spread_kernel, "last_spread", ins, outs, [])
+    ins = (own, *(turn(p, 4 * s, at.size) for s, p in enumerate(sends, 1)), maps, at.flip(maps, "y"))
+    ins = lax.optimization_barrier(ins)
+    outs = (
+        (small((rows, part), F32),) * 3
+        + (small((8, dim), F32),)
+        + (small((heads // 2, width, width), F32),) * 2
+    )
+    return done, run(finish_kernel, "finish", ins, outs, [pltpu.VMEM((deep, rows, 128), F32)])
 
 
 def add_along(value, steps, size):
@@ -1035,6 +1259,27 @@
     part = w_query.shape[1]
     count = rows // CHUNK
     core = lax.axis_index("mp")
+    staged = size % 4 == 0 and dim // size % 16 == 0
+    where = Places(size, staged)
+    units = w_fc.shape[1] // 2
+    cut = (3 * part // feat + 1) // 2 * feat
+    cut_out = (part // feat + 1) // 2 * feat
+    shard_qkv, shard_early, shard_late = pack(
+        (w_query, w_key, w_value, w_out, w_fc, w_down),
+        (
+            ((0, 0, part), (1, 0, part), (2, 0, part)),
+            ((4, 0, units), (5, 0, units), (3, 0, part)),
+            ((4, units, units), (5, units, units)),
+        ),
+    )
+    early = lax.all_gather(shard_early, ("dp", "mp"), axis=0)
+    early = early.reshape(size, 2, *shard_early.shape)
+    if shard_early.shape[0] % 16:
+        early = early.swapaxes(0, 1).reshape(1, 2, dim, -1)
+    fq_oth, fk_oth = swap(fmap_query), swap(fmap_key)
+    if staged:
+        qkv = gather_line(shard_qkv, cut, where)
+        lengths = after(lengths, qkv[0])
 
     ends = jnp.cumsum(lengths[0])
     places = core * rows - 1 + jnp.arange(rows + 1, dtype=jnp.int32)
@@ -1060,26 +1305,13 @@
 
     norms = jnp.stack([norm1_gain, norm1_shift, norm2_gain, norm2_shift])
 
-    where = Places(size)
-    staged = size % 4 == 0
-    units = w_fc.shape[1] // 2
-    cut = (3 * part // feat + 1) // 2 * feat
-    cut_out = (part // feat + 1) // 2 * feat
-    shard_qkv = jnp.concatenate([w_query, w_key, w_value], axis=1)
-    shard_early = jnp.concatenate([w_fc[:, :units], w_down[:, :units], w_out], axis=1)
-    shard_late = jnp.concatenate([w_fc[:, units:], w_down[:, units:]], axis=1)
-    early = lax.all_gather(shard_early, ("dp", "mp"), axis=0)
-    early = early.reshape(size, 2, *shard_early.shape)
-    if shard_early.shape[0] % 16:
-        early = early.swapaxes(0, 1).reshape(1, 2, dim, -1)
-    fq_oth, fk_oth = swap(fmap_query), swap(fmap_key)
-    ready = lax.optimization_barrier((shard_late, norms, aux, mask, kept, carry, where.spots))
-    shard_late, norms, aux, mask, kept, carry, spots = ready
-    where.spots = spots
+    shard_late, norms, aux, mask, kept, carry = lax.optimization_barrier(
+        (shard_late, norms, aux, mask, kept, carry)
+    )
+    spots = where.spots
     if staged:
-        qkv = gather_line(shard_qkv, cut, where)
         qkv = gather_pair(qkv, "xy", where)
-        shard_late, tokens = after(shard_late, qkv[0]), after(tokens, qkv[0])
+        shard_late, tokens = after(shard_late, qkv[0]), after(tokens, qkv[0], mask)
     normed1, normed1_t, cot, cot_t, maps = prepare(
         tokens, cotangent, norms, fmap_query, fq_oth, fmap_key, fk_oth
     )
@@ -1127,59 +1359,69 @@
         spots, hidden, feed, grad_normed, cot, norms, early, units, att_t, att_c, denom, phi_q, aux
     )
     sums_early.wait_for(d_gain2)
-    leaving = after(leaving, sums_early.spread())
-    arriving = lax.ppermute(leaving, "mp", [(1, 0)])
+    started = sums_early.spread()
+    arriving = lax.ppermute(after(leaving, started), "mp", [(1, 0)])
+    d_out_oth = after(d_out_oth, started)
     sums_late = Scatter([(d_late_own, d_late_oth, units), (d_out_own, d_out_oth, cut_out)], where)
+    sums_late.wait_for(started)
+    arriving = after(arriving, sums_late.fold("xy"))
     back = functools.partial(
         attend_back, carry=carry, kept=kept, prefix=prefix, final=final, entering=entering, q_t=q_t, k_t=k_t, maps=maps
     )
     back_inputs = (aux, mask, phi_q, phi_k, phi_k_nat, v_nat, v_ext, g_ext)
     lanes = lambda v: v.reshape(-1, feat)
     grads_oth, maps_oth = back(1, *back_inputs, arriving=arriving)
-    sums_late.wait_for(maps_oth)
-    grads_oth = after(grads_oth, sums_late.fold("xy"))
     total_early = sums_early.end(maps_oth)
-    maps_oth = swap(maps_oth)
-    d_qkv_oth = weight_grads(normed1_t, grads_oth)
-    arriving = after(arriving, d_qkv_oth, total_early)
+    d_qkv_oth = weight_grads(normed1_t, after(grads_oth, total_early))
+    sums_late.wait_for(d_qkv_oth)
+    arriving = after(arriving, sums_late.fold("yx"))
     grads_own, maps_own = back(0, *back_inputs, arriving=arriving)
     sums_late.wait_for(maps_own)
-    grads_own = after(grads_own, sums_late.fold("yx"))
-    map_grads = add_along(lanes(maps_own + maps_oth), [1], size)
+    grads_own = after(grads_own, sums_late.spread())
+    map_grads = lanes(maps_own + swap(maps_oth))
     d_qkv_own = weight_grads(normed1_t, grads_own)
+    if staged:
+        map_grads = map_grads.astype(LOW)
+        for step in [4 << i for i in range(size.bit_length() - 4)]:
+            moved = after(flip(map_grads, step, size), d_qkv_own)
+            map_grads = (map_grads.astype(F32) + moved.astype(F32)).astype(LOW)
     sums_qkv = Scatter([(d_qkv_own, d_qkv_oth, cut)], where)
-    grad_hidden = after(grad_hidden, sums_qkv.fold("xy"))
-    sums_late.wait_for(d_qkv_own)
-    grad_hidden = after(grad_hidden, sums_late.spread())
-    map_grads = add_along(after(map_grads, d_qkv_own), [2], size)
+    grad_hidden = after(grad_hidden, sums_qkv.fold("xy", map_grads if staged else None))
     grad_tokens, d_gain1, d_shift1 = first_back(tokens, norms, grad_hidden, qkv, (grads_own, grads_oth))
-    sums_qkv.wait_for(d_gain1)
-    norm_grads = jnp.concatenate([d_gain1, d_shift1, d_gain2, d_shift2], axis=0)
-    norm_grads = lanes(after(norm_grads, sums_qkv.fold("yx")))
-    norm_grads = add_along(norm_grads + swap(norm_grads), [1, 2], size)
-    small = jnp.concatenate([map_grads, norm_grads], axis=0)
-    small = add_along(after(small, sums_qkv.spread()), [4 << i for i in range(size.bit_length() - 3)], size)
-    map_grads = small[: map_grads.shape[0]].reshape(2, heads // 4, width, 2, width)
-    map_grads = map_grads.swapaxes(2, 3).reshape(2, heads // 2, width, width)
-    norm_grads = small[-norm_grads.shape[0] :].reshape(4, dim)
-    total_late = sums_late.end()
-    grad_qkv = sums_qkv.end()
-    cut_late = units + cut_out
+    norm_grads = (d_gain1, d_shift1, d_gain2, d_shift2)
+    if staged:
+        sums_qkv.wait_for(d_gain1)
+        done, (g_query, g_key, g_value, norm_grads, map_q, map_k) = finish_last(
+            sums_qkv, norm_grads, map_grads, total_early, sums_late.parts, part, heads, width, where
+        )
+        g_fc, g_down, g_out = done
+    else:
+        total_late = sums_late.end()
+        grad_qkv = sums_qkv.end()
+        g_query, g_key, g_value = (grad_qkv[:, i * part : (i + 1) * part] for i in range(3))
+        norm_grads, map_grads = lax.psum((jnp.concatenate(norm_grads, axis=0), map_grads), "dp")
+        map_grads = map_grads.reshape(2, heads // 4, width, 2, width)
+        map_q, map_k = map_grads.swapaxes(2, 3).reshape(2, heads // 2, width, width)
+        cut_late = units + cut_out
+        g_fc = jnp.concatenate([total_early[:, :units], total_late[:, :units]], axis=1)
+        g_down = jnp.concatenate([total_early[:, units:], total_late[:, cut_late : cut_late + units]], axis=1)
+        g_out = jnp.concatenate([total_late[:, units:cut_late], total_late[:, cut_late + units :]], axis=1)
+    norm_grads = norm_grads + swap(norm_grads)
     return (
         mixed,
         grad_tokens,
         norm_grads[0],
         norm_grads[1],
-        grad_qkv[:, :part],
-        grad_qkv[:, part : 2 * part],
-        grad_qkv[:, 2 * part :],
-        jnp.concatenate([total_late[:, units:cut_late], total_late[:, cut_late + units :]], axis=1),
-        map_grads[0],
-        map_grads[1],
+        g_query,
+        g_key,
+        g_value,
+        g_out,
+        map_q,
+        map_k,
         norm_grads[2],
         norm_grads[3],
-        jnp.concatenate([total_early[:, :units], total_late[:, :units]], axis=1),
-        jnp.concatenate([total_early[:, units:], total_late[:, cut_late : cut_late + units]], axis=1),
+        g_fc,
+        g_down,
     )
 
 

time: 306 us -> 270 us (0.88)
  Pallas kernels: 149 us -> 137 us
  local copies, waits for them, and re-layouts: 15.7 us -> 7.19 us
  waiting for transfers between devices: 52.4 us -> 46 us
  starting transfers between devices: 60.7 us -> 55.2 us
  other arithmetic: 9.89 us -> 5.34 us
    pallas_call x28 -> x30, Pallas kernels: 149 us -> 137 us  [call(): pl.pallas_call(kernel, grid_spec=pltpu.PrefetchScalarGridSpec(num_scalar_...]
    ppermute x26 -> x23, starting transfers between devices: 32 us -> 25.2 us  [flip(): return lax.ppermute(piece, 'dp', [(i, i ^ bit) for i in range(size)])]
    ppermute x15, waiting for transfers between devices: 14 us -> 8.54 us  [turn(): lax.ppermute(piece, 'dp', [(i, (i + by) % size) for i in range(size)])]
    ppermute x26 -> x23, waiting for transfers between devices: 31 us -> 25.8 us  [flip(): return lax.ppermute(piece, 'dp', [(i, i ^ bit) for i in range(size)])]
    concatenate x7 -> x0, other arithmetic: 4.3 us -> none  [the longest x1 1.46 us: per_device(): jnp.concatenate([w_fc[:, :units], w_down[:, :units], w_out], axis=1)]
    ppermute x1 -> x2, waiting for transfers between devices: 0.01 us -> 3.26 us  [the longest x1 3.26 us: finish_last(): lax.ppermute(norm_low, 'dp', across)]
    unnamed x78 -> x80, local copies, waits for them, and re-layouts: 6.45 us -> 4.88 us
  transfers between devices with their start and end apart: 56 -> 54, of which waited for: 18 -> 14; matrix products, arithmetic and copies ran while one was open for 6% -> 3% of each run, Pallas kernels for 48% -> 50%
where the time goes in v3:
time: 270 us; the launch traced here: 266 us
  Pallas kernels  137 us (51%)
  starting transfers between devices  55.2 us (20%)
  waiting for transfers between devices  46 us (17%)
  between operations  15.2 us (6%)
  local copies, waits for them, and re-layouts  7.19 us (3%)
  other arithmetic  5.34 us (2%)
    pallas_call x30, Pallas kernels, call(): pl.pallas_call(kernel, grid_spec=pltpu.PrefetchScalarGridSpec(num_scalar_...  137 us
    ppermute x23, waiting for transfers between devices, flip(): return lax.ppermute(piece, 'dp', [(i, i ^ bit) for i in range(size)])  25.8 us
    ppermute x23, starting transfers between devices, flip(): return lax.ppermute(piece, 'dp', [(i, i ^ bit) for i in range(size)])  25.2 us
    ppermute x15, starting transfers between devices, turn(): lax.ppermute(piece, 'dp', [(i, (i + by) % size) for i in range(size)])  24.4 us
    ppermute x15, waiting for transfers between devices, turn(): lax.ppermute(piece, 'dp', [(i, (i + by) % size) for i in range(size)])  8.54 us
    all_gather x1, waiting for transfers between devices, per_device(): early = lax.all_gather(shard_early, ('dp', 'mp'), axis=0)  7.2 us
  transfers between devices with their start and end apart: 54, of which 14 were waited for; matrix products, arithmetic and copies ran while one was open for 3% of the time, Pallas kernels for 50%

profile of v3, /device:TPU:0, one launch (start us, length us, event | category | flops | bytes accessed | tf_op | source)
XLA Modules:
  0.0 266.2 jit_solution(3766236027445242811)
XLA Ops:
  7.3 1.8 pack.1
  9.1 5.0 %collective-permute-start.2 = (bf16[48,1152]{1,0:T(8,128)(2,1)S(1)}, bf16[48,1152]{1,0:T(8,128)(2,1)S(1)}, u32[]{:S(2)}, u32[]{:S(2)}) collective-permute-start(bf16[48,1152]{1,0:T(8,128)(2,1)S(1)} %get-tuple-element.169.refs_0_), channel_id=1, source_target_pairs={{0,24},{2,26},{4,28},{6,30},{8,0},{10,2},{12,4},{14,6},{16,8},{18,... | collective-permute-start | bytes 331784 | tf_op jit(solution)/shard_map/ppermute | solution.py:849
  17.6 6.2 %collective-permute-done.1.refs_2_ = bf16[48,1152]{1,0:T(8,128)(2,1)S(1)} collective-permute-done((bf16[48,1152]{1,0:T(8,128)(2,1)S(1)}, bf16[48,1152]{1,0:T(8,128)(2,1)S(1)}, u32[]{:S(2)}, u32[]{:S(2)}) %collective-permute-start.1) | collective-permute-done | bytes 110624 | tf_op jit(solution)/shard_map/ppermute | solution.py:849
  33.5 2.4 collective-permute-done.4.refs_3_
  38.7 5.2 %prepare.1 = (bf16[1024,768]{1,0:T(8,128)(2,1)S(1)}, bf16[768,1024]{1,0:T(8,128)(2,1)}, bf16[1024,768]{1,0:T(8,128)(2,1)S(1)}, bf16[768,1024]{1,0:T(8,128)(2,1)S(1)}, bf16[4,6,128,128]{3,2,1,0:T(8,128)(2,1)S(1)}) custom-call(bf16[1024,768]{1,0:T(8,128)(2,1)} %tokens.2, bf16[1024,768]{1,0:T(8,128)(2,1)} %cot.1, f32[4,768]{1,0:T(4,128)S(1)} %pad_maximum_fusion.norms, ...), custom_call_target="tpu_custom_call" | custom-call | flops 15000000512 | bytes 1024 | tf_op jit(solution)/shard_map/prepare/pallas_call | solution.py:106
  45.2 5.7 %collective-permute-done.7.refs_1_ = bf16[4,2,48,640]{3,2,1,0:T(8,128)(2,1)S(1)} collective-permute-done((bf16[4,2,48,640]{3,2,1,0:T(8,128)(2,1)S(1)}, bf16[4,2,48,640]{3,2,1,0:T(8,128)(2,1)S(1)}, u32[]{:S(2)}, u32[]{:S(2)}) %collective-permute-start.7) | collective-permute-done | bytes 491552 | tf_op jit(solution)/shard_map/ppermute | solution.py:845
  54.6 2.0 collective-permute-start.11
  56.7 12.4 %project.1 = (bf16[768,1024]{1,0:T(8,128)(2,1)}, bf16[768,1024]{1,0:T(8,128)(2,1)}, bf16[1024,768]{1,0:T(8,128)(2,1)}, bf16[12,80,1024]{2,1,0:T(8,128)(2,1)S(1)}...) custom-call(f32[4]{0:T(128)S(1)} %compare_convert_fusion.kept, ...), custom_call_target="tpu_custom_call" | custom-call | flops 41999998976 | bytes 1024 | tf_op jit(solution)/shard_map/project/pallas_call | solution.py:106
  73.7 7.3 %attend.1 = (bf16[768,1024]{1,0:T(8,128)(2,1)S(1)}, bf16[768,1024]{1,0:T(8,128)(2,1)}, f32[16,1024]{1,0:T(8,128)S(1)}) custom-call(f32[4]{0:T(128)S(1)} %get-tuple-element.179.carry, f32[8,1024]{1,0:T(8,128)S(1)} %convert_element_type.43.aux, bf16[4,256,256]{2,1,0:T(8,128)(2,1)} %and_convert_fusion.mask, ...), custom_call_target="tpu_custom_call" | custom-call | flops 41999998976 | bytes 1024 | tf_op jit(solution)/shard_map/attend/pallas_call | solution.py:106
  82.2 4.3 %collective-permute-done.15.refs_1_ = bf16[4,48,768]{2,1,0:T(8,128)(2,1)S(1)} collective-permute-done((bf16[4,48,768]{2,1,0:T(8,128)(2,1)S(1)}, bf16[4,48,768]{2,1,0:T(8,128)(2,1)S(1)}, u32[]{:S(2)}, u32[]{:S(2)}) %collective-permute-start.15) | collective-permute-done | bytes 294944 | tf_op jit(solution)/shard_map/ppermute | solution.py:845
  89.9 7.2 %all-gather.3.cloned.1.call-done = bf16[1536,1920]{1,0:T(8,128)(2,1)} async-done(((bf16[48,1920]{1,0:T(8,128)(2,1)}), bf16[1536,1920]{1,0:T(8,128)(2,1)}) %all-gather.3.cloned.1.call-update) | async-done | bytes 5898256 | tf_op jit(solution)/shard_map/all_gather | solution.py:1275
  98.5 6.8 %mix.1 = (f32[1024,768]{1,0:T(8,128)}, bf16[1024,768]{1,0:T(8,128)(2,1)S(1)}, bf16[768,1024]{1,0:T(8,128)(2,1)S(1)}) custom-call(s32[4]{0:T(128)S(1)} %pad_add_fusion.spots, bf16[1024,768]{1,0:T(8,128)(2,1)} %tokens.2, f32[4,768]{1,0:T(4,128)S(1)} %pad_maximum_fusion.norms, bf16[16,2,48,1920]{3,2,1,0:T(8,128)(2,1)} %bitcast.50, ...), custom_call_target="tpu_custom_call" | custom-call | flops 20999999488 | bytes 1024 | tf_op jit(solution)/shard_map/mix/pallas_call | solution.py:106
  105.3 10.1 %feed.3 = (f32[1024,768]{1,0:T(8,128)S(1)}, f32[1024,768]{1,0:T(8,128)S(1)}, bf16[768,1536]{1,0:T(8,128)(2,1)S(1)}) custom-call(s32[4]{0:T(128)S(1)} %pad_add_fusion.spots, bf16[1024,768]{1,0:T(8,128)(2,1)S(1)} %get-tuple-element.205.normed, bf16[768,1024]{1,0:T(8,128)(2,1)S(1)} %get-tuple-element.206.normed_t, bf16[1024,768]{1,0:T(8,128)(2,1)S(1)} %copy-done.17, ...), custom_call_target="tpu_custom_call" | custom-call | flops 27000000512 | bytes 1024 | tf_op jit(solution)/shard_map/feed/pallas_call | solution.py:106
  115.8 2.8 %pair.7 = (bf16[4,2,2,48,768]{4,3,2,1,0:T(8,128)(2,1)}, bf16[4,2,2,48,768]{4,3,2,1,0:T(8,128)(2,1)}) custom-call(s32[4]{0:T(128)S(1)} %pad_add_fusion.spots, bf16[4,2,48,768]{3,2,1,0:T(8,128)(2,1)S(1)} %get-tuple-element.202.refs_0_, bf16[4,2,48,768]{3,2,1,0:T(8,128)(2,1)S(1)} %collective-permute-done.17.refs_1_, ...), custom_call_target="tpu_custom_call" | custom-call | bytes 1024 | tf_op jit(solution)/shard_map/pair/pallas_call | solution.py:106
  119.1 10.1 %feed.4 = (f32[1024,768]{1,0:T(8,128)S(1)}, f32[1024,768]{1,0:T(8,128)S(1)}, bf16[768,1536]{1,0:T(8,128)(2,1)S(1)}) custom-call(s32[4]{0:T(128)S(1)} %pad_add_fusion.spots, bf16[1024,768]{1,0:T(8,128)(2,1)S(1)} %get-tuple-element.205.normed, bf16[768,1024]{1,0:T(8,128)(2,1)S(1)} %get-tuple-element.206.normed_t, ...), custom_call_target="tpu_custom_call", output_to_operand_aliasing={{0}: (7, {}), {1}: (8, {})} | custom-call | flops 27000000512 | bytes 1024 | tf_op jit(solution)/shard_map/feed/pallas_call | solution.py:106
  133.1 16.4 %feed.5 = (f32[1024,768]{1,0:T(8,128)S(1)}, f32[1024,768]{1,0:T(8,128)S(1)}, bf16[768,1536]{1,0:T(8,128)(2,1)S(1)}, bf16[768,1536]{1,0:T(8,128)(2,1)S(1)}) custom-call(s32[4]{0:T(128)S(1)} %pad_add_fusion.spots, bf16[1024,768]{1,0:T(8,128)(2,1)S(1)} %get-tuple-element.205.normed, ...), custom_call_target="tpu_custom_call", output_to_operand_aliasing={{0}: (9, {}), {1}: (10, {})} | custom-call | flops 54000001024 | bytes 1024 | tf_op jit(solution)/shard_map/feed/pallas_call | solution.py:106
  152.6 11.4 %middle.1 = (bf16[1024,768]{1,0:T(8,128)(2,1)}, f32[1024,768]{1,0:T(8,128)}, f32[1,768]{1,0:T(1,128)S(1)}, f32[1,768]{1,0:T(1,128)S(1)}, bf16[12,80,1024]{2,1,0:...) custom-call(s32[4]{0:T(128)S(1)} %pad_add_fusion.spots, ...), custom_call_target="tpu_custom_call" | custom-call | flops 38999998464 | bytes 1024 | tf_op jit(solution)/shard_map/middle/pallas_call | solution.py:106
  166.1 2.1 collective-permute-start.30
  169.0 2.4 collective-permute-start.32
  174.9 11.2 %attend_back.2 = (bf16[1152,1024]{1,0:T(8,128)(2,1)S(1)}, f32[2,3,64,128]{3,2,1,0:T(8,128)}) custom-call(f32[4]{0:T(128)S(1)} %copy-done.1, f32[4]{0:T(128)S(1)} %copy-done.15, f32[8,1024]{1,0:T(8,128)S(1)} %convert_element_type.43.aux, bf16[4,256,256]{2,1,0:T(8,128)(2,1)} %and_convert_fusion.mask, bf16[12,128,1024]{2,1,0:T(8,128)(2,1)S(1)} %copy-done.26, ...), custom_call_target="tpu_custom_call" | custom-call | flops 41999998976 | bytes 1024 | tf_op jit(solution)/shard_map/attend_back/pallas_call | solution.py:106
  186.3 3.7 %weight_grads.2 = bf16[768,1152]{1,0:T(8,128)(2,1)S(1)} custom-call(bf16[768,1024]{1,0:T(8,128)(2,1)} %get-tuple-element.234.normed_t, bf16[1152,1024]{1,0:T(8,128)(2,1)S(1)} %get-tuple-element.262.grads.grads_oth), custom_call_target="tpu_custom_call" | custom-call | bytes 1024 | tf_op jit(solution)/shard_map/weight_grads/pallas_call | solution.py:106
  190.5 3.3 %collective-permute-done.29.refs_1_ = bf16[4,2,48,1024]{3,2,1,0:T(8,128)(2,1)S(1)} collective-permute-done((bf16[4,2,48,1024]{3,2,1,0:T(8,128)(2,1)S(1)}, bf16[4,2,48,1024]{3,2,1,0:T(8,128)(2,1)S(1)}, u32[]{:S(2)}, u32[]{:S(2)}) %collective-permute-start.29) | collective-permute-done | bytes 786464 | tf_op jit(solution)/shard_map/ppermute | solution.py:845
  196.8 11.3 %attend_back.3 = (bf16[1152,1024]{1,0:T(8,128)(2,1)S(1)}, f32[2,3,64,128]{3,2,1,0:T(8,128)}) custom-call(f32[4]{0:T(128)S(1)} %copy-done.1, f32[4]{0:T(128)S(1)} %copy-done.15, f32[8,1024]{1,0:T(8,128)S(1)} %convert_element_type.43.aux, bf16[4,256,256]{2,1,0:T(8,128)(2,1)} %and_convert_fusion.mask, bf16[12,128,1024]{2,1,0:T(8,128)(2,1)S(1)} %copy-done.26, ...), custom_call_target="tpu_custom_call" | custom-call | flops 41999998976 | bytes 1024 | tf_op jit(solution)/shard_map/attend_back/pallas_call | solution.py:106
  209.9 2.0 collective-permute-start.41
  212.6 2.2 collective-permute-start.43
  214.8 3.6 %weight_grads.3 = bf16[768,1152]{1,0:T(8,128)(2,1)S(1)} custom-call(bf16[768,1024]{1,0:T(8,128)(2,1)} %get-tuple-element.234.normed_t, bf16[1152,1024]{1,0:T(8,128)(2,1)S(1)} %get-tuple-element.275.grads.grads_own), custom_call_target="tpu_custom_call" | custom-call | bytes 1024 | tf_op jit(solution)/shard_map/weight_grads/pallas_call | solution.py:106
  221.8 8.9 %first_back.1 = (bf16[1024,768]{1,0:T(8,128)(2,1)}, f32[1,768]{1,0:T(1,128)S(1)}, f32[1,768]{1,0:T(1,128)S(1)}) custom-call(bf16[1024,768]{1,0:T(8,128)(2,1)} %tokens.2, f32[4,768]{1,0:T(4,128)S(1)} %pad_maximum_fusion.norms, f32[1024,768]{1,0:T(8,128)} %get-tuple-element.278.grad_hidden, bf16[768,640]{1,0:T(8,128)(2,1)S(1)} %bitcast.42, ...), custom_call_target="tpu_custom_call" | custom-call | flops 27000000512 | bytes 1024 | tf_op jit(solution)/shard_map/first_back/pallas_call | solution.py:106
  230.7 2.7 %collective-permute-done.39.refs_1_ = bf16[5,2,48,640]{3,2,1,0:T(8,128)(2,1)S(1)} collective-permute-done((bf16[5,2,48,640]{3,2,1,0:T(8,128)(2,1)S(1)}, bf16[5,2,48,640]{3,2,1,0:T(8,128)(2,1)S(1)}, u32[]{:S(2)}, u32[]{:S(2)}) %collective-permute-start.39) | collective-permute-done | bytes 614432 | tf_op jit(solution)/shard_map/ppermute | solution.py:845
  239.9 3.3 %collective-permute-done.46.norm_far = bf16[16,768]{1,0:T(8,128)(2,1)S(1)} collective-permute-done((bf16[16,768]{1,0:T(8,128)(2,1)S(1)}, bf16[16,768]{1,0:T(8,128)(2,1)S(1)}, u32[]{:S(2)}, u32[]{:S(2)}) %collective-permute-start.46) | collective-permute-done | bytes 24608 | tf_op jit(solution)/shard_map/ppermute | solution.py:1212
  243.1 3.5 %collective-permute-done.47.maps_moved = bf16[384,128]{1,0:T(8,128)(2,1)S(1)} collective-permute-done((bf16[384,128]{1,0:T(8,128)(2,1)S(1)}, bf16[384,128]{1,0:T(8,128)(2,1)S(1)}, u32[]{:S(2)}, u32[]{:S(2)}) %collective-permute-start.47) | collective-permute-done | bytes 98336 | tf_op jit(solution)/shard_map/ppermute | solution.py:845
  247.4 2.6 collective-permute-start.49
  252.7 3.2 %collective-permute-done.51.refs_5_ = bf16[384,128]{1,0:T(8,128)(2,1)S(1)} collective-permute-done((bf16[384,128]{1,0:T(8,128)(2,1)S(1)}, bf16[384,128]{1,0:T(8,128)(2,1)S(1)}, u32[]{:S(2)}, u32[]{:S(2)}) %collective-permute-start.51) | collective-permute-done | bytes 98336 | tf_op jit(solution)/shard_map/ppermute | solution.py:845
  (224 shorter events, 67.9 us)
Async XLA Ops:
  7.3 89.9 %all-gather.3.cloned.1.call-start = ((), (), s32[]{:S(2)}) async-start(), calls=%async_computation | async-start | bytes 6082560 | tf_op jit(solution)/shard_map/all_gather | solution.py:1275
  15.2 23.6 %collective-permute-start.5 = (bf16[6,64,64]{2,1,0:T(8,128)(2,1)S(1)}, bf16[6,64,64]{2,1,0:T(8,128)(2,1)S(1)}, u32[]{:S(2)}, u32[]{:S(2)}) collective-permute-start(bf16[6,64,64]{2,1,0:T(8,128)(2,1)S(1)} %copy-done.12), channel_id=1, source_target_pairs={{0,1},{1,0},{2,3},{3,2},{4,5},{5,4},{6,7},{7,6},{8,9},{9,8},{10,11... | collective-permute-start | bytes 147464 | tf_op jit(solution)/shard_map/ppermute | solution.py:841
  15.2 23.6 %collective-permute-start.6 = (bf16[6,64,64]{2,1,0:T(8,128)(2,1)S(1)}, bf16[6,64,64]{2,1,0:T(8,128)(2,1)S(1)}, u32[]{:S(2)}, u32[]{:S(2)}) collective-permute-start(bf16[6,64,64]{2,1,0:T(8,128)(2,1)S(1)} %copy-done.13), channel_id=1, source_target_pairs={{0,1},{1,0},{2,3},{3,2},{4,5},{5,4},{6,7},{7,6},{8,9},{9,8},{10,11... | collective-permute-start | bytes 147464 | tf_op jit(solution)/shard_map/ppermute | solution.py:841
  36.6 14.3 %collective-permute-start.8 = (bf16[4,2,48,512]{3,2,1,0:T(8,128)(2,1)S(1)}, bf16[4,2,48,512]{3,2,1,0:T(8,128)(2,1)S(1)}, u32[]{:S(2)}, u32[]{:S(2)}) collective-permute-start(bf16[4,2,48,512]{3,2,1,0:T(8,128)(2,1)S(1)} %get-tuple-element.185.refs_2_), channel_id=1, source_target_pairs={{0,2},{2,0},{4,6},{6,4},{8,10},{10,8},{12,14},{14,12},{16,18},{18,... | collective-permute-start | bytes 1179656 | tf_op jit(solution)/shard_map/ppermute | solution.py:845
  37.2 13.7 %collective-permute-start.7 = (bf16[4,2,48,640]{3,2,1,0:T(8,128)(2,1)S(1)}, bf16[4,2,48,640]{3,2,1,0:T(8,128)(2,1)S(1)}, u32[]{:S(2)}, u32[]{:S(2)}) collective-permute-start(bf16[4,2,48,640]{3,2,1,0:T(8,128)(2,1)S(1)} %get-tuple-element.172.refs_0_), channel_id=1, source_target_pairs={{0,4},{2,6},{4,0},{6,2},{8,12},{10,14},{12,8},{14,10},{16,20},{18,... | collective-permute-start | bytes 1474568 | tf_op jit(solution)/shard_map/ppermute | solution.py:845
  52.3 16.9 %collective-permute-start.13 = (bf16[48,1536]{1,0:T(8,128)(2,1)S(1)}, bf16[48,1536]{1,0:T(8,128)(2,1)S(1)}, u32[]{:S(2)}, u32[]{:S(2)}) collective-permute-start(bf16[48,1536]{1,0:T(8,128)(2,1)S(1)} %get-tuple-element.194.refs_0_), channel_id=1, source_target_pairs={{0,24},{2,26},{4,28},{6,30},{8,0},{10,2},{12,4},{14,6},{16,8},{18,... | collective-permute-start | bytes 442376 | tf_op jit(solution)/shard_map/ppermute | solution.py:849
  53.8 16.1 %collective-permute-start.12 = (bf16[48,1536]{1,0:T(8,128)(2,1)S(1)}, bf16[48,1536]{1,0:T(8,128)(2,1)S(1)}, u32[]{:S(2)}, u32[]{:S(2)}) collective-permute-start(bf16[48,1536]{1,0:T(8,128)(2,1)S(1)} %get-tuple-element.194.refs_0_), channel_id=1, source_target_pairs={{0,16},{2,18},{4,20},{6,22},{8,24},{10,26},{12,28},{14,30},{16,0},... | collective-permute-start | bytes 442376 | tf_op jit(solution)/shard_map/ppermute | solution.py:849
  54.6 14.5 %collective-permute-start.11 = (bf16[48,1536]{1,0:T(8,128)(2,1)S(1)}, bf16[48,1536]{1,0:T(8,128)(2,1)S(1)}, u32[]{:S(2)}, u32[]{:S(2)}) collective-permute-start(bf16[48,1536]{1,0:T(8,128)(2,1)S(1)} %get-tuple-element.194.refs_0_), channel_id=1, source_target_pairs={{0,8},{2,10},{4,12},{6,14},{8,16},{10,18},{12,20},{14,22},{16,24},... | collective-permute-start | bytes 442376 | tf_op jit(solution)/shard_map/ppermute | solution.py:849
  70.5 16.1 %collective-permute-start.15 = (bf16[4,48,768]{2,1,0:T(8,128)(2,1)S(1)}, bf16[4,48,768]{2,1,0:T(8,128)(2,1)S(1)}, u32[]{:S(2)}, u32[]{:S(2)}) collective-permute-start(bf16[4,48,768]{2,1,0:T(8,128)(2,1)S(1)} %get-tuple-element.196.refs_0_), channel_id=1, source_target_pairs={{0,2},{2,0},{4,6},{6,4},{8,10},{10,8},{12,14},{14,12},{16,18},{18,... | collective-permute-start | bytes 884744 | tf_op jit(solution)/shard_map/ppermute | solution.py:845
  71.3 15.7 %collective-permute-start.16 = (bf16[4,48,768]{2,1,0:T(8,128)(2,1)S(1)}, bf16[4,48,768]{2,1,0:T(8,128)(2,1)S(1)}, u32[]{:S(2)}, u32[]{:S(2)}) collective-permute-start(bf16[4,48,768]{2,1,0:T(8,128)(2,1)S(1)} %get-tuple-element.201.refs_2_), channel_id=1, source_target_pairs={{0,4},{2,6},{4,0},{6,2},{8,12},{10,14},{12,8},{14,10},{16,20},{18,... | collective-permute-start | bytes 884744 | tf_op jit(solution)/shard_map/ppermute | solution.py:845
  87.8 28.0 %collective-permute-start.17 = (bf16[4,2,48,768]{3,2,1,0:T(8,128)(2,1)S(1)}, bf16[4,2,48,768]{3,2,1,0:T(8,128)(2,1)S(1)}, u32[]{:S(2)}, u32[]{:S(2)}) collective-permute-start(bf16[4,2,48,768]{3,2,1,0:T(8,128)(2,1)S(1)} %get-tuple-element.202.refs_0_), channel_id=1, source_target_pairs={{0,4},{2,6},{4,0},{6,2},{8,12},{10,14},{12,8},{14,10},{16,20},{18,... | collective-permute-start | bytes 1769480 | tf_op jit(solution)/shard_map/ppermute | solution.py:845
  88.8 26.9 %collective-permute-start.18 = (bf16[4,2,48,768]{3,2,1,0:T(8,128)(2,1)S(1)}, bf16[4,2,48,768]{3,2,1,0:T(8,128)(2,1)S(1)}, u32[]{:S(2)}, u32[]{:S(2)}) collective-permute-start(bf16[4,2,48,768]{3,2,1,0:T(8,128)(2,1)S(1)} %get-tuple-element.212.refs_2_), channel_id=1, source_target_pairs={{0,2},{2,0},{4,6},{6,4},{8,10},{10,8},{12,14},{14,12},{16,18},{18,... | collective-permute-start | bytes 1769480 | tf_op jit(solution)/shard_map/ppermute | solution.py:845
  115.4 13.9 %collective-permute-start.19 = (bf16[768,1536]{1,0:T(8,128)(2,1)S(1)}, bf16[768,1536]{1,0:T(8,128)(2,1)S(1)}, u32[]{:S(2)}, u32[]{:S(2)}) collective-permute-start(bf16[768,1536]{1,0:T(8,128)(2,1)S(1)} %get-tuple-element.210), channel_id=1, source_target_pairs={{0,1},{1,0},{2,3},{3,2},{4,5},{5,4},{6,7},{7,6},{8,9},{9,8},{10,11... | collective-permute-start | bytes 7077896 | tf_op jit(solution)/shard_map/ppermute | solution.py:841
  118.6 14.5 %collective-permute-start.21 = (bf16[768,768]{1,0:T(8,128)(2,1)}, bf16[768,768]{1,0:T(8,128)(2,1)S(1)}, u32[]{:S(2)}, u32[]{:S(2)}) collective-permute-start(bf16[768,768]{1,0:T(8,128)(2,1)} %bitcast.36), channel_id=1, source_target_pairs={{0,1},{1,0},{2,3},{3,2},{4,5},{5,4},{6,7},{7,6},{8,9},{9,8},{10,11... | collective-permute-start | bytes 3538952 | tf_op jit(solution)/shard_map/ppermute | solution.py:841
  118.9 14.2 %collective-permute-start.22 = (bf16[768,768]{1,0:T(8,128)(2,1)}, bf16[768,768]{1,0:T(8,128)(2,1)S(1)}, u32[]{:S(2)}, u32[]{:S(2)}) collective-permute-start(bf16[768,768]{1,0:T(8,128)(2,1)} %bitcast.38), channel_id=1, source_target_pairs={{0,1},{1,0},{2,3},{3,2},{4,5},{5,4},{6,7},{7,6},{8,9},{9,8},{10,11... | collective-permute-start | bytes 3538952 | tf_op jit(solution)/shard_map/ppermute | solution.py:841
  131.0 18.6 %collective-permute-start.20 = (bf16[4,2,48,768]{3,2,1,0:T(8,128)(2,1)S(1)}, bf16[4,2,48,768]{3,2,1,0:T(8,128)(2,1)S(1)}, u32[]{:S(2)}, u32[]{:S(2)}) collective-permute-start(bf16[4,2,48,768]{3,2,1,0:T(8,128)(2,1)S(1)} %get-tuple-element.218), channel_id=1, source_target_pairs={{0,2},{2,0},{4,6},{6,4},{8,10},{10,8},{12,14},{14,12},{16,18},{18,... | collective-permute-start | bytes 1769480 | tf_op jit(solution)/shard_map/ppermute | solution.py:845
  132.4 17.1 %collective-permute-start.23 = (bf16[4,2,48,768]{3,2,1,0:T(8,128)(2,1)S(1)}, bf16[4,2,48,768]{3,2,1,0:T(8,128)(2,1)S(1)}, u32[]{:S(2)}, u32[]{:S(2)}) collective-permute-start(bf16[4,2,48,768]{3,2,1,0:T(8,128)(2,1)S(1)} %get-tuple-element.226), channel_id=1, source_target_pairs={{0,4},{2,6},{4,0},{6,2},{8,12},{10,14},{12,8},{14,10},{16,20},{18,... | collective-permute-start | bytes 1769480 | tf_op jit(solution)/shard_map/ppermute | solution.py:845
  149.5 19.5 %collective-permute-start.27 = (bf16[768,1536]{1,0:T(8,128)(2,1)S(1)}, bf16[768,1536]{1,0:T(8,128)(2,1)S(1)}, u32[]{:S(2)}, u32[]{:S(2)}) collective-permute-start(bf16[768,1536]{1,0:T(8,128)(2,1)S(1)} %get-tuple-element.223), channel_id=1, source_target_pairs={{0,1},{1,0},{2,3},{3,2},{4,5},{5,4},{6,7},{7,6},{8,9},{9,8},{10,11... | collective-permute-start | bytes 7077896 | tf_op jit(solution)/shard_map/ppermute | solution.py:841
  150.5 13.5 %collective-permute-start.24 = (bf16[4,48,768]{2,1,0:T(8,128)(2,1)S(1)}, bf16[4,48,768]{2,1,0:T(8,128)(2,1)S(1)}, u32[]{:S(2)}, u32[]{:S(2)}) collective-permute-start(bf16[4,48,768]{2,1,0:T(8,128)(2,1)S(1)} %get-tuple-element.239), channel_id=1, source_target_pairs={{0,4},{2,6},{4,0},{6,2},{8,12},{10,14},{12,8},{14,10},{16,20},{18,... | collective-permute-start | bytes 884744 | tf_op jit(solution)/shard_map/ppermute | solution.py:845
  166.1 20.0 %collective-permute-start.30 = (bf16[48,1536]{1,0:T(8,128)(2,1)S(1)}, bf16[48,1536]{1,0:T(8,128)(2,1)S(1)}, u32[]{:S(2)}, u32[]{:S(2)}) collective-permute-start(bf16[48,1536]{1,0:T(8,128)(2,1)S(1)} %get-tuple-element.257), channel_id=1, source_target_pairs={{0,8},{2,10},{4,12},{6,14},{8,16},{10,18},{12,20},{14,22},{16,24},... | collective-permute-start | bytes 442376 | tf_op jit(solution)/shard_map/ppermute | solution.py:849
  168.2 18.1 %collective-permute-start.31 = (bf16[48,1536]{1,0:T(8,128)(2,1)S(1)}, bf16[48,1536]{1,0:T(8,128)(2,1)S(1)}, u32[]{:S(2)}, u32[]{:S(2)}) collective-permute-start(bf16[48,1536]{1,0:T(8,128)(2,1)S(1)} %get-tuple-element.260), channel_id=1, source_target_pairs={{0,16},{2,18},{4,20},{6,22},{8,24},{10,26},{12,28},{14,30},{16,0},... | collective-permute-start | bytes 442376 | tf_op jit(solution)/shard_map/ppermute | solution.py:849
  169.0 17.2 %collective-permute-start.32 = (bf16[48,1536]{1,0:T(8,128)(2,1)S(1)}, bf16[48,1536]{1,0:T(8,128)(2,1)S(1)}, u32[]{:S(2)}, u32[]{:S(2)}) collective-permute-start(bf16[48,1536]{1,0:T(8,128)(2,1)S(1)} %get-tuple-element.261), channel_id=1, source_target_pairs={{0,24},{2,26},{4,28},{6,30},{8,0},{10,2},{12,4},{14,6},{16,8},{18,... | collective-permute-start | bytes 442376 | tf_op jit(solution)/shard_map/ppermute | solution.py:849
  172.8 21.0 %collective-permute-start.33 = (bf16[4,2,48,896]{3,2,1,0:T(8,128)(2,1)S(1)}, bf16[4,2,48,896]{3,2,1,0:T(8,128)(2,1)S(1)}, u32[]{:S(2)}, u32[]{:S(2)}) collective-permute-start(bf16[4,2,48,896]{3,2,1,0:T(8,128)(2,1)S(1)} %get-tuple-element.265), channel_id=1, source_target_pairs={{0,4},{2,6},{4,0},{6,2},{8,12},{10,14},{12,8},{14,10},{16,20},{18,... | collective-permute-start | bytes 2064392 | tf_op jit(solution)/shard_map/ppermute | solution.py:845
  174.3 19.5 %collective-permute-start.29 = (bf16[4,2,48,1024]{3,2,1,0:T(8,128)(2,1)S(1)}, bf16[4,2,48,1024]{3,2,1,0:T(8,128)(2,1)S(1)}, u32[]{:S(2)}, u32[]{:S(2)}) collective-permute-start(bf16[4,2,48,1024]{3,2,1,0:T(8,128)(2,1)S(1)} %get-tuple-element.253), channel_id=1, source_target_pairs={{0,2},{2,0},{4,6},{6,4},{8,10},{10,8},{12,14},{14,12},{16,18},{18,... | collective-permute-start | bytes 2359304 | tf_op jit(solution)/shard_map/ppermute | solution.py:845
  186.1 22.0 %collective-permute-start.37 = (f32[2,3,64,128]{3,2,1,0:T(8,128)}, f32[2,3,64,128]{3,2,1,0:T(8,128)S(1)}, u32[]{:S(2)}, u32[]{:S(2)}) collective-permute-start(f32[2,3,64,128]{3,2,1,0:T(8,128)} %get-tuple-element.258), channel_id=1, source_target_pairs={{0,1},{1,0},{2,3},{3,2},{4,5},{5,4},{6,7},{7,6},{8,9},{9,8},{10,11... | collective-permute-start | bytes 589832 | tf_op jit(solution)/shard_map/ppermute | solution.py:841
  190.0 28.6 %collective-permute-start.36 = (bf16[768,1152]{1,0:T(8,128)(2,1)S(1)}, bf16[768,1152]{1,0:T(8,128)(2,1)S(1)}, u32[]{:S(2)}, u32[]{:S(2)}) collective-permute-start(bf16[768,1152]{1,0:T(8,128)(2,1)S(1)} %weight_grads.2), channel_id=1, source_target_pairs={{0,1},{1,0},{2,3},{3,2},{4,5},{5,4},{6,7},{7,6},{8,9},{9,8},{10,11... | collective-permute-start | bytes 5308424 | tf_op jit(solution)/shard_map/ppermute | solution.py:841
  194.8 14.4 %collective-permute-start.35 = (bf16[4,48,896]{2,1,0:T(8,128)(2,1)S(1)}, bf16[4,48,896]{2,1,0:T(8,128)(2,1)S(1)}, u32[]{:S(2)}, u32[]{:S(2)}) collective-permute-start(bf16[4,48,896]{2,1,0:T(8,128)(2,1)S(1)} %get-tuple-element.273), channel_id=1, source_target_pairs={{0,2},{2,0},{4,6},{6,4},{8,10},{10,8},{12,14},{14,12},{16,18},{18,... | collective-permute-start | bytes 1032200 | tf_op jit(solution)/shard_map/ppermute | solution.py:845
  195.4 13.7 %collective-permute-start.34 = (bf16[4,48,1024]{2,1,0:T(8,128)(2,1)S(1)}, bf16[4,48,1024]{2,1,0:T(8,128)(2,1)S(1)}, u32[]{:S(2)}, u32[]{:S(2)}) collective-permute-start(bf16[4,48,1024]{2,1,0:T(8,128)(2,1)S(1)} %get-tuple-element.269), channel_id=1, source_target_pairs={{0,4},{2,6},{4,0},{6,2},{8,12},{10,14},{12,8},{14,10},{16,20},{18,... | collective-permute-start | bytes 1179656 | tf_op jit(solution)/shard_map/ppermute | solution.py:845
  209.9 23.5 %collective-permute-start.41 = (bf16[48,1920]{1,0:T(8,128)(2,1)S(1)}, bf16[48,1920]{1,0:T(8,128)(2,1)S(1)}, u32[]{:S(2)}, u32[]{:S(2)}) collective-permute-start(bf16[48,1920]{1,0:T(8,128)(2,1)S(1)} %get-tuple-element.287), channel_id=1, source_target_pairs={{0,8},{2,10},{4,12},{6,14},{8,16},{10,18},{12,20},{14,22},{16,24},... | collective-permute-start | bytes 552968 | tf_op jit(solution)/shard_map/ppermute | solution.py:849
  212.0 21.4 %collective-permute-start.42 = (bf16[48,1920]{1,0:T(8,128)(2,1)S(1)}, bf16[48,1920]{1,0:T(8,128)(2,1)S(1)}, u32[]{:S(2)}, u32[]{:S(2)}) collective-permute-start(bf16[48,1920]{1,0:T(8,128)(2,1)S(1)} %get-tuple-element.288), channel_id=1, source_target_pairs={{0,16},{2,18},{4,20},{6,22},{8,24},{10,26},{12,28},{14,30},{16,0},... | collective-permute-start | bytes 552968 | tf_op jit(solution)/shard_map/ppermute | solution.py:849
  212.6 20.8 %collective-permute-start.43 = (bf16[48,1920]{1,0:T(8,128)(2,1)S(1)}, bf16[48,1920]{1,0:T(8,128)(2,1)S(1)}, u32[]{:S(2)}, u32[]{:S(2)}) collective-permute-start(bf16[48,1920]{1,0:T(8,128)(2,1)S(1)} %get-tuple-element.289), channel_id=1, source_target_pairs={{0,24},{2,26},{4,28},{6,30},{8,0},{10,2},{12,4},{14,6},{16,8},{18,... | collective-permute-start | bytes 552968 | tf_op jit(solution)/shard_map/ppermute | solution.py:849
  219.6 13.8 %collective-permute-start.40 = (bf16[4,2,48,512]{3,2,1,0:T(8,128)(2,1)S(1)}, bf16[4,2,48,512]{3,2,1,0:T(8,128)(2,1)S(1)}, u32[]{:S(2)}, u32[]{:S(2)}) collective-permute-start(bf16[4,2,48,512]{3,2,1,0:T(8,128)(2,1)S(1)} %get-tuple-element.284), channel_id=1, source_target_pairs={{0,4},{2,6},{4,0},{6,2},{8,12},{10,14},{12,8},{14,10},{16,20},{18,... | collective-permute-start | bytes 1179656 | tf_op jit(solution)/shard_map/ppermute | solution.py:845
  (60 other events, 516.1 us)
Sparse Core Ops, SparseCore 0:
  15.8 81.2 all-gather.2
